TPU v7x, 32 devices: a whole 2x2x4 slice. The times are simulated.
32 devices in a mesh: seq: 4 (over y, x), nbr: 8 (over z, core).
Axes of the slice: x: 2, y: 2, z: 4, core: 2. Of those that a mesh axis runs over, the one named last changes fastest.
Arguments:
- tokens: bfloat16 [2048, 4096], P(('seq', 'nbr')), may hold values from -7 to 7
- nbr_embed: bfloat16 [64, 128, 896], P('seq', 'nbr'), may hold values from -7 to 7
- neighbour_table: int32 [32, 2], P('seq'), may hold values from 0 to 63, as said below
- valid_counts: int32 [32], replicated, may hold values from 1 to 2
- dec_proj: bfloat16 [4096, 3, 4096], P(None, None, 'nbr'), may hold values from -1 to 1
- enc_query: bfloat16 [896, 4096], P(None, 'nbr'), may hold values from -2 to 2
- enc_out: bfloat16 [4096, 896], P('nbr'), may hold values from -0.09375 to 0.09375
- enc_gain: float32 [896], replicated, may hold values from 0.1 to 1.9
- nbr_proj: bfloat16 [896, 2, 4096], P(None, None, 'nbr'), may hold values from -2 to 2
- out_proj: bfloat16 [4096, 4096], P('nbr'), may hold values from -0.09375 to 0.09375
Outputs:
- cross_out: bfloat16 [2048, 4096], P(('seq', 'nbr'))
- encoded: bfloat16 [8192, 896], P(('seq', 'nbr'))
Inputs may be any that keep to these rules, and one draw needn't show every extreme that they name: `neighbour_table`: for each block b of 8 groups in order, the entries of those groups are a permutation of the neighbour rows b * 16 to (b + 1) * 16 - 1.
All inputs are finite; a program needn't handle non-finite values.
Results may differ from a plain program's by a relative error of at most 0.025.
Values may be sent and summed in bfloat16 or wider, within the bound.
No kernel may reach another device: no remote copies, remote signals or barrier semaphores. Data moves between devices by JAX's collectives and lax.ppermute only.
A program may use at most 128 MiB of HBM per device.

v0:
```python
import jax
import jax.numpy as jnp
from jax import lax
from jax.sharding import PartitionSpec as P

HEAD_DIM = 128
GROUP = 64
NLEN = 128
SEQ_LEN = 2048


def passed_along(block, axis, distance):
    devices = range(lax.axis_size(axis))
    route = [(i - distance, i) for i in devices if i - distance in devices]
    return lax.ppermute(block, axis, route)


def plain_softmax(scores):
    peak = jnp.max(scores, axis=-1, keepdims=True)
    raised = jnp.exp(scores - peak)
    return (raised / jnp.sum(raised, axis=-1, keepdims=True)).astype(jnp.bfloat16)


def masked_softmax(scores, allowed):
    live = jnp.any(allowed, axis=-1, keepdims=True)
    peak = jnp.max(jnp.where(allowed, scores, -1e30), axis=-1, keepdims=True)
    peak = jnp.where(live, peak, 0.0)
    raised = jnp.where(allowed, jnp.exp(scores - peak), 0.0)
    denominator = jnp.where(live, jnp.sum(raised, axis=-1, keepdims=True), 1.0)
    return (raised / denominator).astype(jnp.bfloat16)


def normed_rows(raw_rows, partial_sum, enc_gain):
    combined = raw_rows.astype(jnp.float32) + partial_sum
    factor = lax.rsqrt(jnp.mean(combined * combined, axis=-1, keepdims=True) + 1e-06)
    return (combined * factor * enc_gain).astype(jnp.bfloat16)


def local(
    tokens,
    nbr_embed,
    neighbour_table,
    valid_counts,
    dec_proj,
    enc_query,
    enc_out,
    enc_gain,
    nbr_proj,
    out_proj,
):
    n_nbr = lax.axis_size("nbr")
    seq_index = lax.axis_index("seq")
    member = lax.axis_index("nbr")
    model_width = tokens.shape[1]
    local_width = dec_proj.shape[2]
    head_dev = local_width // HEAD_DIM
    scale = 1.0 / HEAD_DIM**0.5
    dec_flat = dec_proj.reshape(model_width, 3 * local_width)
    projected = jnp.dot(
        lax.all_gather(tokens, "nbr", axis=0, tiled=True),
        dec_flat,
        preferred_element_type=jnp.float32,
    ).astype(jnp.bfloat16)
    tok_grp = projected.shape[0]
    ch_grp = tok_grp // GROUP
    queries = projected[:, :local_width]
    cond_key = projected[:, local_width : 2 * local_width].reshape(
        ch_grp, GROUP, head_dev, HEAD_DIM
    )
    cond_value = projected[:, 2 * local_width :].reshape(ch_grp, GROUP, head_dev, HEAD_DIM)
    grp_embed = lax.all_gather(nbr_embed, "nbr", axis=1, tiled=True)
    nb_grp = grp_embed.shape[0]
    enc_width = grp_embed.shape[2]
    row_ids = neighbour_table.reshape(-1) - seq_index * nb_grp
    ordered = jnp.take(grp_embed, row_ids, axis=0).reshape(-1, enc_width)
    enc_queries = jnp.dot(ordered, enc_query, preferred_element_type=jnp.float32).astype(
        jnp.bfloat16
    )
    enc_queries = enc_queries.reshape(ch_grp, -1, head_dev, HEAD_DIM)
    enc_scores = (
        jnp.einsum("cqhd,ckhd->chqk", enc_queries, cond_key, preferred_element_type=jnp.float32)
        * scale
    )
    enc_weights = plain_softmax(enc_scores)
    enc_att = jnp.einsum(
        "chqk,ckhd->cqhd", enc_weights, cond_value, preferred_element_type=jnp.float32
    ).astype(jnp.bfloat16)
    enc_att = enc_att.reshape(-1, local_width)
    share_rows = enc_att.shape[0] // n_nbr
    summed = lax.psum(jnp.dot(enc_att, enc_out, preferred_element_type=jnp.float32), "nbr")
    encoded_all = normed_rows(ordered, summed, enc_gain)
    encoded_mine = lax.dynamic_slice_in_dim(encoded_all, member * share_rows, share_rows, 0)
    nbr_kv = jnp.dot(
        encoded_all,
        nbr_proj.reshape(enc_width, 2 * local_width),
        preferred_element_type=jnp.float32,
    ).astype(jnp.bfloat16)
    nbr_kv = nbr_kv.reshape(ch_grp, -1, 2 * local_width)
    previous = passed_along(nbr_kv[-1], "seq", 1)
    kv_ext = jnp.concatenate([previous[None], nbr_kv], axis=0)
    key_rows = kv_ext.shape[1]
    kv_ext = kv_ext.reshape(ch_grp + 1, key_rows, 2, head_dev, HEAD_DIM)
    counts_pad = jnp.concatenate([jnp.zeros((1,), jnp.int32), valid_counts], axis=0)
    counts_ext = lax.dynamic_slice_in_dim(counts_pad, seq_index * ch_grp, ch_grp + 1, 0)
    query_pad = jnp.concatenate(
        [
            jnp.zeros((1, local_width), jnp.bfloat16),
            queries,
            jnp.zeros((GROUP - 1, local_width), jnp.bfloat16),
        ],
        axis=0,
    )
    query_pad = query_pad.reshape(ch_grp + 1, GROUP, head_dev, HEAD_DIM)
    local_ids = jnp.arange((ch_grp + 1) * GROUP, dtype=jnp.int32) - 1
    global_ids = seq_index * tok_grp + local_ids
    active = (local_ids >= 0) & (local_ids < tok_grp) & (global_ids % SEQ_LEN >= GROUP - 1)
    active = active.reshape(ch_grp + 1, GROUP)
    key_slot = jnp.arange(key_rows, dtype=jnp.int32) // NLEN
    slot_live = key_slot[None, :] < counts_ext[:, None]
    allowed = active[:, None, :, None] & slot_live[:, None, None, :]
    cca_scores = (
        jnp.einsum(
            "bqhd,bkhd->bhqk", query_pad, kv_ext[:, :, 0], preferred_element_type=jnp.float32
        )
        * scale
    )
    cca_weights = masked_softmax(cca_scores, allowed)
    cca_att = jnp.einsum(
        "bhqk,bkhd->bqhd", cca_weights, kv_ext[:, :, 1], preferred_element_type=jnp.float32
    ).astype(jnp.bfloat16)
    cca_att = cca_att.reshape(-1, local_width)[1 : tok_grp + 1]
    cross_out = lax.psum_scatter(
        jnp.dot(cca_att, out_proj, preferred_element_type=jnp.float32).astype(jnp.bfloat16),
        "nbr",
        scatter_dimension=0,
        tiled=True,
    )
    return (cross_out, encoded_mine)


def solution(mesh):
    return jax.shard_map(
        local,
        mesh=mesh,
        in_specs=(
            P(("seq", "nbr"), None),
            P("seq", "nbr", None),
            P("seq", None),
            P(),
            P(None, None, "nbr"),
            P(None, "nbr"),
            P("nbr", None),
            P(),
            P(None, None, "nbr"),
            P("nbr", None),
        ),
        out_specs=(P(("seq", "nbr"), None), P(("seq", "nbr"), None)),
        check_vma=False,
    )
```

profile of v0, /device:TPU:0, one launch (start us, length us, event | category | flops | bytes accessed | tf_op | source)
XLA Modules:
  0.0 385.3 jit_solution(4106731107551120309)
XLA Ops:
  7.2 0.0 copy-start
  7.2 0.0 all-gather.3.cloned.1.call-start
  7.2 0.7 all-gather.3.cloned.1.call-update
  7.9 0.0 all-gather.5.cloned.1.call-start
  8.0 0.7 all-gather.5.cloned.1.call-update
  8.7 0.0 all-reduce.2.cloned.1.call-start
  8.7 0.7 broadcast_subtract_fusion
  9.4 0.1 copy.31
  9.5 0.1 sub.52
  9.6 0.1 sub.51
  9.6 16.7 %copy.33 = bf16[4096,3,512]{0,2,1:T(8,128)(2,1)} copy(bf16[4096,3,512]{2,0,1:T(8,128)(2,1)} %param.14) | data formatting | bytes 25165824 | tf_op args[4]
  26.4 0.1 broadcast_bitcast_fusion
  26.5 28.5 %all-gather.3.cloned.1.call-done = bf16[16,128,896]{2,1,0:T(8,128)(2,1)} async-done(((bf16[16,16,896]{2,1,0:T(8,128)(2,1)}), bf16[16,128,896]{2,1,0:T(8,128)(2,1)}) %all-gather.3.cloned.1.call-update) | async-done | bytes 3670032 | tf_op jit(solution)/shard_map/all_gather | solution.py:71
  55.0 4.8 %gather_fusion = bf16[16,128,896]{2,1,0:T(8,128)(2,1)} fusion(bf16[16,128,896]{2,1,0:T(8,128)(2,1)} %all-gather.3.cloned.1.call-done, s32[1024]{0:T(1024)S(1)} %pad_clamp_fusion), kind=kCustom, calls=%fused_computation | custom fusion | bytes 7340096 | tf_op jit(solution)/shard_map/jit(_take)/gather | solution.py:75
  59.8 2.5 bitcast_select_fusion
  62.2 3.8 convolution_convert_fusion.3
  66.0 2.5 reshape.164
  68.5 34.1 %all-gather.5.cloned.1.call-done = bf16[512,4096]{1,0:T(8,128)(2,1)} async-done(((bf16[64,4096]{1,0:T(8,128)(2,1)}), bf16[512,4096]{1,0:T(8,128)(2,1)}) %all-gather.5.cloned.1.call-update) | async-done | bytes 4194320 | tf_op jit(solution)/shard_map/all_gather | solution.py:60
  102.6 11.1 %convolution_convert_fusion.2 = bf16[512,1536]{1,0:T(8,128)(2,1)S(1)} fusion(bf16[512,4096]{1,0:T(8,128)(2,1)} %all-gather.5.cloned.1.call-done, bf16[4096,1536]{0,1:T(8,128)(2,1)} %bitcast.49), kind=kOutput, calls=%fused_computation.9 | convolution fusion | flops 6443237376 | bytes 18350080 | tf_op jit(solution)/shard_map/dot_general | solution.py:59
  113.7 1.2 fusion.37
  114.9 1.2 reshape.165
  116.1 0.8 fusion.3
  116.9 1.3 copy-done.6
  118.3 1.2 fusion.38
  119.5 0.1 reshape.163
  119.6 2.6 convert_bitcast_fusion
  122.1 1.2 copy.37
  123.3 0.7 copy.42
  124.0 5.4 %fusion.39 = f32[2048,896]{1,0:T(8,128)} fusion(bf16[2048,512]{0,1:T(8,128)(2,1)S(1)} %bitcast.52, bf16[512,896]{1,0:T(8,128)(2,1)S(1)} %copy-done), kind=kOutput, calls=%fused_computation.78 | convolution fusion | flops 1879048192 | bytes 10354688 | tf_op jit(solution)/shard_map/dot_general | solution.py:90
  129.4 0.0 all-reduce.2.cloned.1.call-update
  129.5 0.0 reduce-scatter.2.cloned.1.call-start
  129.5 1.4 copy-done.9
  130.9 1.7 copy.43
  132.7 0.1 pad_add_fusion
  132.8 0.1 dynamic_slice.6
  132.9 0.1 broadcast_compare_fusion
  132.9 151.3 %all-reduce.2.cloned.1.call-done = f32[2048,896]{1,0:T(8,128)} async-done(((f32[2048,896]{1,0:T(8,128)}), f32[2048,896]{1,0:T(8,128)}) %all-reduce.2.cloned.1.call-update) | async-done | bytes 7340048 | tf_op jit(solution)/shard_map/psum | solution.py:90
  284.2 5.6 %multiply_reduce_fusion = f32[2048]{0:T(1024)S(1)} fusion(f32[2048,896]{1,0:T(8,128)} %all-reduce.2.cloned.1.call-done, bf16[16,128,896]{2,1,0:T(8,128)(2,1)} %gather_fusion, pred[2048]{0:T(1024)(128)(4,1)S(1)} %broadcast_bitcast_fusion), kind=kLoop, calls=%fused_computation.3 | loop fusion | flops 9172992 | bytes 11020288 | tf_op jit(solution)/shard_map/reduce_sum | solution.py:35
  289.9 1.7 copy-done.3
  291.6 1.9 multiply_convert_fusion
  293.6 0.0 copy-start.7
  293.6 4.7 %convolution_convert_fusion.1 = bf16[2048,1024]{1,0:T(8,128)(2,1)S(1)} fusion(bf16[2048,896]{1,0:T(8,128)(2,1)S(1)} %multiply_convert_fusion, bf16[896,1024]{1,0:T(8,128)(2,1)S(1)} %bitcast.54), kind=kOutput, calls=%fused_computation.7 | convolution fusion | flops 3760193536 | bytes 9699328 | tf_op jit(solution)/shard_map/dot_general | solution.py:93
  298.3 1.9 copy-done.4
  300.3 3.4 collective-permute-start
  303.7 0.4 and_reduce_fusion
  304.1 0.1 pad.2.clone
  304.1 0.1 broadcast_and_fusion
  304.3 0.3 maximum_maximum_fusion
  304.6 0.1 reshape.168
  304.7 8.0 %concatenate.15 = bf16[8,256,2,4,128]{4,3,2,1,0:T(4,128)(2,1)} reshape(bf16[2048,1024]{1,0:T(8,128)(2,1)} %copy-done.4) | data formatting | bytes 8388608 | tf_op jit(solution)/shard_map/concatenate | solution.py:100
  312.7 2.0 collective-permute-done
  314.7 0.4 concatenate.14
  315.0 0.1 copy_dynamic-update-slice_fusion.1
  315.1 3.6 copy_dynamic-update-slice_fusion
  318.7 1.1 select_reduce_fusion
  319.8 1.0 fusion.6
  320.8 1.3 fusion.8
  322.1 0.5 copy.41
  322.6 0.1 copy.58
  322.7 0.3 copy-done.12
  323.0 4.3 %convolution_convert_fusion = bf16[512,4096]{1,0:T(8,128)(2,1)} fusion(bf16[512,4096]{1,0:T(8,128)(2,1)S(1)} %copy-done.12, bf16[576,512]{1,0:T(8,128)(2,1)S(1)} %bitcast.55), kind=kOutput, calls=%fused_computation.5 | convolution fusion | flops 2149580800 | bytes 8912896 | tf_op jit(solution)/shard_map/dot_general | solution.py:133
  327.3 0.0 reduce-scatter.2.cloned.1.call-update
  327.3 1.9 constant_dynamic-slice_fusion
  329.2 49.6 %reduce-scatter.2.cloned.1.call-done = bf16[64,4096]{1,0:T(8,128)(2,1)} async-done(((bf16[512,4096]{1,0:T(8,128)(2,1)}), bf16[64,4096]{1,0:T(8,128)(2,1)}) %reduce-scatter.2.cloned.1.call-update) | async-done | bytes 524304 | tf_op jit(solution)/shard_map/reduce_scatter | solution.py:132
  (34 shorter events, 0.2 us)
Async XLA Ops:
  7.2 116.9 %copy-start = (bf16[512,896]{1,0:T(8,128)(2,1)S(1)}, bf16[512,896]{1,0:T(8,128)(2,1)}, u32[]{:S(2)}) copy-start(bf16[512,896]{1,0:T(8,128)(2,1)} %param.16) | copy-start | bytes 2752516
  7.2 47.8 %all-gather.3.cloned.1.call-start = ((), (), s32[]{:S(2)}) async-start(), calls=%async_computation.1 | async-start | bytes 4128768 | tf_op jit(solution)/shard_map/all_gather | solution.py:71
  7.9 94.7 %all-gather.5.cloned.1.call-start = ((), (), s32[]{:S(2)}) async-start(), calls=%async_computation.2 | async-start | bytes 4718592 | tf_op jit(solution)/shard_map/all_gather | solution.py:60
  8.7 275.5 %all-reduce.2.cloned.1.call-start = ((), (), s32[]{:S(2)}) async-start(), calls=%async_computation.3 | async-start | bytes 14680064 | tf_op jit(solution)/shard_map/psum | solution.py:90
  59.7 2.5 copy-start.13
  116.9 1.3 copy-start.6
  118.3 1.2 copy-start.8
  129.4 1.5 copy-start.9
  129.5 3.2 copy-start.14
  129.5 249.3 %reduce-scatter.2.cloned.1.call-start = ((), (), s32[]{:S(2)}) async-start(), calls=%async_computation.4 | async-start | bytes 4718592 | tf_op jit(solution)/shard_map/reduce_scatter | solution.py:132
  132.9 156.9 %copy-start.11 = (f32[896]{0:T(1024)S(1)}, f32[896]{0:T(1024)}, u32[]{:S(2)}) copy-start(f32[896]{0:T(1024)} %param.17) | copy-start | bytes 10756
  284.2 5.7 %copy-start.2 = (bf16[16,128,896]{2,1,0:T(8,128)(2,1)S(1)}, bf16[16,128,896]{2,1,0:T(8,128)(2,1)}, u32[]{:S(2)}) copy-start(bf16[16,128,896]{2,1,0:T(8,128)(2,1)} %gather_fusion) | copy-start | bytes 11010052
  284.2 7.4 %copy-start.3 = (f32[2048,896]{1,0:T(8,128)S(1)}, f32[2048,896]{1,0:T(8,128)}, u32[]{:S(2)}) copy-start(f32[2048,896]{1,0:T(8,128)} %all-reduce.2.cloned.1.call-done) | copy-start | bytes 22020100
  291.6 1.9 copy-start.10
  293.5 4.7 %copy-start.5 = (bf16[2048,896]{1,0:T(8,128)(2,1)}, bf16[2048,896]{1,0:T(8,128)(2,1)S(1)}, u32[]{:S(2)}) copy-start(bf16[2048,896]{1,0:T(8,128)(2,1)S(1)} %multiply_convert_fusion) | copy-start | bytes 11010052
  293.6 10.7 %copy-start.7 = (bf16[512,512]{1,0:T(8,128)(2,1)S(1)}, bf16[512,512]{1,0:T(8,128)(2,1)}, u32[]{:S(2)}) copy-start(bf16[512,512]{1,0:T(8,128)(2,1)} %get-tuple-element.2) | copy-start | bytes 1572868
  298.3 1.9 copy-start.4
  300.3 14.4 %collective-permute-start = (bf16[256,1024]{1,0:T(8,128)(2,1)S(1)}, bf16[256,1024]{1,0:T(8,128)(2,1)S(1)}, u32[]{:S(2)}, u32[]{:S(2)}) collective-permute-start(bf16[256,1024]{1,0:T(8,128)(2,1)S(1)} %slice.34), channel_id=1, source_target_pairs={{0,8},{8,16},{16,24},{1,9},{9,17},{17,25},{2,10},{10,18},{18,26},{... | collective-permute-start | bytes 1572872 | tf_op jit(solution)/shard_map/ppermute | solution.py:15
  320.8 2.2 copy-start.12
  327.3 51.5 %copy-start.1 = (bf16[512,896]{1,0:T(8,128)(2,1)S(1)}, bf16[512,896]{1,0:T(8,128)(2,1)}, u32[]{:S(2)}) copy-start(bf16[512,896]{1,0:T(8,128)(2,1)} %param.16) | copy-start | bytes 2752516
Sparse Core Ops, SparseCore 0:
  9.6 45.2 all-gather.2
  56.5 46.0 all-gather.4
  129.6 154.5 all-reduce.1
  327.4 51.3 reduce-scatter.1
where the time goes:
time: 386 us; the launch traced here: 385 us
  waiting for transfers between devices  267 us (69%)
  local copies, waits for them, and re-layouts  52 us (13%)
  matrix products  35 us (9%)
  between operations  14.1 us (4%)
  other arithmetic  13.9 us (4%)
    psum x1, waiting for transfers between devices, local(): lax.psum(jnp.dot(enc_att, enc_out, preferred_element_type=jnp.float32), '...  151 us
    reduce_scatter x1, waiting for transfers between devices, local(): lax.psum_scatter(jnp.dot(cca_att, out_proj, preferred_element_type=jnp.fl...  49.6 us
    all_gather x1, waiting for transfers between devices, local(): lax.all_gather(tokens, 'nbr', axis=0, tiled=True)  34.1 us
    all_gather x1, waiting for transfers between devices, local(): grp_embed = lax.all_gather(nbr_embed, 'nbr', axis=1, tiled=True)  28.5 us
    unnamed x35, local copies, waits for them, and re-layouts  26.1 us
    concatenate x3, local copies, waits for them, and re-layouts, local(): kv_ext = jnp.concatenate([previous[None], nbr_kv], axis=0)  11.9 us
    dot_general x1, matrix products, local(): jnp.dot(lax.all_gather(tokens, 'nbr', axis=0, tiled=True), dec_flat, pref...  11.1 us
  transfers between devices with their start and end apart: 5, of which 5 were waited for; matrix products, arithmetic and copies ran while one was open for 11% of the time, Pallas kernels for 0%

commit v1 on v0

v1 whole, which is shorter than its diff:
```python
import functools

import jax
import jax.numpy as jnp
from jax import lax
from jax.experimental import pallas as pl
from jax.experimental.pallas import tpu as pltpu
from jax.sharding import PartitionSpec as P

HEAD_DIM = 128
GROUP = 64
NLEN = 128
SEQ_LEN = 2048
SCALE = 1.0 / HEAD_DIM**0.5
F32 = jnp.float32
BF16 = jnp.bfloat16
HBM = pl.BlockSpec(memory_space=pl.ANY)
SMEM = pl.BlockSpec(memory_space=pltpu.SMEM)
VMEM = pl.BlockSpec(memory_space=pltpu.VMEM)


def params():
    return pltpu.CompilerParams(vmem_limit_bytes=48 * 1024 * 1024)


def dot(a, b):
    return jnp.dot(a, b, preferred_element_type=F32)


def dot_t(a, b):
    return lax.dot_general(a, b, (((1,), (1,)), ((), ())), preferred_element_type=F32)


def swapped(x, nz):
    return lax.ppermute(x, "nbr", [(n, n ^ 1) for n in range(2 * nz)])


def line_gather(chip, nz):
    near, far, held = [], [], chip
    for s in range(1, nz):
        up = [(2 * z, 2 * z + 2) for z in range(s - 1, nz - 1)]
        down = [(2 * z + 1, 2 * z - 1) for z in range(1, nz - s + 1)]
        held = lax.ppermute(held, "nbr", up + down)
        near.append(held)
        arrived = [(2 * z, 2 * z + 1) for z in range(s, nz)] + [(2 * z + 1, 2 * z) for z in range(nz - s)]
        far.append(lax.ppermute(held, "nbr", arrived))
    return near, far


def line_sums(parts, other, z, core, nz):
    sign = 1 - 2 * core
    recv = None
    for s in range(1, nz):
        target = jnp.clip(z + sign * (nz - s), 0, nz - 1)
        send = lax.dynamic_index_in_dim(parts, target, 0, False).astype(F32)
        send += lax.dynamic_index_in_dim(other, target, 0, False).astype(F32)
        if recv is not None:
            send += recv.astype(F32)
        up = [(2 * t, 2 * t + 2) for t in range(0, s)]
        down = [(2 * t + 1, 2 * t - 1) for t in range(nz - s, nz)]
        recv = lax.ppermute(send.astype(BF16), "nbr", up + down)
    return recv, swapped(recv, nz)


def copies_in(pos, chip, near, far, place, sems, nz):
    z, core = pos[0], pos[1]
    todo = [(chip, z, None)]
    for s in range(1, nz):
        low = core == 0
        todo.append((near[s - 1], jnp.where(low, z - s, z + s), True))
        todo.append((far[s - 1], jnp.where(low, z + s, z - s), True))
    k = 0
    jobs = []
    for ref, j, check in todo:
        ok = None if check is None else (j >= 0) & (j < nz)
        for src, dst in place(ref, jnp.clip(j, 0, nz - 1)):
            jobs.append((ok, pltpu.make_async_copy(src, dst, sems.at[k])))
            k += 1
    return jobs


def begin(jobs):
    for ok, job in jobs:
        if ok is None:
            job.start()
        else:
            pl.when(ok)(job.start)


def finish(jobs):
    for ok, job in jobs:
        if ok is None:
            job.wait()
        else:
            pl.when(ok)(job.wait)


def proj_kernel(nz, *refs):
    pos, chip = refs[0], refs[1]
    near, far = refs[2 : nz + 1], refs[nz + 1 : 2 * nz]
    w, out, rows, sems = refs[2 * nz :]

    @pl.when(pl.program_id(0) == 0)
    def _():
        jobs = copies_in(pos, chip, near, far, lambda ref, j: [(ref, rows.at[j])], sems, nz)
        begin(jobs)
        finish(jobs)

    out[...] = dot(rows[...].reshape(-1, rows.shape[2]), w[...]).astype(BF16)


def project(pos, chip, near, far, w, nz):
    rows, depth = chip.shape
    width = w.shape[1]
    block = 256
    return pl.pallas_call(
        functools.partial(proj_kernel, nz),
        grid=(width // block,),
        in_specs=[SMEM] + [HBM] * (2 * nz - 1) + [pl.BlockSpec((depth, block), lambda i: (0, i))],
        out_specs=pl.BlockSpec((nz * rows, block), lambda i: (0, i)),
        out_shape=jax.ShapeDtypeStruct((nz * rows, width), BF16),
        scratch_shapes=[pltpu.VMEM((nz, rows, depth), BF16), pltpu.SemaphoreType.DMA((2 * nz - 1,))],
        compiler_params=params(),
        cost_estimate=pl.CostEstimate(
            flops=2 * nz * rows * depth * width, bytes_accessed=2 * depth * (width + nz * rows), transcendentals=0
        ),
        name="project",
    )(pos, chip, *near, *far, w)


def enc_kernel(nz, groups, j, *refs):
    pos, chip = refs[0], refs[1]
    near, far = refs[2 : nz + 1], refs[nz + 1 : 2 * nz]
    wq, keys, values, wo, out, own, rows, sems = refs[2 * nz :]

    def place(ref, i):
        return [(ref.at[c, j], rows.at[:, i, c]) for c in range(2)]

    jobs = copies_in(pos, chip, near, far, place, sems, nz)
    begin(jobs)
    finish(jobs)
    width = wq.shape[0]
    own[...] = rows[pos[0]].reshape(-1, width)

    def step(i, carry):
        q = dot(rows[i].reshape(-1, width), wq[...]).astype(BF16)
        here = pl.ds(pl.multiple_of((groups * i + j) * GROUP, GROUP), GROUP)
        k, v = keys[here, :], values[here, :]
        att = []
        for h in range(0, k.shape[1], HEAD_DIM):
            scores = dot_t(q[:, h : h + HEAD_DIM], k[:, h : h + HEAD_DIM]) * SCALE
            raised = jnp.exp(scores - jnp.max(scores, axis=-1, keepdims=True))
            weights = (raised / jnp.sum(raised, axis=-1, keepdims=True)).astype(BF16)
            att.append(dot(weights, v[:, h : h + HEAD_DIM]).astype(BF16))
        out[i] = dot(jnp.concatenate(att, axis=1), wo[...]).astype(BF16)
        return carry

    lax.fori_loop(0, nz, step, 0)


def encode(pos, chip, near, far, wq, projected, wo, nz, j):
    _, groups, _, part, width = chip.shape
    tokens = projected.shape[0]
    heads = wq.shape[1]
    rows = nz * 2 * part
    return pl.pallas_call(
        functools.partial(enc_kernel, nz, groups, j),
        grid=(1,),
        in_specs=[SMEM]
        + [HBM] * (2 * nz - 1)
        + [
            VMEM,
            pl.BlockSpec((tokens, heads), lambda i: (0, 1)),
            pl.BlockSpec((tokens, heads), lambda i: (0, 2)),
            VMEM,
        ],
        out_specs=[VMEM, VMEM],
        out_shape=[
            jax.ShapeDtypeStruct((nz, rows, width), BF16),
            jax.ShapeDtypeStruct((rows, width), BF16),
        ],
        scratch_shapes=[
            pltpu.VMEM((nz, nz, 2, part, width), BF16),
            pltpu.SemaphoreType.DMA((2 * (2 * nz - 1),)),
        ],
        compiler_params=params(),
        cost_estimate=pl.CostEstimate(
            flops=nz * rows * heads * (4 * width + 4 * GROUP),
            bytes_accessed=4 * nz * rows * width + 4 * heads * (width + tokens),
            transcendentals=nz * rows * heads // 2,
        ),
        name="encode",
    )(pos, chip, *near, *far, wq, projected, projected, wo)


def norm_kernel(pos, parts, other, recv, swap, raw, gain, out):
    total = parts[0].astype(F32) + other[0].astype(F32)
    total += recv[...].astype(F32) + swap[...].astype(F32)
    combined = raw[...].astype(F32) + total
    factor = lax.rsqrt(jnp.mean(combined * combined, axis=-1, keepdims=True) + 1e-06)
    out[...] = (combined * factor * gain[...]).astype(BF16)


def normed(pos, parts, other, recv, swap, raw, gain):
    shape = recv.shape
    mine = pl.BlockSpec((1,) + shape, lambda i, pos: (pos[0], 0, 0))
    flat = pl.BlockSpec(shape, lambda i, pos: (0, 0))
    return pl.pallas_call(
        norm_kernel,
        grid_spec=pltpu.PrefetchScalarGridSpec(
            num_scalar_prefetch=1,
            grid=(1,),
            in_specs=[mine, mine, flat, flat, flat, pl.BlockSpec((1, shape[1]), lambda i, pos: (0, 0))],
            out_specs=flat,
        ),
        out_shape=jax.ShapeDtypeStruct(shape, BF16),
        compiler_params=params(),
        name="normed",
    )(pos, parts, other, recv, swap, raw, gain)


def cca_kernel(nz, groups, j, *refs):
    wrap = j == groups - 1
    pos, counts, chip = refs[0], refs[1], refs[2]
    near, far = refs[3 : nz + 2], refs[nz + 2 : 2 * nz + 1]
    refs = refs[2 * nz + 1 :]
    if wrap:
        previous, refs = refs[0], refs[1:]
    queries, wkv, wo, out, rows, out_w, att, sems = refs
    load = pltpu.make_async_copy(wo, out_w, sems.at[2 * nz - 1])
    load.start()
    jobs = copies_in(pos, chip, near, far, lambda ref, i: [(ref, rows.at[i])], sems, nz)
    if wrap:
        jobs.append((None, pltpu.make_async_copy(previous, rows.at[nz], sems.at[2 * nz])))
    begin(jobs)
    finish(jobs)
    heads = queries.shape[1]
    keys = rows.shape[1]
    slot = lax.broadcasted_iota(jnp.int32, (GROUP, keys), 1) // (keys // (4 * nz)) % 2
    first = lax.broadcasted_iota(jnp.int32, (GROUP, heads), 0) == 0

    def attend(block, i):
        kv = dot(rows[i], wkv[...]).astype(BF16)
        count = counts[block]
        here = pl.ds(pl.multiple_of(block * GROUP, GROUP), GROUP)
        q = queries[here, :]
        allowed = slot < count
        parts = []
        for h in range(0, heads, HEAD_DIM):
            scores = dot_t(q[:, h : h + HEAD_DIM], kv[:, h : h + HEAD_DIM]) * SCALE
            peak = jnp.max(jnp.where(allowed, scores, -1e30), axis=-1, keepdims=True)
            raised = jnp.where(allowed, jnp.exp(jnp.where(allowed, scores - peak, 0.0)), 0.0)
            total = jnp.where(count > 0, jnp.sum(raised, axis=-1, keepdims=True), 1.0)
            weights = (raised / total).astype(BF16)
            parts.append(dot(weights, kv[:, heads + h : heads + h + HEAD_DIM]).astype(BF16))
        return jnp.concatenate(parts, axis=1)

    if wrap:
        att[0] = attend(0, nz)

        def step(i, carry):
            got = attend(groups * (i + 1), i)
            att[i] = jnp.where(first, got, att[i])
            att[jnp.minimum(i + 1, nz)] = got
            return carry
    else:

        def step(i, carry):
            att[i] = attend(groups * i + j + 1, i)
            return carry

    lax.fori_loop(0, nz, step, 0)
    load.wait()
    for i in range(nz):
        out[i] = dot(att[i], out_w[...]).astype(BF16)


def cross(pos, counts, chip, near, far, previous, queries, wkv, wo, nz, groups, j):
    keys, width = chip.shape
    heads = queries.shape[1]
    model = wo.shape[1]
    extra = [] if previous is None else [previous]
    return pl.pallas_call(
        functools.partial(cca_kernel, nz, groups, j),
        in_specs=[SMEM, SMEM] + [HBM] * (2 * nz - 1 + len(extra)) + [VMEM, VMEM, HBM],
        out_specs=VMEM,
        out_shape=jax.ShapeDtypeStruct((nz, GROUP, model), BF16),
        scratch_shapes=[
            pltpu.VMEM((nz + 1, keys, width), BF16),
            pltpu.VMEM(wo.shape, BF16),
            pltpu.VMEM((nz + 1, GROUP, heads), BF16),
            pltpu.SemaphoreType.DMA((2 * nz + 1,)),
        ],
        compiler_params=params(),
        cost_estimate=pl.CostEstimate(
            flops=2 * nz * heads * (2 * keys * width + 2 * GROUP * keys + GROUP * model),
            bytes_accessed=2 * (heads * (2 * width + model) + nz * (keys * width + GROUP * model)),
            transcendentals=nz * GROUP * keys * heads // HEAD_DIM,
        ),
        name="cross",
    )(pos, counts, chip, *near, *far, *extra, queries, wkv, wo)


def local(
    tokens,
    nbr_embed,
    neighbour_table,
    valid_counts,
    dec_proj,
    enc_query,
    enc_out,
    enc_gain,
    nbr_proj,
    out_proj,
):
    nz = lax.axis_size("nbr") // 2
    n_seq = lax.axis_size("seq")
    seq_index = lax.axis_index("seq")
    member = lax.axis_index("nbr")
    z, core = member // 2, member % 2
    pos = jnp.stack([z, core]).astype(jnp.int32)
    rows_dev, model_width = tokens.shape
    local_width = dec_proj.shape[2]
    ch_grp, slots = neighbour_table.shape
    groups = ch_grp // nz
    tok_grp = ch_grp * GROUP
    nb_grp, share, enc_width = nbr_embed.shape

    def both(own, axis=0):
        got = swapped(own, nz)
        return jnp.concatenate([jnp.where(core == 0, own, got), jnp.where(core == 0, got, own)], axis=axis)

    tok_chip = both(tokens)
    ids = neighbour_table.reshape(nz, groups, slots).transpose(1, 0, 2).reshape(-1) - seq_index * nb_grp
    ordered = jnp.take(nbr_embed, ids, axis=0, mode="clip").reshape(1, groups, nz, slots * share, enc_width)
    nbr_chip = both(ordered)
    tok_near, tok_far = line_gather(tok_chip, nz)
    nbr_near, nbr_far = line_gather(nbr_chip, nz)

    projected = project(pos, tok_chip, tok_near, tok_far, dec_proj.reshape(model_width, 3 * local_width), nz)
    queries = jnp.pad(projected[:, :local_width], ((1, GROUP - 1), (0, 0)))
    wkv = nbr_proj.reshape(enc_width, 2 * local_width)
    counts = lax.dynamic_slice_in_dim(
        jnp.concatenate([jnp.zeros((1,), jnp.int32), valid_counts]), seq_index * ch_grp, ch_grp + 1, 0
    )
    starts = (seq_index * tok_grp) % SEQ_LEN == 0
    counts = jnp.where(starts & (jnp.arange(ch_grp + 1) == 0), 0, counts)

    order = [groups - 1] + list(range(groups - 1))
    parts = {j: encode(pos, nbr_chip, nbr_near, nbr_far, enc_query, projected, enc_out, nz, j) for j in order}
    enc_own = {}
    gathered = {}
    for j in order:
        part, raw = parts[j]
        other = swapped(part, nz)
        recv, swap = line_sums(part, other, z, core, nz)
        enc_own[j] = normed(pos, part, other, recv, swap, raw, enc_gain.reshape(1, -1))
        gathered[j] = line_gather(enc_own[j], nz)

    near, far = gathered[groups - 1]
    last = enc_own[groups - 1]
    for s in range(1, nz):
        last = jnp.where(z == nz - 1 - s, jnp.where(core == 0, far[s - 1], near[s - 1]), last)
    previous = lax.ppermute(last, "seq", [(i, i + 1) for i in range(n_seq - 1)])

    sums = {}
    for j in order[1:] + order[:1]:
        part = cross(
            pos, counts, enc_own[j], *gathered[j], previous if j == groups - 1 else None,
            queries, wkv, out_proj, nz, groups, j,
        )
        other = swapped(part, nz)
        recv, swap = line_sums(part, other, z, core, nz)
        total = lax.dynamic_index_in_dim(part, z, 0, False).astype(F32)
        total += lax.dynamic_index_in_dim(other, z, 0, False).astype(F32)
        sums[j] = (total + recv.astype(F32) + swap.astype(F32)).astype(BF16)
    turn = sums[groups - 1]
    chip_out = jnp.concatenate([turn[1:]] + [sums[j] for j in range(groups - 1)] + [turn[:1]], axis=0)
    cross_out = lax.dynamic_slice_in_dim(chip_out, core * rows_dev, rows_dev, 0)

    chip_enc = jnp.stack([enc_own[j] for j in range(groups)]).reshape(groups, 2 * nz, slots, share, enc_width)
    chip_enc = chip_enc.transpose(0, 2, 1, 3, 4).reshape(-1, enc_width)
    enc_rows = chip_enc.shape[0] // 2
    encoded = lax.dynamic_slice_in_dim(chip_enc, core * enc_rows, enc_rows, 0)
    return (cross_out, encoded)


def solution(mesh):
    return jax.shard_map(
        local,
        mesh=mesh,
        in_specs=(
            P(("seq", "nbr"), None),
            P("seq", "nbr", None),
            P("seq", None),
            P(),
            P(None, None, "nbr"),
            P(None, "nbr"),
            P("nbr", None),
            P(),
            P(None, None, "nbr"),
            P("nbr", None),
        ),
        out_specs=(P(("seq", "nbr"), None), P(("seq", "nbr"), None)),
        check_vma=False,
    )
```

time: 386 us -> 321 us (0.83)
  waiting for transfers between devices: 267 us -> 47.6 us
  starting transfers between devices: 3.56 us -> 140 us
  Pallas kernels: 0 us -> 67.8 us
  matrix products: 35 us -> 0 us
  between operations: 14.1 us -> 1.38 us
  local copies, waits for them, and re-layouts: 52 us -> 43.8 us
  other arithmetic: 13.9 us -> 18.3 us
    psum x1 -> x0, waiting for transfers between devices: 151 us -> none  [local(): lax.psum(jnp.dot(enc_att, enc_out, preferred_element_type=jnp.float32), '...]
    ppermute x1 -> x47, starting transfers between devices: 3.41 us -> 140 us  [the longest x12 46.9 us: line_sums(): recv = lax.ppermute(send.astype(BF16), 'nbr', up + down)]
    pallas_call x0 -> x7, Pallas kernels: none -> 67.8 us  [the longest x2 30.6 us: cross(): pl.pallas_call(functools.partial(cca_kernel, nz, groups, j), in_specs=[SM...]
    all_gather x2 -> x0, waiting for transfers between devices: 62.5 us -> none  [the longest x1 34.1 us: local(): lax.all_gather(tokens, 'nbr', axis=0, tiled=True)]
    reduce_scatter x1 -> x0, waiting for transfers between devices: 49.6 us -> none  [local(): lax.psum_scatter(jnp.dot(cca_att, out_proj, preferred_element_type=jnp.fl...]
    ppermute x1 -> x47, waiting for transfers between devices: 1.95 us -> 47.6 us  [the longest x12 23 us: line_gather(): held = lax.ppermute(held, 'nbr', up + down)]
    dot_general x9 -> x0, matrix products: 35 us -> none  [the longest x1 11.1 us: local(): jnp.dot(lax.all_gather(tokens, 'nbr', axis=0, tiled=True), dec_flat, pref...]
    reshape x4 -> x2, local copies, waits for them, and re-layouts: 3.97 us -> 16.7 us  [the longest x1 16.7 us: local(): dec_proj.reshape(model_width, 3 * local_width)]
  transfers between devices with their start and end apart: 5 -> 47, of which waited for: 5 -> 20; matrix products, arithmetic and copies ran while one was open for 11% -> 17% of each run, Pallas kernels for 0% -> 18%
where the time goes in v1:
time: 321 us; the launch traced here: 319 us
  starting transfers between devices  140 us (44%)
  Pallas kernels  67.8 us (21%)
  waiting for transfers between devices  47.6 us (15%)
  local copies, waits for them, and re-layouts  43.8 us (14%)
  other arithmetic  18.3 us (6%)
    ppermute x12, starting transfers between devices, line_sums(): recv = lax.ppermute(send.astype(BF16), 'nbr', up + down)  46.9 us
    ppermute x10, starting transfers between devices, swapped(): return lax.ppermute(x, 'nbr', [(n, n ^ 1) for n in range(2 * nz)])  41.1 us
    ppermute x12, starting transfers between devices, line_gather(): held = lax.ppermute(held, 'nbr', up + down)  32.6 us
    pallas_call x2, Pallas kernels, cross(): pl.pallas_call(functools.partial(cca_kernel, nz, groups, j), in_specs=[SM...  30.6 us
    unnamed x44, local copies, waits for them, and re-layouts  24 us
    ppermute x12, waiting for transfers between devices, line_gather(): held = lax.ppermute(held, 'nbr', up + down)  23 us
    pallas_call x2, Pallas kernels, encode(): pl.pallas_call(functools.partial(enc_kernel, nz, groups, j), grid=(1,), i...  20.2 us
    reshape x1, local copies, waits for them, and re-layouts, local(): dec_proj.reshape(model_width, 3 * local_width)  16.7 us
  transfers between devices with their start and end apart: 47, of which 20 were waited for; matrix products, arithmetic and copies ran while one was open for 17% of the time, Pallas kernels for 18%

profile of v1, /device:TPU:0, one launch (start us, length us, event | category | flops | bytes accessed | tf_op | source)
XLA Modules:
  0.0 318.5 jit_solution(2963532863398313999)
XLA Ops:
  1.2 1.7 collective-permute-done.7
  4.1 5.8 %collective-permute-start.8 = (bf16[128,4096]{1,0:T(8,128)(2,1)S(1)}, bf16[128,4096]{1,0:T(8,128)(2,1)}, u32[]{:S(2)}, u32[]{:S(2)}) collective-permute-start(bf16[128,4096]{1,0:T(8,128)(2,1)S(1)} %pad_maximum_fusion.refs_1_), channel_id=1, source_target_pairs={{0,2},{2,4},{4,6},{3,1},{5,3},{7,5},{8,10},{10,12},{12,14},{11,9},... | collective-permute-start | bytes 3145736 | tf_op jit(solution)/shard_map/ppermute | solution.py:43
  11.0 1.8 collective-permute-done
  12.9 8.4 %collective-permute-done.8.refs_2_ = bf16[128,4096]{1,0:T(8,128)(2,1)} collective-permute-done((bf16[128,4096]{1,0:T(8,128)(2,1)S(1)}, bf16[128,4096]{1,0:T(8,128)(2,1)}, u32[]{:S(2)}, u32[]{:S(2)}) %collective-permute-start.8) | collective-permute-done | bytes 1048608 | tf_op jit(solution)/shard_map/ppermute | solution.py:43
  21.3 1.6 collective-permute-start.9
  23.0 7.4 %collective-permute-start.1 = (bf16[2,2,4,32,896]{4,3,2,1,0:T(8,128)(2,1)S(1)}, bf16[2,2,4,32,896]{4,3,2,1,0:T(8,128)(2,1)S(1)}, u32[]{:S(2)}, u32[]{:S(2)}) collective-permute-start(bf16[2,2,4,32,896]{4,3,2,1,0:T(8,128)(2,1)S(1)} %pad_maximum_fusion.1.refs_1_), channel_id=1, source_target_pairs={{0,2},{2,4},{4,6},{3,1},{5,3},{7,5},{8,10},{10,12},{12,14},{11,9},... | collective-permute-start | bytes 2752520 | tf_op jit(solution)/shard_map/ppermute | solution.py:43
  30.4 10.8 %collective-permute-done.1.refs_2_ = bf16[2,2,4,32,896]{4,3,2,1,0:T(8,128)(2,1)S(1)} collective-permute-done((bf16[2,2,4,32,896]{4,3,2,1,0:T(8,128)(2,1)S(1)}, bf16[2,2,4,32,896]{4,3,2,1,0:T(8,128)(2,1)S(1)}, u32[]{:S(2)}, u32[]{:S(2)}) %collective-permute-start.1) | collective-permute-done | bytes 917536 | tf_op jit(solution)/shard_map/ppermute | solution.py:43
  42.0 1.7 collective-permute-start.10
  43.6 1.3 collective-permute-start.11
  44.9 1.6 collective-permute-start.3
  47.8 1.3 collective-permute-start.13
  49.1 1.3 collective-permute-start.4
  50.4 2.8 collective-permute-done.11.refs_5_
  55.5 1.3 collective-permute-start.6
  56.8 16.9 %copy.16 = bf16[4096,3,512]{0,2,1:T(8,128)(2,1)} copy(bf16[4096,3,512]{2,0,1:T(8,128)(2,1)} %param.14) | data formatting | bytes 25165824 | tf_op args[4]
  73.8 16.7 %copy.17.refs_8_ = bf16[4096,1536]{1,0:T(8,128)(2,1)} copy(bf16[4096,1536]{0,1:T(8,128)(2,1)} %bitcast.70) | data formatting | bytes 25165824 | tf_op jit(solution)/shard_map/reshape | solution.py:340
  93.0 12.9 %project.1.refs_9_.refs_10_ = bf16[512,1536]{1,0:T(8,128)(2,1)} custom-call(s32[2]{0:T(128)S(1)} %pad_add_fusion.refs_0_.pos, bf16[128,4096]{1,0:T(8,128)(2,1)S(1)} %copy-done.7, bf16[128,4096]{1,0:T(8,128)(2,1)} %collective-permute-done.8.refs_2_, bf16[128,4096]{1,0:T(8,128)(2,1)} %collective-permute-done.9.refs_3_, ...), custom_call_target="tpu_custom_call" | custom-call | flops 6442450944 | bytes 16777216 | tf_op jit(solution)/shard_map/project/pallas_call | solution.py:116
  105.9 10.1 %encode.2 = (bf16[4,256,896]{2,1,0:T(8,128)(2,1)}, bf16[256,896]{1,0:T(8,128)(2,1)S(1)}) custom-call(s32[2]{0:T(128)S(1)} %pad_add_fusion.refs_0_.pos, bf16[2,2,4,32,896]{4,3,2,1,0:T(8,128)(2,1)S(1)} %pad_maximum_fusion.1.refs_1_, bf16[2,2,4,32,896]{4,3,2,1,0:T(8,128)(2,1)S(1)} %collective-permute-done.1.refs_2_, ...), custom_call_target="tpu_custom_call" | custom-call | flops 2013265920 | bytes 6553600 | tf_op jit(solution)/shard_map/encode/pallas_call | solution.py:166
  116.8 27.8 %collective-permute-start.14 = (bf16[4,256,896]{2,1,0:T(8,128)(2,1)}, bf16[4,256,896]{2,1,0:T(8,128)(2,1)}, u32[]{:S(2)}, u32[]{:S(2)}) collective-permute-start(bf16[4,256,896]{2,1,0:T(8,128)(2,1)} %get-tuple-element.6.parts), channel_id=1, source_target_pairs={{0,1},{1,0},{2,3},{3,2},{4,5},{5,4},{6,7},{7,6},{8,9},{9,8},{10,11... | collective-permute-start | bytes 5505032 | tf_op jit(solution)/shard_map/ppermute | solution.py:35
  144.7 10.1 %encode.3 = (bf16[4,256,896]{2,1,0:T(8,128)(2,1)}, bf16[256,896]{1,0:T(8,128)(2,1)S(1)}) custom-call(s32[2]{0:T(128)S(1)} %pad_add_fusion.refs_0_.pos, bf16[2,2,4,32,896]{4,3,2,1,0:T(8,128)(2,1)S(1)} %pad_maximum_fusion.1.refs_1_, bf16[2,2,4,32,896]{4,3,2,1,0:T(8,128)(2,1)S(1)} %collective-permute-done.1.refs_2_, ...), custom_call_target="tpu_custom_call" | custom-call | flops 2013265920 | bytes 6553600 | tf_op jit(solution)/shard_map/encode/pallas_call | solution.py:166
  154.9 1.4 fusion.16
  156.3 2.1 collective-permute-start.15
  160.3 2.1 collective-permute-start.32
  163.6 1.5 fusion.10
  165.1 5.3 %collective-permute-start.16 = (bf16[256,896]{1,0:T(8,128)(2,1)S(1)}, bf16[256,896]{1,0:T(8,128)(2,1)}, u32[]{:S(2)}, u32[]{:S(2)}) collective-permute-start(bf16[256,896]{1,0:T(8,128)(2,1)S(1)} %fusion.10), channel_id=1, source_target_pairs={{0,2},{2,4},{5,3},{7,5},{8,10},{10,12},{13,11},{15,13},{16,18},{18... | collective-permute-start | bytes 1376264 | tf_op jit(solution)/shard_map/ppermute | solution.py:61
  170.4 1.3 fusion.8
  171.7 3.5 %collective-permute-start.33 = (bf16[256,896]{1,0:T(8,128)(2,1)S(1)}, bf16[256,896]{1,0:T(8,128)(2,1)}, u32[]{:S(2)}, u32[]{:S(2)}) collective-permute-start(bf16[256,896]{1,0:T(8,128)(2,1)S(1)} %fusion.8), channel_id=1, source_target_pairs={{0,2},{2,4},{5,3},{7,5},{8,10},{10,12},{13,11},{15,13},{16,18},{18... | collective-permute-start | bytes 1376264 | tf_op jit(solution)/shard_map/ppermute | solution.py:61
  175.6 1.6 fusion.11
  177.2 4.4 %collective-permute-start.17 = (bf16[256,896]{1,0:T(8,128)(2,1)S(1)}, bf16[256,896]{1,0:T(8,128)(2,1)S(1)}, u32[]{:S(2)}, u32[]{:S(2)}) collective-permute-start(bf16[256,896]{1,0:T(8,128)(2,1)S(1)} %fusion.11), channel_id=1, source_target_pairs={{0,2},{2,4},{4,6},{3,1},{5,3},{7,5},{8,10},{10,12},{12,14},{11,9},... | collective-permute-start | bytes 1376264 | tf_op jit(solution)/shard_map/ppermute | solution.py:61
  181.6 1.3 fusion.9
  182.9 3.4 %collective-permute-start.34 = (bf16[256,896]{1,0:T(8,128)(2,1)S(1)}, bf16[256,896]{1,0:T(8,128)(2,1)S(1)}, u32[]{:S(2)}, u32[]{:S(2)}) collective-permute-start(bf16[256,896]{1,0:T(8,128)(2,1)S(1)} %fusion.9), channel_id=1, source_target_pairs={{0,2},{2,4},{4,6},{3,1},{5,3},{7,5},{8,10},{10,12},{12,14},{11,9},... | collective-permute-start | bytes 1376264 | tf_op jit(solution)/shard_map/ppermute | solution.py:61
  187.5 2.5 collective-permute-start.18
  190.0 2.4 collective-permute-done.34.recv
  192.4 2.6 collective-permute-start.35
  195.1 2.0 normed.2.refs_2_
  197.1 3.7 %collective-permute-start.19 = (bf16[256,896]{1,0:T(8,128)(2,1)S(1)}, bf16[256,896]{1,0:T(8,128)(2,1)S(1)}, u32[]{:S(2)}, u32[]{:S(2)}) collective-permute-start(bf16[256,896]{1,0:T(8,128)(2,1)S(1)} %normed.2.refs_2_), channel_id=1, source_target_pairs={{0,2},{2,4},{4,6},{3,1},{5,3},{7,5},{8,10},{10,12},{12,14},{11,9},... | collective-permute-start | bytes 1376264 | tf_op jit(solution)/shard_map/ppermute | solution.py:43
  200.8 2.0 normed.3.refs_2_
  202.8 4.4 %collective-permute-start.36 = (bf16[256,896]{1,0:T(8,128)(2,1)S(1)}, bf16[256,896]{1,0:T(8,128)(2,1)}, u32[]{:S(2)}, u32[]{:S(2)}) collective-permute-start(bf16[256,896]{1,0:T(8,128)(2,1)S(1)} %normed.3.refs_2_), channel_id=1, source_target_pairs={{0,2},{2,4},{4,6},{3,1},{5,3},{7,5},{8,10},{10,12},{12,14},{11,9},... | collective-permute-start | bytes 1376264 | tf_op jit(solution)/shard_map/ppermute | solution.py:43
  207.1 1.5 collective-permute-start.20
  208.6 3.7 %collective-permute-done.36.refs_3_ = bf16[256,896]{1,0:T(8,128)(2,1)} collective-permute-done((bf16[256,896]{1,0:T(8,128)(2,1)S(1)}, bf16[256,896]{1,0:T(8,128)(2,1)}, u32[]{:S(2)}, u32[]{:S(2)}) %collective-permute-start.36) | collective-permute-done | bytes 458784 | tf_op jit(solution)/shard_map/ppermute | solution.py:43
  212.4 1.4 collective-permute-start.37
  213.8 1.4 collective-permute-start.21
  216.5 1.4 collective-permute-start.38
  219.3 1.3 collective-permute-start.24
  220.6 1.3 collective-permute-start.39
  224.0 1.3 collective-permute-start.41
  225.3 2.0 copy.19
  229.0 1.3 select_select_fusion
  230.3 3.6 %collective-permute-start.25 = (bf16[256,896]{1,0:T(8,128)(2,1)S(1)}, bf16[256,896]{1,0:T(8,128)(2,1)S(1)}, u32[]{:S(2)}, u32[]{:S(2)}) collective-permute-start(bf16[256,896]{1,0:T(8,128)(2,1)S(1)} %select_select_fusion), channel_id=1, source_target_pairs={{0,8},{8,16},{16,24},{1,9},{9,17},{17,25},{2,10},{10,18},{18,26},{... | collective-permute-start | bytes 1376264 | tf_op jit(solution)/shard_map/ppermute | solution.py:364
  233.9 2.0 collective-permute-done.41.refs_8_
  235.9 14.5 %cross.3 = bf16[4,64,4096]{2,1,0:T(8,128)(2,1)} custom-call(s32[2]{0:T(128)S(1)} %pad_add_fusion.refs_0_.pos, s32[9]{0:T(128)S(1)} %and_select_fusion.refs_1_, bf16[256,896]{1,0:T(8,128)(2,1)S(1)} %normed.3.refs_2_, bf16[256,896]{1,0:T(8,128)(2,1)} %collective-permute-done.36.refs_3_, bf16[256,896]{1,0:T(8,128)(2,1)} %collective-permute-done.37.refs_4_, ...), custom_call_target="tpu_custom_call" | custom-call | flops 3087007744 | bytes 9961472 | tf_op jit(solution)/shard_map/cross/pallas_call | solution.py:283
  250.4 7.4 %collective-permute-start.42 = (bf16[4,64,4096]{2,1,0:T(8,128)(2,1)}, bf16[4,64,4096]{2,1,0:T(8,128)(2,1)S(1)}, u32[]{:S(2)}, u32[]{:S(2)}) collective-permute-start(bf16[4,64,4096]{2,1,0:T(8,128)(2,1)} %cross.3), channel_id=1, source_target_pairs={{0,1},{1,0},{2,3},{3,2},{4,5},{5,4},{6,7},{7,6},{8,9},{9,8},{10,11... | collective-permute-start | bytes 6291464 | tf_op jit(solution)/shard_map/ppermute | solution.py:35
  257.8 16.1 %cross.2 = bf16[4,64,4096]{2,1,0:T(8,128)(2,1)} custom-call(s32[2]{0:T(128)S(1)} %pad_add_fusion.refs_0_.pos, s32[9]{0:T(128)S(1)} %and_select_fusion.refs_1_, bf16[256,896]{1,0:T(8,128)(2,1)S(1)} %normed.2.refs_2_, bf16[256,896]{1,0:T(8,128)(2,1)S(1)} %collective-permute-done.19.refs_3_, bf16[256,896]{1,0:T(8,128)(2,1)} %collective-permute-done.20.refs_4_, ...), custom_call_target="tpu_custom_call" | custom-call | flops 3087007744 | bytes 9961472 | tf_op jit(solution)/shard_map/cross/pallas_call | solution.py:283
  274.2 4.5 %collective-permute-start.43 = (bf16[64,4096]{1,0:T(8,128)(2,1)S(1)}, bf16[64,4096]{1,0:T(8,128)(2,1)S(1)}, u32[]{:S(2)}, u32[]{:S(2)}) collective-permute-start(bf16[64,4096]{1,0:T(8,128)(2,1)S(1)} %fusion.13), channel_id=1, source_target_pairs={{0,2},{7,5},{8,10},{15,13},{16,18},{23,21},{24,26},{31,29}} | collective-permute-start | bytes 1572872 | tf_op jit(solution)/shard_map/ppermute | solution.py:61
  278.7 1.6 fusion.12
  280.3 3.8 %collective-permute-start.27 = (bf16[64,4096]{1,0:T(8,128)(2,1)S(1)}, bf16[64,4096]{1,0:T(8,128)(2,1)S(1)}, u32[]{:S(2)}, u32[]{:S(2)}) collective-permute-start(bf16[64,4096]{1,0:T(8,128)(2,1)S(1)} %fusion.12), channel_id=1, source_target_pairs={{0,2},{7,5},{8,10},{15,13},{16,18},{23,21},{24,26},{31,29}} | collective-permute-start | bytes 1572872 | tf_op jit(solution)/shard_map/ppermute | solution.py:61
  285.6 4.4 %collective-permute-start.44 = (bf16[64,4096]{1,0:T(8,128)(2,1)S(1)}, bf16[64,4096]{1,0:T(8,128)(2,1)S(1)}, u32[]{:S(2)}, u32[]{:S(2)}) collective-permute-start(bf16[64,4096]{1,0:T(8,128)(2,1)S(1)} %fusion), channel_id=1, source_target_pairs={{0,2},{2,4},{5,3},{7,5},{8,10},{10,12},{13,11},{15,13},{16,18},{18... | collective-permute-start | bytes 1572872 | tf_op jit(solution)/shard_map/ppermute | solution.py:61
  291.2 4.4 %collective-permute-start.28 = (bf16[64,4096]{1,0:T(8,128)(2,1)S(1)}, bf16[64,4096]{1,0:T(8,128)(2,1)S(1)}, u32[]{:S(2)}, u32[]{:S(2)}) collective-permute-start(bf16[64,4096]{1,0:T(8,128)(2,1)S(1)} %fusion.4), channel_id=1, source_target_pairs={{0,2},{2,4},{5,3},{7,5},{8,10},{10,12},{13,11},{15,13},{16,18},{18... | collective-permute-start | bytes 1572872 | tf_op jit(solution)/shard_map/ppermute | solution.py:61
  296.8 4.4 %collective-permute-start.45 = (bf16[64,4096]{1,0:T(8,128)(2,1)S(1)}, bf16[64,4096]{1,0:T(8,128)(2,1)S(1)}, u32[]{:S(2)}, u32[]{:S(2)}) collective-permute-start(bf16[64,4096]{1,0:T(8,128)(2,1)S(1)} %fusion.1), channel_id=1, source_target_pairs={{0,2},{2,4},{4,6},{3,1},{5,3},{7,5},{8,10},{10,12},{12,14},{11,9},... | collective-permute-start | bytes 1572872 | tf_op jit(solution)/shard_map/ppermute | solution.py:61
  302.5 4.4 %collective-permute-start.29 = (bf16[64,4096]{1,0:T(8,128)(2,1)S(1)}, bf16[64,4096]{1,0:T(8,128)(2,1)S(1)}, u32[]{:S(2)}, u32[]{:S(2)}) collective-permute-start(bf16[64,4096]{1,0:T(8,128)(2,1)S(1)} %fusion.5), channel_id=1, source_target_pairs={{0,2},{2,4},{4,6},{3,1},{5,3},{7,5},{8,10},{10,12},{12,14},{11,9},... | collective-permute-start | bytes 1572872 | tf_op jit(solution)/shard_map/ppermute | solution.py:61
  308.9 4.6 %collective-permute-done.29 = bf16[64,4096]{1,0:T(8,128)(2,1)S(1)} collective-permute-done((bf16[64,4096]{1,0:T(8,128)(2,1)S(1)}, bf16[64,4096]{1,0:T(8,128)(2,1)S(1)}, u32[]{:S(2)}, u32[]{:S(2)}) %collective-permute-start.29) | collective-permute-done | bytes 524320 | tf_op jit(solution)/shard_map/ppermute | solution.py:61
  313.5 1.5 fusion.3
  315.5 1.5 fusion.7
  317.1 1.4 fusion.15
  (119 shorter events, 29.2 us)
Async XLA Ops:
  0.6 9.6 %copy-start = (bf16[16,16,896]{2,1,0:T(8,128)(2,1)S(1)}, bf16[16,16,896]{2,1,0:T(8,128)(2,1)}, u32[]{:S(2)}) copy-start(bf16[16,16,896]{2,1,0:T(8,128)(2,1)} %param.11) | copy-start | bytes 1376260
  0.6 2.3 collective-permute-start.7
  1.2 8.8 %copy-start.19 = (s32[8,2]{0,1:T(2,128)S(1)}, s32[8,2]{0,1:T(2,128)}, u32[]{:S(2)}) copy-start(s32[8,2]{0,1:T(2,128)} %param.12) | copy-start | bytes 196
  4.1 18.8 %copy-start.6 = (bf16[128,4096]{1,0:T(8,128)(2,1)}, bf16[128,4096]{1,0:T(8,128)(2,1)S(1)}, u32[]{:S(2)}) copy-start(bf16[128,4096]{1,0:T(8,128)(2,1)S(1)} %pad_maximum_fusion.refs_1_) | copy-start | bytes 3145732
  4.1 17.2 %collective-permute-start.8 = (bf16[128,4096]{1,0:T(8,128)(2,1)S(1)}, bf16[128,4096]{1,0:T(8,128)(2,1)}, u32[]{:S(2)}, u32[]{:S(2)}) collective-permute-start(bf16[128,4096]{1,0:T(8,128)(2,1)S(1)} %pad_maximum_fusion.refs_1_), channel_id=1, source_target_pairs={{0,2},{2,4},{4,6},{3,1},{5,3},{7,5},{8,10},{10,12},{12,14},{11,9},... | collective-permute-start | bytes 3145736 | tf_op jit(solution)/shard_map/ppermute | solution.py:43
  10.9 1.9 collective-permute-start
  21.3 20.7 %collective-permute-start.9 = (bf16[128,4096]{1,0:T(8,128)(2,1)}, bf16[128,4096]{1,0:T(8,128)(2,1)}, u32[]{:S(2)}, u32[]{:S(2)}) collective-permute-start(bf16[128,4096]{1,0:T(8,128)(2,1)} %collective-permute-done.8.refs_2_), channel_id=1, source_target_pairs={{2,4},{4,6},{3,1},{5,3},{10,12},{12,14},{11,9},{13,11},{18,20},{20... | collective-permute-start | bytes 3145736 | tf_op jit(solution)/shard_map/ppermute | solution.py:43
  23.0 18.2 %collective-permute-start.1 = (bf16[2,2,4,32,896]{4,3,2,1,0:T(8,128)(2,1)S(1)}, bf16[2,2,4,32,896]{4,3,2,1,0:T(8,128)(2,1)S(1)}, u32[]{:S(2)}, u32[]{:S(2)}) collective-permute-start(bf16[2,2,4,32,896]{4,3,2,1,0:T(8,128)(2,1)S(1)} %pad_maximum_fusion.1.refs_1_), channel_id=1, source_target_pairs={{0,2},{2,4},{4,6},{3,1},{5,3},{7,5},{8,10},{10,12},{12,14},{11,9},... | collective-permute-start | bytes 2752520 | tf_op jit(solution)/shard_map/ppermute | solution.py:43
  41.2 3.7 %collective-permute-start.2 = (bf16[2,2,4,32,896]{4,3,2,1,0:T(8,128)(2,1)S(1)}, bf16[2,2,4,32,896]{4,3,2,1,0:T(8,128)(2,1)S(1)}, u32[]{:S(2)}, u32[]{:S(2)}) collective-permute-start(bf16[2,2,4,32,896]{4,3,2,1,0:T(8,128)(2,1)S(1)} %collective-permute-done.1.refs_2_), channel_id=1, source_target_pairs={{2,4},{4,6},{3,1},{5,3},{10,12},{12,14},{11,9},{13,11},{18,20},{20... | collective-permute-start | bytes 2752520 | tf_op jit(solution)/shard_map/ppermute | solution.py:43
  42.0 5.9 %collective-permute-start.10 = (bf16[128,4096]{1,0:T(8,128)(2,1)}, bf16[128,4096]{1,0:T(8,128)(2,1)}, u32[]{:S(2)}, u32[]{:S(2)}) collective-permute-start(bf16[128,4096]{1,0:T(8,128)(2,1)} %collective-permute-done.9.refs_3_), channel_id=1, source_target_pairs={{4,6},{3,1},{12,14},{11,9},{20,22},{19,17},{28,30},{27,25}} | collective-permute-start | bytes 3145736 | tf_op jit(solution)/shard_map/ppermute | solution.py:43
  43.6 9.6 %collective-permute-start.11 = (bf16[128,4096]{1,0:T(8,128)(2,1)}, bf16[128,4096]{1,0:T(8,128)(2,1)S(1)}, u32[]{:S(2)}, u32[]{:S(2)}) collective-permute-start(bf16[128,4096]{1,0:T(8,128)(2,1)} %collective-permute-done.8.refs_2_), channel_id=1, source_target_pairs={{2,3},{4,5},{6,7},{1,0},{3,2},{5,4},{10,11},{12,13},{14,15},{9,8},... | collective-permute-start | bytes 3145736 | tf_op jit(solution)/shard_map/ppermute | solution.py:46
  44.9 10.6 %collective-permute-start.3 = (bf16[2,2,4,32,896]{4,3,2,1,0:T(8,128)(2,1)S(1)}, bf16[2,2,4,32,896]{4,3,2,1,0:T(8,128)(2,1)}, u32[]{:S(2)}, u32[]{:S(2)}) collective-permute-start(bf16[2,2,4,32,896]{4,3,2,1,0:T(8,128)(2,1)S(1)} %collective-permute-done.2.refs_3_), channel_id=1, source_target_pairs={{4,6},{3,1},{12,14},{11,9},{20,22},{19,17},{28,30},{27,25}} | collective-permute-start | bytes 2752520 | tf_op jit(solution)/shard_map/ppermute | solution.py:43
  46.5 44.0 %collective-permute-start.12 = (bf16[128,4096]{1,0:T(8,128)(2,1)}, bf16[128,4096]{1,0:T(8,128)(2,1)}, u32[]{:S(2)}, u32[]{:S(2)}) collective-permute-start(bf16[128,4096]{1,0:T(8,128)(2,1)} %collective-permute-done.9.refs_3_), channel_id=1, source_target_pairs={{4,5},{6,7},{1,0},{3,2},{12,13},{14,15},{9,8},{11,10},{20,21},{22,... | collective-permute-start | bytes 3145736 | tf_op jit(solution)/shard_map/ppermute | solution.py:46
  47.8 42.7 %collective-permute-start.13 = (bf16[128,4096]{1,0:T(8,128)(2,1)}, bf16[128,4096]{1,0:T(8,128)(2,1)}, u32[]{:S(2)}, u32[]{:S(2)}) collective-permute-start(bf16[128,4096]{1,0:T(8,128)(2,1)} %collective-permute-done.10.refs_4_), channel_id=1, source_target_pairs={{6,7},{1,0},{14,15},{9,8},{22,23},{17,16},{30,31},{25,24}} | collective-permute-start | bytes 3145736 | tf_op jit(solution)/shard_map/ppermute | solution.py:46
  49.1 56.8 %collective-permute-start.4 = (bf16[2,2,4,32,896]{4,3,2,1,0:T(8,128)(2,1)S(1)}, bf16[2,2,4,32,896]{4,3,2,1,0:T(8,128)(2,1)}, u32[]{:S(2)}, u32[]{:S(2)}) collective-permute-start(bf16[2,2,4,32,896]{4,3,2,1,0:T(8,128)(2,1)S(1)} %collective-permute-done.1.refs_2_), channel_id=1, source_target_pairs={{2,3},{4,5},{6,7},{1,0},{3,2},{5,4},{10,11},{12,13},{14,15},{9,8},... | collective-permute-start | bytes 2752520 | tf_op jit(solution)/shard_map/ppermute | solution.py:46
  54.2 51.7 %collective-permute-start.5 = (bf16[2,2,4,32,896]{4,3,2,1,0:T(8,128)(2,1)S(1)}, bf16[2,2,4,32,896]{4,3,2,1,0:T(8,128)(2,1)}, u32[]{:S(2)}, u32[]{:S(2)}) collective-permute-start(bf16[2,2,4,32,896]{4,3,2,1,0:T(8,128)(2,1)S(1)} %collective-permute-done.2.refs_3_), channel_id=1, source_target_pairs={{4,5},{6,7},{1,0},{3,2},{12,13},{14,15},{9,8},{11,10},{20,21},{22,... | collective-permute-start | bytes 2752520 | tf_op jit(solution)/shard_map/ppermute | solution.py:46
  55.5 50.4 %collective-permute-start.6 = (bf16[2,2,4,32,896]{4,3,2,1,0:T(8,128)(2,1)}, bf16[2,2,4,32,896]{4,3,2,1,0:T(8,128)(2,1)}, u32[]{:S(2)}, u32[]{:S(2)}) collective-permute-start(bf16[2,2,4,32,896]{4,3,2,1,0:T(8,128)(2,1)} %collective-permute-done.3.refs_4_), channel_id=1, source_target_pairs={{6,7},{1,0},{14,15},{9,8},{22,23},{17,16},{30,31},{25,24}} | collective-permute-start | bytes 2752520 | tf_op jit(solution)/shard_map/ppermute | solution.py:46
  90.5 1.2 copy-start.7
  116.8 38.1 %collective-permute-start.14 = (bf16[4,256,896]{2,1,0:T(8,128)(2,1)}, bf16[4,256,896]{2,1,0:T(8,128)(2,1)}, u32[]{:S(2)}, u32[]{:S(2)}) collective-permute-start(bf16[4,256,896]{2,1,0:T(8,128)(2,1)} %get-tuple-element.6.parts), channel_id=1, source_target_pairs={{0,1},{1,0},{2,3},{3,2},{4,5},{5,4},{6,7},{7,6},{8,9},{9,8},{10,11... | collective-permute-start | bytes 5505032 | tf_op jit(solution)/shard_map/ppermute | solution.py:35
  154.8 10.3 %copy-start.8 = (bf16[256,896]{1,0:T(8,128)(2,1)}, bf16[256,896]{1,0:T(8,128)(2,1)S(1)}, u32[]{:S(2)}) copy-start(bf16[256,896]{1,0:T(8,128)(2,1)S(1)} %get-tuple-element.9.raw) | copy-start | bytes 1376260
  154.8 4.2 %collective-permute-start.31 = (bf16[4,256,896]{2,1,0:T(8,128)(2,1)}, bf16[4,256,896]{2,1,0:T(8,128)(2,1)}, u32[]{:S(2)}, u32[]{:S(2)}) collective-permute-start(bf16[4,256,896]{2,1,0:T(8,128)(2,1)} %get-tuple-element.8.parts), channel_id=1, source_target_pairs={{0,1},{1,0},{2,3},{3,2},{4,5},{5,4},{6,7},{7,6},{8,9},{9,8},{10,11... | collective-permute-start | bytes 5505032 | tf_op jit(solution)/shard_map/ppermute | solution.py:35
  154.9 15.5 %copy-start.2 = (bf16[4,256,896]{2,1,0:T(8,128)(2,1)S(1)}, bf16[4,256,896]{2,1,0:T(8,128)(2,1)}, u32[]{:S(2)}) copy-start(bf16[4,256,896]{2,1,0:T(8,128)(2,1)} %get-tuple-element.8.parts) | copy-start | bytes 5505028
  156.3 7.3 %collective-permute-start.15 = (bf16[256,896]{1,0:T(8,128)(2,1)S(1)}, bf16[256,896]{1,0:T(8,128)(2,1)}, u32[]{:S(2)}, u32[]{:S(2)}) collective-permute-start(bf16[256,896]{1,0:T(8,128)(2,1)S(1)} %fusion.16), channel_id=1, source_target_pairs={{0,2},{7,5},{8,10},{15,13},{16,18},{23,21},{24,26},{31,29}} | collective-permute-start | bytes 1376264 | tf_op jit(solution)/shard_map/ppermute | solution.py:61
  160.3 10.1 %collective-permute-start.32 = (bf16[256,896]{1,0:T(8,128)(2,1)S(1)}, bf16[256,896]{1,0:T(8,128)(2,1)}, u32[]{:S(2)}, u32[]{:S(2)}) collective-permute-start(bf16[256,896]{1,0:T(8,128)(2,1)S(1)} %fusion.17), channel_id=1, source_target_pairs={{0,2},{7,5},{8,10},{15,13},{16,18},{23,21},{24,26},{31,29}} | collective-permute-start | bytes 1376264 | tf_op jit(solution)/shard_map/ppermute | solution.py:61
  165.1 10.5 %collective-permute-start.16 = (bf16[256,896]{1,0:T(8,128)(2,1)S(1)}, bf16[256,896]{1,0:T(8,128)(2,1)}, u32[]{:S(2)}, u32[]{:S(2)}) collective-permute-start(bf16[256,896]{1,0:T(8,128)(2,1)S(1)} %fusion.10), channel_id=1, source_target_pairs={{0,2},{2,4},{5,3},{7,5},{8,10},{10,12},{13,11},{15,13},{16,18},{18... | collective-permute-start | bytes 1376264 | tf_op jit(solution)/shard_map/ppermute | solution.py:61
  171.7 23.3 %copy-start.18 = (f32[896]{0:T(1024)S(1)}, f32[896]{0:T(1024)}, u32[]{:S(2)}) copy-start(f32[896]{0:T(1024)} %param.17) | copy-start | bytes 10756
  171.7 23.3 %copy-start.11 = (bf16[256,896]{1,0:T(8,128)(2,1)S(1)}, bf16[256,896]{1,0:T(8,128)(2,1)}, u32[]{:S(2)}) copy-start(bf16[256,896]{1,0:T(8,128)(2,1)} %copy-done.10) | copy-start | bytes 1376260
  171.7 9.8 %collective-permute-start.33 = (bf16[256,896]{1,0:T(8,128)(2,1)S(1)}, bf16[256,896]{1,0:T(8,128)(2,1)}, u32[]{:S(2)}, u32[]{:S(2)}) collective-permute-start(bf16[256,896]{1,0:T(8,128)(2,1)S(1)} %fusion.8), channel_id=1, source_target_pairs={{0,2},{2,4},{5,3},{7,5},{8,10},{10,12},{13,11},{15,13},{16,18},{18... | collective-permute-start | bytes 1376264 | tf_op jit(solution)/shard_map/ppermute | solution.py:61
  175.3 19.8 %copy-start.3 = (bf16[4,256,896]{2,1,0:T(8,128)(2,1)S(1)}, bf16[4,256,896]{2,1,0:T(8,128)(2,1)}, u32[]{:S(2)}) copy-start(bf16[4,256,896]{2,1,0:T(8,128)(2,1)} %get-tuple-element.6.parts) | copy-start | bytes 5505028
  177.2 10.3 %collective-permute-start.17 = (bf16[256,896]{1,0:T(8,128)(2,1)S(1)}, bf16[256,896]{1,0:T(8,128)(2,1)S(1)}, u32[]{:S(2)}, u32[]{:S(2)}) collective-permute-start(bf16[256,896]{1,0:T(8,128)(2,1)S(1)} %fusion.11), channel_id=1, source_target_pairs={{0,2},{2,4},{4,6},{3,1},{5,3},{7,5},{8,10},{10,12},{12,14},{11,9},... | collective-permute-start | bytes 1376264 | tf_op jit(solution)/shard_map/ppermute | solution.py:61
  182.9 9.5 %collective-permute-start.34 = (bf16[256,896]{1,0:T(8,128)(2,1)S(1)}, bf16[256,896]{1,0:T(8,128)(2,1)S(1)}, u32[]{:S(2)}, u32[]{:S(2)}) collective-permute-start(bf16[256,896]{1,0:T(8,128)(2,1)S(1)} %fusion.9), channel_id=1, source_target_pairs={{0,2},{2,4},{4,6},{3,1},{5,3},{7,5},{8,10},{10,12},{12,14},{11,9},... | collective-permute-start | bytes 1376264 | tf_op jit(solution)/shard_map/ppermute | solution.py:61
  187.5 7.5 %collective-permute-start.18 = (bf16[256,896]{1,0:T(8,128)(2,1)S(1)}, bf16[256,896]{1,0:T(8,128)(2,1)S(1)}, u32[]{:S(2)}, u32[]{:S(2)}) collective-permute-start(bf16[256,896]{1,0:T(8,128)(2,1)S(1)} %collective-permute-done.17.recv), channel_id=1, source_target_pairs={{0,1},{1,0},{2,3},{3,2},{4,5},{5,4},{6,7},{7,6},{8,9},{9,8},{10,11... | collective-permute-start | bytes 1376264 | tf_op jit(solution)/shard_map/ppermute | solution.py:35
  192.4 8.3 %collective-permute-start.35 = (bf16[256,896]{1,0:T(8,128)(2,1)S(1)}, bf16[256,896]{1,0:T(8,128)(2,1)S(1)}, u32[]{:S(2)}, u32[]{:S(2)}) collective-permute-start(bf16[256,896]{1,0:T(8,128)(2,1)S(1)} %collective-permute-done.34.recv), channel_id=1, source_target_pairs={{0,1},{1,0},{2,3},{3,2},{4,5},{5,4},{6,7},{7,6},{8,9},{9,8},{10,11... | collective-permute-start | bytes 1376264 | tf_op jit(solution)/shard_map/ppermute | solution.py:35
  195.1 5.7 %copy-start.9 = (bf16[256,896]{1,0:T(8,128)(2,1)S(1)}, bf16[256,896]{1,0:T(8,128)(2,1)}, u32[]{:S(2)}) copy-start(bf16[256,896]{1,0:T(8,128)(2,1)} %copy-done.8) | copy-start | bytes 1376260
  197.1 10.1 %collective-permute-start.19 = (bf16[256,896]{1,0:T(8,128)(2,1)S(1)}, bf16[256,896]{1,0:T(8,128)(2,1)S(1)}, u32[]{:S(2)}, u32[]{:S(2)}) collective-permute-start(bf16[256,896]{1,0:T(8,128)(2,1)S(1)} %normed.2.refs_2_), channel_id=1, source_target_pairs={{0,2},{2,4},{4,6},{3,1},{5,3},{7,5},{8,10},{10,12},{12,14},{11,9},... | collective-permute-start | bytes 1376264 | tf_op jit(solution)/shard_map/ppermute | solution.py:43
  200.7 24.5 %copy-start.20 = (s32[32]{0:T(128)S(1)}, s32[32]{0:T(128)}, u32[]{:S(2)}) copy-start(s32[32]{0:T(128)} %param.13) | copy-start | bytes 388
  202.8 9.6 %collective-permute-start.36 = (bf16[256,896]{1,0:T(8,128)(2,1)S(1)}, bf16[256,896]{1,0:T(8,128)(2,1)}, u32[]{:S(2)}, u32[]{:S(2)}) collective-permute-start(bf16[256,896]{1,0:T(8,128)(2,1)S(1)} %normed.3.refs_2_), channel_id=1, source_target_pairs={{0,2},{2,4},{4,6},{3,1},{5,3},{7,5},{8,10},{10,12},{12,14},{11,9},... | collective-permute-start | bytes 1376264 | tf_op jit(solution)/shard_map/ppermute | solution.py:43
  207.1 6.7 %collective-permute-start.20 = (bf16[256,896]{1,0:T(8,128)(2,1)S(1)}, bf16[256,896]{1,0:T(8,128)(2,1)}, u32[]{:S(2)}, u32[]{:S(2)}) collective-permute-start(bf16[256,896]{1,0:T(8,128)(2,1)S(1)} %collective-permute-done.19.refs_3_), channel_id=1, source_target_pairs={{2,4},{4,6},{3,1},{5,3},{10,12},{12,14},{11,9},{13,11},{18,20},{20... | collective-permute-start | bytes 1376264 | tf_op jit(solution)/shard_map/ppermute | solution.py:43
  212.4 4.2 %collective-permute-start.37 = (bf16[256,896]{1,0:T(8,128)(2,1)}, bf16[256,896]{1,0:T(8,128)(2,1)}, u32[]{:S(2)}, u32[]{:S(2)}) collective-permute-start(bf16[256,896]{1,0:T(8,128)(2,1)} %collective-permute-done.36.refs_3_), channel_id=1, source_target_pairs={{2,4},{4,6},{3,1},{5,3},{10,12},{12,14},{11,9},{13,11},{18,20},{20... | collective-permute-start | bytes 1376264 | tf_op jit(solution)/shard_map/ppermute | solution.py:43
  213.8 5.5 %collective-permute-start.21 = (bf16[256,896]{1,0:T(8,128)(2,1)}, bf16[256,896]{1,0:T(8,128)(2,1)}, u32[]{:S(2)}, u32[]{:S(2)}) collective-permute-start(bf16[256,896]{1,0:T(8,128)(2,1)} %collective-permute-done.20.refs_4_), channel_id=1, source_target_pairs={{4,6},{3,1},{12,14},{11,9},{20,22},{19,17},{28,30},{27,25}} | collective-permute-start | bytes 1376264 | tf_op jit(solution)/shard_map/ppermute | solution.py:43
  215.2 6.6 %collective-permute-start.22 = (bf16[256,896]{1,0:T(8,128)(2,1)S(1)}, bf16[256,896]{1,0:T(8,128)(2,1)S(1)}, u32[]{:S(2)}, u32[]{:S(2)}) collective-permute-start(bf16[256,896]{1,0:T(8,128)(2,1)S(1)} %collective-permute-done.19.refs_3_), channel_id=1, source_target_pairs={{2,3},{4,5},{6,7},{1,0},{3,2},{5,4},{10,11},{12,13},{14,15},{9,8},... | collective-permute-start | bytes 1376264 | tf_op jit(solution)/shard_map/ppermute | solution.py:46
  216.5 7.4 %collective-permute-start.38 = (bf16[256,896]{1,0:T(8,128)(2,1)}, bf16[256,896]{1,0:T(8,128)(2,1)}, u32[]{:S(2)}, u32[]{:S(2)}) collective-permute-start(bf16[256,896]{1,0:T(8,128)(2,1)} %collective-permute-done.37.refs_4_), channel_id=1, source_target_pairs={{4,6},{3,1},{12,14},{11,9},{20,22},{19,17},{28,30},{27,25}} | collective-permute-start | bytes 1376264 | tf_op jit(solution)/shard_map/ppermute | solution.py:43
  218.0 10.7 %collective-permute-start.23 = (bf16[256,896]{1,0:T(8,128)(2,1)}, bf16[256,896]{1,0:T(8,128)(2,1)}, u32[]{:S(2)}, u32[]{:S(2)}) collective-permute-start(bf16[256,896]{1,0:T(8,128)(2,1)} %collective-permute-done.20.refs_4_), channel_id=1, source_target_pairs={{4,5},{6,7},{1,0},{3,2},{12,13},{14,15},{9,8},{11,10},{20,21},{22,... | collective-permute-start | bytes 1376264 | tf_op jit(solution)/shard_map/ppermute | solution.py:46
  219.3 9.7 %collective-permute-start.24 = (bf16[256,896]{1,0:T(8,128)(2,1)}, bf16[256,896]{1,0:T(8,128)(2,1)}, u32[]{:S(2)}, u32[]{:S(2)}) collective-permute-start(bf16[256,896]{1,0:T(8,128)(2,1)} %collective-permute-done.21.refs_5_), channel_id=1, source_target_pairs={{6,7},{1,0},{14,15},{9,8},{22,23},{17,16},{30,31},{25,24}} | collective-permute-start | bytes 1376264 | tf_op jit(solution)/shard_map/ppermute | solution.py:46
  220.6 13.3 %collective-permute-start.39 = (bf16[256,896]{1,0:T(8,128)(2,1)}, bf16[256,896]{1,0:T(8,128)(2,1)}, u32[]{:S(2)}, u32[]{:S(2)}) collective-permute-start(bf16[256,896]{1,0:T(8,128)(2,1)} %collective-permute-done.36.refs_3_), channel_id=1, source_target_pairs={{2,3},{4,5},{6,7},{1,0},{3,2},{5,4},{10,11},{12,13},{14,15},{9,8},... | collective-permute-start | bytes 1376264 | tf_op jit(solution)/shard_map/ppermute | solution.py:46
  222.7 11.3 %collective-permute-start.40 = (bf16[256,896]{1,0:T(8,128)(2,1)}, bf16[256,896]{1,0:T(8,128)(2,1)}, u32[]{:S(2)}, u32[]{:S(2)}) collective-permute-start(bf16[256,896]{1,0:T(8,128)(2,1)} %collective-permute-done.37.refs_4_), channel_id=1, source_target_pairs={{4,5},{6,7},{1,0},{3,2},{12,13},{14,15},{9,8},{11,10},{20,21},{22,... | collective-permute-start | bytes 1376264 | tf_op jit(solution)/shard_map/ppermute | solution.py:46
  224.0 12.0 %collective-permute-start.41 = (bf16[256,896]{1,0:T(8,128)(2,1)}, bf16[256,896]{1,0:T(8,128)(2,1)}, u32[]{:S(2)}, u32[]{:S(2)}) collective-permute-start(bf16[256,896]{1,0:T(8,128)(2,1)} %collective-permute-done.38.refs_5_), channel_id=1, source_target_pairs={{6,7},{1,0},{14,15},{9,8},{22,23},{17,16},{30,31},{25,24}} | collective-permute-start | bytes 1376264 | tf_op jit(solution)/shard_map/ppermute | solution.py:46
  227.3 1.6 copy-start.5
  230.3 27.5 %collective-permute-start.25 = (bf16[256,896]{1,0:T(8,128)(2,1)S(1)}, bf16[256,896]{1,0:T(8,128)(2,1)S(1)}, u32[]{:S(2)}, u32[]{:S(2)}) collective-permute-start(bf16[256,896]{1,0:T(8,128)(2,1)S(1)} %select_select_fusion), channel_id=1, source_target_pairs={{0,8},{8,16},{16,24},{1,9},{9,17},{17,25},{2,10},{10,18},{18,26},{... | collective-permute-start | bytes 1376264 | tf_op jit(solution)/shard_map/ppermute | solution.py:364
  250.4 23.6 %copy-start.15 = (bf16[4,64,4096]{2,1,0:T(8,128)(2,1)S(1)}, bf16[4,64,4096]{2,1,0:T(8,128)(2,1)}, u32[]{:S(2)}) copy-start(bf16[4,64,4096]{2,1,0:T(8,128)(2,1)} %cross.3) | copy-start | bytes 6291460
  250.4 23.6 %collective-permute-start.42 = (bf16[4,64,4096]{2,1,0:T(8,128)(2,1)}, bf16[4,64,4096]{2,1,0:T(8,128)(2,1)S(1)}, u32[]{:S(2)}, u32[]{:S(2)}) collective-permute-start(bf16[4,64,4096]{2,1,0:T(8,128)(2,1)} %cross.3), channel_id=1, source_target_pairs={{0,1},{1,0},{2,3},{3,2},{4,5},{5,4},{6,7},{7,6},{8,9},{9,8},{10,11... | collective-permute-start | bytes 6291464 | tf_op jit(solution)/shard_map/ppermute | solution.py:35
  274.0 4.8 %collective-permute-start.26 = (bf16[4,64,4096]{2,1,0:T(8,128)(2,1)}, bf16[4,64,4096]{2,1,0:T(8,128)(2,1)S(1)}, u32[]{:S(2)}, u32[]{:S(2)}) collective-permute-start(bf16[4,64,4096]{2,1,0:T(8,128)(2,1)} %cross.2), channel_id=1, source_target_pairs={{0,1},{1,0},{2,3},{3,2},{4,5},{5,4},{6,7},{7,6},{8,9},{9,8},{10,11... | collective-permute-start | bytes 6291464 | tf_op jit(solution)/shard_map/ppermute | solution.py:35
  274.1 22.6 %copy-start.16 = (bf16[4,64,4096]{2,1,0:T(8,128)(2,1)}, bf16[4,64,4096]{2,1,0:T(8,128)(2,1)S(1)}, u32[]{:S(2)}) copy-start(bf16[4,64,4096]{2,1,0:T(8,128)(2,1)S(1)} %collective-permute-done.42) | copy-start | bytes 6291460
  274.2 16.8 %copy-start.14 = (bf16[4,64,4096]{2,1,0:T(8,128)(2,1)S(1)}, bf16[4,64,4096]{2,1,0:T(8,128)(2,1)}, u32[]{:S(2)}) copy-start(bf16[4,64,4096]{2,1,0:T(8,128)(2,1)} %cross.2) | copy-start | bytes 6291460
  274.2 11.2 %collective-permute-start.43 = (bf16[64,4096]{1,0:T(8,128)(2,1)S(1)}, bf16[64,4096]{1,0:T(8,128)(2,1)S(1)}, u32[]{:S(2)}, u32[]{:S(2)}) collective-permute-start(bf16[64,4096]{1,0:T(8,128)(2,1)S(1)} %fusion.13), channel_id=1, source_target_pairs={{0,2},{7,5},{8,10},{15,13},{16,18},{23,21},{24,26},{31,29}} | collective-permute-start | bytes 1572872 | tf_op jit(solution)/shard_map/ppermute | solution.py:61
  278.7 23.5 %copy-start.17 = (bf16[4,64,4096]{2,1,0:T(8,128)(2,1)}, bf16[4,64,4096]{2,1,0:T(8,128)(2,1)S(1)}, u32[]{:S(2)}) copy-start(bf16[4,64,4096]{2,1,0:T(8,128)(2,1)S(1)} %collective-permute-done.26) | copy-start | bytes 6291460
  280.3 10.7 %collective-permute-start.27 = (bf16[64,4096]{1,0:T(8,128)(2,1)S(1)}, bf16[64,4096]{1,0:T(8,128)(2,1)S(1)}, u32[]{:S(2)}, u32[]{:S(2)}) collective-permute-start(bf16[64,4096]{1,0:T(8,128)(2,1)S(1)} %fusion.12), channel_id=1, source_target_pairs={{0,2},{7,5},{8,10},{15,13},{16,18},{23,21},{24,26},{31,29}} | collective-permute-start | bytes 1572872 | tf_op jit(solution)/shard_map/ppermute | solution.py:61
  285.6 11.1 %collective-permute-start.44 = (bf16[64,4096]{1,0:T(8,128)(2,1)S(1)}, bf16[64,4096]{1,0:T(8,128)(2,1)S(1)}, u32[]{:S(2)}, u32[]{:S(2)}) collective-permute-start(bf16[64,4096]{1,0:T(8,128)(2,1)S(1)} %fusion), channel_id=1, source_target_pairs={{0,2},{2,4},{5,3},{7,5},{8,10},{10,12},{13,11},{15,13},{16,18},{18... | collective-permute-start | bytes 1572872 | tf_op jit(solution)/shard_map/ppermute | solution.py:61
  291.2 11.1 %collective-permute-start.28 = (bf16[64,4096]{1,0:T(8,128)(2,1)S(1)}, bf16[64,4096]{1,0:T(8,128)(2,1)S(1)}, u32[]{:S(2)}, u32[]{:S(2)}) collective-permute-start(bf16[64,4096]{1,0:T(8,128)(2,1)S(1)} %fusion.4), channel_id=1, source_target_pairs={{0,2},{2,4},{5,3},{7,5},{8,10},{10,12},{13,11},{15,13},{16,18},{18... | collective-permute-start | bytes 1572872 | tf_op jit(solution)/shard_map/ppermute | solution.py:61
  296.8 11.1 %collective-permute-start.45 = (bf16[64,4096]{1,0:T(8,128)(2,1)S(1)}, bf16[64,4096]{1,0:T(8,128)(2,1)S(1)}, u32[]{:S(2)}, u32[]{:S(2)}) collective-permute-start(bf16[64,4096]{1,0:T(8,128)(2,1)S(1)} %fusion.1), channel_id=1, source_target_pairs={{0,2},{2,4},{4,6},{3,1},{5,3},{7,5},{8,10},{10,12},{12,14},{11,9},... | collective-permute-start | bytes 1572872 | tf_op jit(solution)/shard_map/ppermute | solution.py:61
  302.5 11.1 %collective-permute-start.29 = (bf16[64,4096]{1,0:T(8,128)(2,1)S(1)}, bf16[64,4096]{1,0:T(8,128)(2,1)S(1)}, u32[]{:S(2)}, u32[]{:S(2)}) collective-permute-start(bf16[64,4096]{1,0:T(8,128)(2,1)S(1)} %fusion.5), channel_id=1, source_target_pairs={{0,2},{2,4},{4,6},{3,1},{5,3},{7,5},{8,10},{10,12},{12,14},{11,9},... | collective-permute-start | bytes 1572872 | tf_op jit(solution)/shard_map/ppermute | solution.py:61
  307.9 5.6 %collective-permute-start.46 = (bf16[64,4096]{1,0:T(8,128)(2,1)S(1)}, bf16[64,4096]{1,0:T(8,128)(2,1)S(1)}, u32[]{:S(2)}, u32[]{:S(2)}) collective-permute-start(bf16[64,4096]{1,0:T(8,128)(2,1)S(1)} %collective-permute-done.45), channel_id=1, source_target_pairs={{0,1},{1,0},{2,3},{3,2},{4,5},{5,4},{6,7},{7,6},{8,9},{9,8},{10,11... | collective-permute-start | bytes 1572872 | tf_op jit(solution)/shard_map/ppermute | solution.py:35
  313.5 1.9 collective-permute-start.30
  313.5 5.0 %copy-start.1 = (bf16[16,16,896]{2,1,0:T(8,128)(2,1)S(1)}, bf16[16,16,896]{2,1,0:T(8,128)(2,1)}, u32[]{:S(2)}) copy-start(bf16[16,16,896]{2,1,0:T(8,128)(2,1)} %param.11) | copy-start | bytes 1376260
  (4 other events, 3.7 us)

commit v2 on v0

--- a/solution.py
+++ b/solution.py
@@ -1,12 +1,23 @@
+import functools
+
 import jax
 import jax.numpy as jnp
 from jax import lax
+from jax.experimental import pallas as pl
+from jax.experimental.pallas import tpu as pltpu
 from jax.sharding import PartitionSpec as P
 
 HEAD_DIM = 128
 GROUP = 64
 NLEN = 128
 SEQ_LEN = 2048
+SCALE = 1.0 / HEAD_DIM**0.5
+F32 = jnp.float32
+BF16 = jnp.bfloat16
+HBM = pl.BlockSpec(memory_space=pltpu.HBM)
+ANY = pl.BlockSpec(memory_space=pl.ANY)
+SMEM = pl.BlockSpec(memory_space=pltpu.SMEM)
+VMEM = pl.BlockSpec(memory_space=pltpu.VMEM)
 
 
 def passed_along(block, axis, distance):
@@ -36,7 +47,7 @@
     return (combined * factor * enc_gain).astype(jnp.bfloat16)
 
 
-def local(
+def by_heads(
     tokens,
     nbr_embed,
     neighbour_table,
@@ -138,6 +149,430 @@
     return (cross_out, encoded_mine)
 
 
+def params(mib):
+    return pltpu.CompilerParams(vmem_limit_bytes=mib * 1024 * 1024)
+
+
+def dot(a, b):
+    return jnp.dot(a, b, preferred_element_type=F32)
+
+
+def dot_t(a, b):
+    return lax.dot_general(a, b, (((1,), (1,)), ((), ())), preferred_element_type=F32)
+
+
+def swapped(x, nz):
+    return lax.ppermute(x, "nbr", [(n, n ^ 1) for n in range(2 * nz)])
+
+
+ENDS, MIDDLE = (0, 3), (1, 2)
+
+
+def hop(x, flip, chips=(0, 1, 2, 3)):
+    return lax.ppermute(x, "nbr", [(2 * z + c, 2 * (z ^ flip) + c) for z in chips for c in range(2)])
+
+
+def scattered(part):
+    two = part(2)
+    outer = hop(two, 2, ENDS)
+    three, two = part(3, two)
+    passed, middle = hop(three, 1, ENDS), hop(three, 3, MIDDLE)
+    one, three = part(1, three)
+    one = hop(one, 1)
+    inner = hop((two.astype(F32) + passed.astype(F32)).astype(BF16), 2, MIDDLE)
+    own, one, outer = part(0, one, outer)
+    return [own, one, outer, inner, middle]
+
+
+def fetches(pos, parts, place, sems):
+    inside = (pos[0] == 1) | (pos[0] == 2)
+    when = [None, None, None, inside, jnp.logical_not(inside)]
+    k = 0
+    jobs = []
+    for ref, ok, flip in zip(parts, when, (0, 1, 2, 3, 3)):
+        for src, dst in place(ref, pos[0] ^ flip):
+            jobs.append((ok, pltpu.make_async_copy(src, dst, sems.at[k])))
+            k += 1
+    return jobs
+
+
+def each(jobs, act):
+    for ok, job in jobs:
+        if ok is None:
+            act(job)
+        else:
+            pl.when(ok)(functools.partial(act, job))
+
+
+def begin(jobs):
+    each(jobs, lambda job: job.start())
+
+
+def finish(jobs):
+    each(jobs, lambda job: job.wait())
+
+
+def proj_kernel(pos, own, other, w, mine, theirs, held, sems):
+    pieces, depth, width = held.shape
+    loads = [pltpu.make_async_copy(w.at[p], held.at[p], sems.at[p]) for p in range(pieces)]
+    for load in loads:
+        load.start()
+    rows = jnp.concatenate([own[...].reshape(-1, depth), other[...].reshape(-1, depth)], axis=0)
+    for p in range(pieces):
+        loads[p].wait()
+        got = dot(rows, held[p]).astype(BF16).reshape(2, 4, GROUP, width)
+        for c, out in enumerate((mine, theirs)):
+            for flip in range(4):
+                out[pos[0] ^ flip, :, pl.ds(p * width, width)] = got[c, flip]
+
+
+def project(pos, own, other, w):
+    _, rows, depth = own.shape
+    pieces, _, width = w.shape
+    shape = jax.ShapeDtypeStruct((4, rows, pieces * width), BF16)
+    return pl.pallas_call(
+        proj_kernel,
+        in_specs=[SMEM, VMEM, VMEM, HBM],
+        out_specs=[VMEM, VMEM],
+        out_shape=[shape, shape],
+        scratch_shapes=[pltpu.VMEM(w.shape, BF16), pltpu.SemaphoreType.DMA((pieces,))],
+        compiler_params=params(50),
+        cost_estimate=pl.CostEstimate(
+            flops=16 * rows * depth * width * pieces,
+            bytes_accessed=2 * depth * (width * pieces + 8 * rows),
+            transcendentals=0,
+        ),
+        name="project",
+    )(pos, own, other, w)
+
+
+def enc_kernel(flip, pos, *refs):
+    parts, weights, refs = refs[:5], (refs[5:9], refs[9:13]), refs[13:]
+    out, refs = refs[0], refs[1:]
+    if flip == 0:
+        raw, refs = refs[0], refs[1:]
+    rows, att, sems = refs
+    i = pos[0] ^ flip
+    jobs = fetches(pos, parts, lambda ref, j: [(ref.at[c, i], rows.at[j, c]) for c in range(2)], sems)
+    begin(jobs)
+    finish(jobs)
+    x = rows[...].reshape(out.shape)
+    if flip == 0:
+        raw[...] = x
+    here = pl.ds(pl.multiple_of(i * GROUP, GROUP), GROUP)
+    total = None
+    for wq, keys, values, wo in weights:
+        q = dot(x, wq[...]).astype(BF16)
+        for h in range(0, wq.shape[1], HEAD_DIM):
+            cols = pl.ds(h, HEAD_DIM)
+            scores = dot_t(keys[here, cols], q[:, h : h + HEAD_DIM]) * SCALE
+            raised = jnp.exp(scores - jnp.max(scores, axis=0, keepdims=True))
+            share = (raised / jnp.sum(raised, axis=0, keepdims=True)).astype(BF16)
+            att[:, cols] = lax.dot_general(
+                share, values[here, cols], (((0,), (0,)), ((), ())), preferred_element_type=F32
+            ).astype(BF16)
+        part = dot(att[...], wo[...])
+        total = part if total is None else total + part
+    out[...] = total.astype(BF16)
+
+
+def encode(pos, parts, flip, queries, projected, outs):
+    _, _, part, width = parts[0].shape
+    tokens = projected[0].shape[0]
+    heads = queries[0].shape[1]
+    rows = 8 * part
+    kv = [pl.BlockSpec((tokens, heads), lambda i: (0, 1)), pl.BlockSpec((tokens, heads), lambda i: (0, 2))]
+    shape = jax.ShapeDtypeStruct((rows, width), BF16)
+    args = []
+    for wq, proj, wo in zip(queries, projected, outs):
+        args += [wq, proj, proj, wo]
+    return pl.pallas_call(
+        functools.partial(enc_kernel, flip),
+        grid=(1,),
+        in_specs=[SMEM] + [ANY] * 5 + ([VMEM] + kv + [VMEM]) * 2,
+        out_specs=[VMEM] * (1 if flip else 2),
+        out_shape=[shape] * (1 if flip else 2),
+        scratch_shapes=[
+            pltpu.VMEM((4, 2, part, width), BF16),
+            pltpu.VMEM((rows, heads), BF16),
+            pltpu.SemaphoreType.DMA((10,)),
+        ],
+        compiler_params=params(32),
+        cost_estimate=pl.CostEstimate(
+            flops=2 * rows * heads * (4 * width + 4 * GROUP),
+            bytes_accessed=4 * rows * width + 8 * heads * width,
+            transcendentals=rows * heads,
+        ),
+        name="encode",
+    )(pos, *parts, *args)
+
+
+def norm_kernel(nz, *refs):
+    raw, gain, out = refs[nz:]
+    combined = raw[...].astype(F32) + sum(r[...].astype(F32) for r in refs[:nz])
+    factor = lax.rsqrt(jnp.mean(combined * combined, axis=-1, keepdims=True) + 1e-06)
+    out[...] = (combined * factor * gain[...]).astype(BF16)
+
+
+def normed(parts, raw, gain):
+    return pl.pallas_call(
+        functools.partial(norm_kernel, len(parts)),
+        in_specs=[VMEM] * (len(parts) + 2),
+        out_specs=VMEM,
+        out_shape=jax.ShapeDtypeStruct(raw.shape, BF16),
+        compiler_params=params(8),
+        name="normed",
+    )(*parts, raw, gain)
+
+
+def attention(i, core, counts, x, wkvs, queries, out):
+    keys, heads = x.shape[0], wkvs[0].shape[1] // 2
+    slot = lax.broadcasted_iota(jnp.int32, (GROUP, keys), 1) // (keys // 16) % 2
+    first = lax.broadcasted_iota(jnp.int32, (GROUP, 2 * heads), 0) == 0
+    allowed = slot < counts[i]
+    q = jnp.where(first, queries[i], queries[i + core])
+    for w, wkv in enumerate(wkvs):
+        kv = dot(x, wkv[...]).astype(BF16)
+        for h in range(0, heads, HEAD_DIM):
+            at = heads * w + h
+            scores = dot_t(q[:, at : at + HEAD_DIM], kv[:, h : h + HEAD_DIM]) * SCALE
+            scores = jnp.where(allowed, scores, -1e30)
+            raised = jnp.where(allowed, jnp.exp(scores - jnp.max(scores, axis=-1, keepdims=True)), 0.0)
+            share = (raised / jnp.sum(raised, axis=-1, keepdims=True)).astype(BF16)
+            out[:, pl.ds(at, HEAD_DIM)] = dot(share, kv[:, heads + h : heads + h + HEAD_DIM]).astype(BF16)
+
+
+def attend_kernel(flips, pos, counts, *refs):
+    n = len(flips)
+    rows, (own_kv, other_kv, queries), refs = refs[:n], refs[n : n + 3], refs[n + 3 :]
+    outs = refs[-n:] if n == 1 else refs[1 : n + 1]
+    for flip, x, out in zip(flips, rows, outs):
+        attention(pos[0] ^ flip, pos[1], counts, x[...], (own_kv, other_kv), queries, out)
+    if n > 1:
+        z = pos[0]
+        refs[-1][...] = jnp.where(z == 3, refs[0][...], jnp.where(z == 2, outs[0][...], outs[1][...]))
+
+
+def attend(pos, counts, flips, rows, wkvs, queries, *earlier):
+    keys, width = rows[0].shape
+    both = wkvs[0].shape[1]
+    n = len(flips)
+    return pl.pallas_call(
+        functools.partial(attend_kernel, flips),
+        in_specs=[SMEM, SMEM] + [VMEM] * (n + 3 + len(earlier)),
+        out_specs=[VMEM] * (n + len(earlier)),
+        out_shape=[jax.ShapeDtypeStruct((GROUP, both), BF16)] * (n + len(earlier)),
+        compiler_params=params(40),
+        cost_estimate=pl.CostEstimate(
+            flops=4 * n * keys * both * (width + GROUP),
+            bytes_accessed=2 * (2 * width * both + n * keys * width),
+            transcendentals=n * GROUP * keys * both // HEAD_DIM,
+        ),
+        name="attend",
+    )(pos, counts, *rows, *wkvs, queries, *earlier)
+
+
+def loads_of(wos, loaded, sems):
+    heads, model = wos[0].shape
+    pieces = sems.shape[1]
+    piece = model // pieces
+    return [
+        [
+            pltpu.make_async_copy(
+                wos[w].at[:, pl.ds(p * piece, piece)], loaded.at[p, pl.ds(w * heads, heads)], sems.at[w, p]
+            )
+            for w in range(2)
+        ]
+        for p in range(pieces)
+    ]
+
+
+def last_kernel(pos, counts, middle, far, own_kv, other_kv, queries, *refs):
+    atts, before, wos, outs, (got, held, loaded, sems) = refs[:3], refs[3], refs[4:6], refs[6:10], refs[10:]
+    loads = loads_of(wos, loaded, sems)
+    for load in sum(loads, []):
+        load.start()
+    z, core = pos[0], pos[1]
+    x = jnp.where((z == 1) | (z == 2), middle[...], far[...])
+    attention(z ^ 3, core, counts, x, (own_kv, other_kv), queries, got)
+    held[0] = before[...]
+    for flip, att in enumerate((*atts, got)):
+        held[(z ^ flip) + 1] = att[...]
+    first = lax.broadcasted_iota(jnp.int32, got.shape, 0) == 0
+    rows = []
+    for flip in range(4):
+        i = (z ^ flip) + 1
+        rows.append(jnp.where(first, held[i], held[i - core]))
+    rows = jnp.concatenate(rows, axis=0)
+    piece = loaded.shape[2]
+    for p, pair in enumerate(loads):
+        for load in pair:
+            load.wait()
+        result = dot(rows, loaded[p]).astype(BF16)
+        for flip in range(4):
+            outs[flip][:, pl.ds(p * piece, piece)] = result[flip * GROUP : (flip + 1) * GROUP]
+
+
+def last_attend(pos, counts, middle, far, wkvs, queries, atts, before, wos):
+    keys, width = middle.shape
+    heads, model = wos[0].shape
+    pieces = 4
+    return pl.pallas_call(
+        last_kernel,
+        in_specs=[SMEM, SMEM] + [VMEM] * 9 + [HBM, ANY],
+        out_specs=[VMEM] * 5,
+        out_shape=[jax.ShapeDtypeStruct((GROUP, model), BF16)] * 4 + [jax.ShapeDtypeStruct(before.shape, BF16)],
+        scratch_shapes=[
+            pltpu.VMEM((5,) + before.shape, BF16),
+            pltpu.VMEM((pieces, 2 * heads, model // pieces), BF16),
+            pltpu.SemaphoreType.DMA((2, pieces)),
+        ],
+        compiler_params=params(48),
+        cost_estimate=pl.CostEstimate(
+            flops=16 * GROUP * heads * model + 8 * keys * heads * (width + GROUP),
+            bytes_accessed=4 * heads * model + 8 * GROUP * model,
+            transcendentals=2 * GROUP * keys * heads // HEAD_DIM,
+        ),
+        name="last_attend",
+    )(pos, counts, middle, far, *wkvs, queries, *atts, before, *wos)
+
+
+def late_kernel(before, own_w, other_w, out, loaded, sems):
+    loads = loads_of((own_w, other_w), loaded, sems)
+    for load in sum(loads, []):
+        load.start()
+    first = lax.broadcasted_iota(jnp.int32, before.shape, 0) == 0
+    rows = jnp.where(first, 0.0, before[...].astype(F32)).astype(BF16)
+    piece = loaded.shape[2]
+    for p, pair in enumerate(loads):
+        for load in pair:
+            load.wait()
+        out[:, pl.ds(p * piece, piece)] = dot(rows, loaded[p]).astype(BF16)
+
+
+def late_out(before, wos):
+    heads, model = wos[0].shape
+    pieces = 4
+    return pl.pallas_call(
+        late_kernel,
+        in_specs=[VMEM, HBM, ANY],
+        out_specs=VMEM,
+        out_shape=jax.ShapeDtypeStruct((GROUP, model), BF16),
+        scratch_shapes=[
+            pltpu.VMEM((pieces, 2 * heads, model // pieces), BF16),
+            pltpu.SemaphoreType.DMA((2, pieces)),
+        ],
+        compiler_params=params(48),
+        cost_estimate=pl.CostEstimate(
+            flops=4 * GROUP * heads * model, bytes_accessed=4 * heads * model, transcendentals=0
+        ),
+        name="late_out",
+    )(before, *wos)
+
+
+def by_groups(
+    tokens,
+    nbr_embed,
+    neighbour_table,
+    valid_counts,
+    dec_proj,
+    enc_query,
+    enc_out,
+    enc_gain,
+    nbr_proj,
+    out_proj,
+):
+    nz = lax.axis_size("nbr") // 2
+    n_seq = lax.axis_size("seq")
+    seq_index = lax.axis_index("seq")
+    member = lax.axis_index("nbr")
+    z, core = member // 2, member % 2
+    pos = jnp.stack([z, core]).astype(jnp.int32)
+    width = dec_proj.shape[2]
+    ch_grp, slots = neighbour_table.shape
+    nb_grp, share, enc_width = nbr_embed.shape
+
+    ids = neighbour_table.reshape(nz, 2, slots) - seq_index * nb_grp
+
+    def picked(c):
+        mine = lax.dynamic_index_in_dim(ids, c, 1, False).reshape(-1)
+        return jnp.take(nbr_embed, mine, axis=0, mode="clip").reshape(nz, slots * share, enc_width)
+
+    held = lax.optimization_barrier
+
+    two, one = hop(tokens, 2), hop(tokens, 1)
+    nbr_own = jnp.stack([picked(core), swapped(picked(1 - core), nz)])
+    two, one, own, nbr_own, enc_query, enc_out, nbr_proj, out_proj = held(
+        (two, one, tokens, nbr_own, enc_query, enc_out, nbr_proj, out_proj)
+    )
+    far, middle = hop(two, 1, MIDDLE), hop(own, 3, MIDDLE)
+    nbr_two, nbr_one = hop(nbr_own, 2), hop(nbr_own, 1)
+    encqs = (enc_query, swapped(enc_query, nz))
+    column = jnp.stack([own, one, two, jnp.where((z == 1) | (z == 2), middle, far)])
+    wkv = nbr_proj.reshape(enc_width, 2 * width)
+    encos, wkvs, outps = [(w, swapped(w, nz)) for w in (enc_out, wkv, out_proj)]
+    column, encos, wkvs, outps = held((column, encos, wkvs, outps))
+    mine, theirs = project(pos, column, swapped(column, nz), dec_proj.transpose(1, 0, 2))
+    mine, theirs, nbr_two, nbr_one, nbr_own, encqs, enc_out, nbr_proj, out_proj = held(
+        (mine, theirs, nbr_two, nbr_one, nbr_own, encqs, enc_out, nbr_proj, out_proj)
+    )
+    nbrs = (nbr_own, nbr_one, nbr_two, hop(nbr_own, 3, MIDDLE), hop(nbr_two, 1, MIDDLE))
+    projected = [p.reshape(nz * GROUP, 3 * width) for p in (mine, swapped(theirs, nz))]
+
+    last = jnp.concatenate([p[:, :width].reshape(nz, GROUP, width)[:, GROUP - 1 :] for p in projected], axis=2)
+    others = jnp.concatenate([theirs[:, :, :width], swapped(mine[:, :, :width], nz)], axis=2)
+    queries = jnp.concatenate([last, others[:, : GROUP - 1]], axis=1)
+    odd = range(1, 2 * nz, 2)
+    back = [((q + 1) * 2 * nz + n, q * 2 * nz + n) for q in range(n_seq - 1) for n in odd]
+    queries = jnp.concatenate([queries, lax.ppermute(queries[:1], ("seq", "nbr"), back)])
+    counts = lax.dynamic_index_in_dim(
+        lax.dynamic_slice_in_dim(valid_counts, seq_index * ch_grp, ch_grp, 0).reshape(nz, 2), core, 1, False
+    )
+
+    nbrs, queries, encos, wkvs, outps = held((nbrs, queries, encos, wkvs, outps))
+    raws = []
+
+    def part(flip, *after):
+        after, here = held((after, pos))
+        got = encode(here, nbrs, flip, encqs, projected, encos)
+        raws.extend(got[1:])
+        return [got[0], *after] if after else got[0]
+
+    arrived = scattered(part)
+    enc_own = normed(arrived, raws[0], enc_gain.reshape(1, -1))
+    enc_two, enc_one = hop(enc_own, 2), hop(enc_own, 1)
+    atts = list(attend(pos, counts, (0,), (enc_own,), wkvs, queries))
+    enc_two, enc_mine, atts[0] = lax.optimization_barrier((enc_two, enc_own, atts[0]))
+    enc_middle, enc_far = hop(enc_mine, 3, MIDDLE), hop(enc_two, 1, MIDDLE)
+    *more, before = attend(pos, counts, (1, 2), (enc_one, enc_two), wkvs, queries, atts[0])
+    atts += more
+
+    def onward(x, chips):
+        route = [(q * 2 * nz + 2 * i + 1, (q + 1) * 2 * nz + 2 * i + 1) for q in range(n_seq - 1) for i in chips]
+        got = lax.ppermute(x, ("seq", "nbr"), route)
+        return jnp.where((seq_index * ch_grp * GROUP) % SEQ_LEN == 0, 0, got).astype(BF16)
+
+    before = onward(before, (1, 2, 3))
+    *outs, last = last_attend(pos, counts, enc_middle, enc_far, wkvs, queries, atts, before, outps)
+    arrived = scattered(lambda flip, *after: [outs[flip], *after] if after else outs[flip])
+    arrived.append(late_out(onward(last, (0,)), outps))
+    mine = sum(part.astype(F32) for part in arrived).astype(BF16)
+    theirs = swapped(mine, nz)
+    cross_out = jnp.concatenate([theirs[1:], mine[:1]], axis=0)
+
+    encoded = enc_own.reshape(nz, 2, slots, share, enc_width)
+    encoded = jnp.where(core == 0, encoded, encoded[:, ::-1]).transpose(2, 0, 1, 3, 4).reshape(-1, enc_width)
+    return (cross_out, encoded)
+
+
+def local(*args):
+    tokens, table = args[0], args[2]
+    chips = lax.axis_size("nbr") // 2
+    if chips == 4 and table.shape[0] == 8 and tokens.shape[0] == GROUP:
+        return by_groups(*args)
+    return by_heads(*args)
+
+
 def solution(mesh):
     return jax.shard_map(
         local,

time: 386 us -> 227 us (0.59)
  waiting for transfers between devices: 267 us -> 108 us
  Pallas kernels: 0 us -> 50.8 us
  starting transfers between devices: 3.56 us -> 49.3 us
  local copies, waits for them, and re-layouts: 52 us -> 9.64 us
  matrix products: 35 us -> 0 us
  between operations: 14.1 us -> 1.16 us
  other arithmetic: 13.9 us -> 7.14 us
    psum x1 -> x0, waiting for transfers between devices: 151 us -> none  [local(): lax.psum(jnp.dot(enc_att, enc_out, preferred_element_type=jnp.float32), '...]
    ppermute x1 -> x34, waiting for transfers between devices: 1.95 us -> 108 us  [the longest x22 107 us: hop(): lax.ppermute(x, 'nbr', [(2 * z + c, 2 * (z ^ flip) + c) for z in chips fo...]
    all_gather x2 -> x0, waiting for transfers between devices: 62.5 us -> none  [the longest x1 34.1 us: local(): lax.all_gather(tokens, 'nbr', axis=0, tiled=True)]
    pallas_call x0 -> x10, Pallas kernels: none -> 50.8 us  [the longest x4 14.1 us: encode(): pl.pallas_call(functools.partial(enc_kernel, flip), grid=(1,), in_specs=[...]
    reduce_scatter x1 -> x0, waiting for transfers between devices: 49.6 us -> none  [local(): lax.psum_scatter(jnp.dot(cca_att, out_proj, preferred_element_type=jnp.fl...]
    ppermute x1 -> x34, starting transfers between devices: 3.41 us -> 49.3 us  [the longest x22 38.4 us: hop(): lax.ppermute(x, 'nbr', [(2 * z + c, 2 * (z ^ flip) + c) for z in chips fo...]
    dot_general x9 -> x0, matrix products: 35 us -> none  [the longest x1 11.1 us: local(): jnp.dot(lax.all_gather(tokens, 'nbr', axis=0, tiled=True), dec_flat, pref...]
    unnamed x35 -> x29, local copies, waits for them, and re-layouts: 26.1 us -> 6.52 us
  transfers between devices with their start and end apart: 5 -> 34, of which waited for: 5 -> 16; matrix products, arithmetic and copies ran while one was open for 11% -> 5% of each run, Pallas kernels for 0% -> 16%
where the time goes in v2:
time: 227 us; the launch traced here: 226 us
  waiting for transfers between devices  108 us (48%)
  Pallas kernels  50.8 us (22%)
  starting transfers between devices  49.3 us (22%)
  local copies, waits for them, and re-layouts  9.64 us (4%)
  other arithmetic  7.14 us (3%)
    ppermute x22, waiting for transfers between devices, hop(): lax.ppermute(x, 'nbr', [(2 * z + c, 2 * (z ^ flip) + c) for z in chips fo...  107 us
    ppermute x22, starting transfers between devices, hop(): lax.ppermute(x, 'nbr', [(2 * z + c, 2 * (z ^ flip) + c) for z in chips fo...  38.4 us
    pallas_call x4, Pallas kernels, encode(): pl.pallas_call(functools.partial(enc_kernel, flip), grid=(1,), in_specs=[...  14.1 us
    pallas_call x2, Pallas kernels, attend(): pl.pallas_call(functools.partial(attend_kernel, flips), in_specs=[SMEM, S...  13.7 us
    pallas_call x1, Pallas kernels, project(): pl.pallas_call(proj_kernel, in_specs=[SMEM, VMEM, VMEM, HBM], out_specs=[...  10.8 us
    pallas_call x1, Pallas kernels, last_attend(): pl.pallas_call(last_kernel, in_specs=[SMEM, SMEM] + [VMEM] * 9 + [HBM, AN...  8.27 us
    ppermute x9, starting transfers between devices, swapped(): return lax.ppermute(x, 'nbr', [(n, n ^ 1) for n in range(2 * nz)])  8.2 us
    unnamed x29, local copies, waits for them, and re-layouts  6.52 us
  transfers between devices with their start and end apart: 34, of which 16 were waited for; matrix products, arithmetic and copies ran while one was open for 5% of the time, Pallas kernels for 16%

profile of v2, /device:TPU:0, one launch (start us, length us, event | category | flops | bytes accessed | tf_op | source)
XLA Modules:
  0.0 226.1 jit_solution(11639580875364551629)
XLA Ops:
  0.6 4.1 %collective-permute-start = (bf16[64,4096]{1,0:T(8,128)(2,1)}, bf16[64,4096]{1,0:T(8,128)(2,1)}, u32[]{:S(2)}, u32[]{:S(2)}) collective-permute-start(bf16[64,4096]{1,0:T(8,128)(2,1)} %param.10), channel_id=1, source_target_pairs={{0,4},{1,5},{2,6},{3,7},{4,0},{5,1},{6,2},{7,3},{8,12},{9,13},{10,... | collective-permute-start | bytes 1572872 | tf_op jit(solution)/shard_map/ppermute | solution.py:172
  4.7 1.6 collective-permute-start.1
  6.3 0.7 broadcast_subtract_fusion
  7.4 0.6 gather_fusion.1
  8.3 0.6 gather_fusion
  8.8 0.7 collective-permute-done.2
  9.5 0.8 pad_maximum_fusion.4.refs_0_
  10.3 18.0 %collective-permute-done = bf16[64,4096]{1,0:T(8,128)(2,1)} collective-permute-done((bf16[64,4096]{1,0:T(8,128)(2,1)}, bf16[64,4096]{1,0:T(8,128)(2,1)}, u32[]{:S(2)}, u32[]{:S(2)}) %collective-permute-start) | collective-permute-done | bytes 524320 | tf_op jit(solution)/shard_map/ppermute | solution.py:172
  28.4 1.5 collective-permute-start.3
  29.9 1.3 collective-permute-start.4
  31.2 2.0 copy.18
  33.2 0.6 collective-permute-start.6
  33.9 12.6 %collective-permute-done.4 = bf16[64,4096]{1,0:T(8,128)(2,1)} collective-permute-done((bf16[64,4096]{1,0:T(8,128)(2,1)}, bf16[64,4096]{1,0:T(8,128)(2,1)}, u32[]{:S(2)}, u32[]{:S(2)}) %collective-permute-start.4) | collective-permute-done | bytes 524320 | tf_op jit(solution)/shard_map/ppermute | solution.py:172
  46.4 1.1 select_bitcast_fusion
  47.6 1.7 pad_maximum_fusion.own
  50.0 3.9 %collective-permute-start.9 = (bf16[2,4,32,896]{3,2,1,0:T(8,128)(2,1)S(1)}, bf16[2,4,32,896]{3,2,1,0:T(8,128)(2,1)S(1)}, u32[]{:S(2)}, u32[]{:S(2)}) collective-permute-start(bf16[2,4,32,896]{3,2,1,0:T(8,128)(2,1)S(1)} %copy-done.4), channel_id=1, source_target_pairs={{0,4},{1,5},{2,6},{3,7},{4,0},{5,1},{6,2},{7,3},{8,12},{9,13},{10,... | collective-permute-start | bytes 1376264 | tf_op jit(solution)/shard_map/ppermute | solution.py:172
  53.9 1.4 copy-done.12
  55.3 10.8 %project.1 = (bf16[4,64,1536]{2,1,0:T(8,128)(2,1)S(1)}, bf16[4,64,1536]{2,1,0:T(8,128)(2,1)S(1)}) custom-call(s32[2]{0:T(128)S(1)} %pad_add_fusion.pos, bf16[4,64,4096]{2,1,0:T(8,128)(2,1)S(1)} %pad_maximum_fusion.own, bf16[4,64,4096]{2,1,0:T(8,128)(2,1)} %copy-done.12, bf16[3,4096,512]{2,1,0:T(8,128)(2,1)} %bitcast.59), custom_call_target="tpu_custom_call" | custom-call | flops 6442450944 | bytes 16777216 | tf_op jit(solution)/shard_map/project/pallas_call | solution.py:233
  66.1 6.0 %collective-permute-done.10.refs_1_ = bf16[2,4,32,896]{3,2,1,0:T(8,128)(2,1)S(1)} collective-permute-done((bf16[2,4,32,896]{3,2,1,0:T(8,128)(2,1)S(1)}, bf16[2,4,32,896]{3,2,1,0:T(8,128)(2,1)S(1)}, u32[]{:S(2)}, u32[]{:S(2)}) %collective-permute-start.10) | collective-permute-done | bytes 458784 | tf_op jit(solution)/shard_map/ppermute | solution.py:172
  72.1 2.2 collective-permute-done.9.refs_2_
  74.9 0.7 collective-permute-start.12
  75.6 1.3 collective-permute-start.13
  77.1 0.7 collective-permute-start.16
  77.8 1.0 pad_maximum_fusion.1.refs_3_.refs_4_.queries
  78.8 11.2 %collective-permute-done.13.refs_4_ = bf16[2,4,32,896]{3,2,1,0:T(8,128)(2,1)S(1)} collective-permute-done((bf16[2,4,32,896]{3,2,1,0:T(8,128)(2,1)S(1)}, bf16[2,4,32,896]{3,2,1,0:T(8,128)(2,1)S(1)}, u32[]{:S(2)}, u32[]{:S(2)}) %collective-permute-start.13) | collective-permute-done | bytes 458784 | tf_op jit(solution)/shard_map/ppermute | solution.py:172
  90.0 3.5 %encode.4 = bf16[256,896]{1,0:T(8,128)(2,1)S(1)} custom-call(s32[2]{0:T(128)S(1)} %pad_add_fusion.pos, bf16[2,4,32,896]{3,2,1,0:T(8,128)(2,1)S(1)} %copy-done.4, bf16[2,4,32,896]{3,2,1,0:T(8,128)(2,1)S(1)} %collective-permute-done.10.refs_1_, bf16[2,4,32,896]{3,2,1,0:T(8,128)(2,1)S(1)} %collective-permute-done.9.refs_2_, ...), custom_call_target="tpu_custom_call" | custom-call | flops 1006632960 | bytes 4587520 | tf_op jit(solution)/shard_map/encode/pallas_call | solution.py:289
  93.4 3.5 %encode.5 = bf16[256,896]{1,0:T(8,128)(2,1)S(1)} custom-call(s32[2]{0:T(128)S(1)} %pad_add_fusion.pos, bf16[2,4,32,896]{3,2,1,0:T(8,128)(2,1)S(1)} %copy-done.4, bf16[2,4,32,896]{3,2,1,0:T(8,128)(2,1)S(1)} %collective-permute-done.10.refs_1_, bf16[2,4,32,896]{3,2,1,0:T(8,128)(2,1)S(1)} %collective-permute-done.9.refs_2_, ...), custom_call_target="tpu_custom_call" | custom-call | flops 1006632960 | bytes 4587520 | tf_op jit(solution)/shard_map/encode/pallas_call | solution.py:289
  96.9 1.6 collective-permute-start.19
  98.5 2.2 collective-permute-start.18
  100.7 0.7 collective-permute-start.21
  101.4 3.6 %encode.6 = bf16[256,896]{1,0:T(8,128)(2,1)S(1)} custom-call(s32[2]{0:T(128)S(1)} %pad_add_fusion.pos, bf16[2,4,32,896]{3,2,1,0:T(8,128)(2,1)S(1)} %copy-done.4, bf16[2,4,32,896]{3,2,1,0:T(8,128)(2,1)S(1)} %collective-permute-done.10.refs_1_, bf16[2,4,32,896]{3,2,1,0:T(8,128)(2,1)S(1)} %collective-permute-done.9.refs_2_, ...), custom_call_target="tpu_custom_call" | custom-call | flops 1006632960 | bytes 4587520 | tf_op jit(solution)/shard_map/encode/pallas_call | solution.py:289
  105.0 1.2 collective-permute-start.17
  106.3 3.2 %collective-permute-done.19 = bf16[256,896]{1,0:T(8,128)(2,1)S(1)} collective-permute-done((bf16[256,896]{1,0:T(8,128)(2,1)S(1)}, bf16[256,896]{1,0:T(8,128)(2,1)S(1)}, u32[]{:S(2)}, u32[]{:S(2)}) %collective-permute-start.19) | collective-permute-done | bytes 458784 | tf_op jit(solution)/shard_map/ppermute | solution.py:172
  109.6 1.3 collective-permute-start.20
  110.9 16.4 %collective-permute-done.17.refs_1_ = bf16[256,896]{1,0:T(8,128)(2,1)S(1)} collective-permute-done((bf16[256,896]{1,0:T(8,128)(2,1)S(1)}, bf16[256,896]{1,0:T(8,128)(2,1)S(1)}, u32[]{:S(2)}, u32[]{:S(2)}) %collective-permute-start.17) | collective-permute-done | bytes 458784 | tf_op jit(solution)/shard_map/ppermute | solution.py:172
  127.3 3.5 %encode.7 = (bf16[256,896]{1,0:T(8,128)(2,1)S(1)}, bf16[256,896]{1,0:T(8,128)(2,1)S(1)}) custom-call(s32[2]{0:T(128)S(1)} %pad_add_fusion.pos, bf16[2,4,32,896]{3,2,1,0:T(8,128)(2,1)S(1)} %copy-done.4, bf16[2,4,32,896]{3,2,1,0:T(8,128)(2,1)S(1)} %collective-permute-done.10.refs_1_, bf16[2,4,32,896]{3,2,1,0:T(8,128)(2,1)S(1)} %collective-permute-done.9.refs_2_, ...), custom_call_target="tpu_custom_call" | custom-call | flops 1006632960 | bytes 4587520 | tf_op jit(solution)/shard_map/encode/pallas_call | solution.py:289
  130.8 0.9 collective-permute-done.20.refs_3_
  132.3 2.6 %collective-permute-start.22 = (bf16[256,896]{1,0:T(8,128)(2,1)S(1)}, bf16[256,896]{1,0:T(8,128)(2,1)}, u32[]{:S(2)}, u32[]{:S(2)}) collective-permute-start(bf16[256,896]{1,0:T(8,128)(2,1)S(1)} %normed.1.refs_0_), channel_id=1, source_target_pairs={{0,4},{1,5},{2,6},{3,7},{4,0},{5,1},{6,2},{7,3},{8,12},{9,13},{10,... | collective-permute-start | bytes 1376264 | tf_op jit(solution)/shard_map/ppermute | solution.py:172
  135.6 4.8 %attend.2.refs_5_.refs_0_ = bf16[64,1024]{1,0:T(8,128)(2,1)S(1)} custom-call(s32[2]{0:T(128)S(1)} %pad_add_fusion.pos, s32[4]{0:T(128)S(1)} %dynamic-slice_reduce_fusion.counts, bf16[256,896]{1,0:T(8,128)(2,1)S(1)} %normed.1.refs_0_, bf16[896,1024]{1,0:T(8,128)(2,1)S(1)} %bitcast.46, bf16[896,1024]{1,0:T(8,128)(2,1)} %collective-permute-done.6.refs_2_.refs_3_.other_kv, ...), custom_call_target="tpu_custom_call" | custom-call | flops 1006632960 | bytes 4128768 | tf_op jit(solution)/shard_map/attend/pallas_call | solution.py:360
  140.4 13.6 %collective-permute-done.22.refs_1_ = bf16[256,896]{1,0:T(8,128)(2,1)} collective-permute-done((bf16[256,896]{1,0:T(8,128)(2,1)S(1)}, bf16[256,896]{1,0:T(8,128)(2,1)}, u32[]{:S(2)}, u32[]{:S(2)}) %collective-permute-start.22) | collective-permute-done | bytes 458784 | tf_op jit(solution)/shard_map/ppermute | solution.py:172
  154.0 1.4 collective-permute-start.23
  155.4 1.3 collective-permute-start.24
  156.7 8.9 %attend.3 = (bf16[64,1024]{1,0:T(8,128)(2,1)S(1)}, bf16[64,1024]{1,0:T(8,128)(2,1)S(1)}, bf16[64,1024]{1,0:T(8,128)(2,1)}) custom-call(s32[2]{0:T(128)S(1)} %pad_add_fusion.pos, s32[4]{0:T(128)S(1)} %dynamic-slice_reduce_fusion.counts, bf16[256,896]{1,0:T(8,128)(2,1)} %collective-permute-done.25.refs_0_, bf16[256,896]{1,0:T(8,128)(2,1)} %collective-permute-done.22.refs_1_, ...), custom_call_target="tpu_custom_call" | custom-call | flops 2013265920 | bytes 4587520 | tf_op jit(solution)/shard_map/attend/pallas_call | solution.py:360
  165.7 0.7 copy-done.6
  166.3 0.7 copy-done.8
  167.0 1.3 collective-permute-start.26
  168.3 0.6 collective-permute-done.24.far
  169.0 0.9 copy-done.7
  169.9 0.9 copy-done.9
  170.8 8.3 %last_attend.1 = (bf16[64,4096]{1,0:T(8,128)(2,1)S(1)}, bf16[64,4096]{1,0:T(8,128)(2,1)S(1)}, bf16[64,4096]{1,0:T(8,128)(2,1)S(1)}, bf16[64,4096]{1,0:T(8,128)(2,1)S(1)}, bf16[64,1024]{1,0:T(8,128)(2,1)S(1)}) custom-call(s32[2]{0:T(128)S(1)} %pad_add_fusion.pos, s32[4]{0:T(128)S(1)} %dynamic-slice_reduce_fusion.counts, ...), custom_call_target="tpu_custom_call" | custom-call | flops 3154116608 | bytes 10485760 | tf_op jit(solution)/shard_map/last_attend/pallas_call | solution.py:420
  179.0 4.8 %collective-permute-start.29 = (bf16[64,4096]{1,0:T(8,128)(2,1)S(1)}, bf16[64,4096]{1,0:T(8,128)(2,1)S(1)}, u32[]{:S(2)}, u32[]{:S(2)}) collective-permute-start(bf16[64,4096]{1,0:T(8,128)(2,1)S(1)} %get-tuple-element.110), channel_id=1, source_target_pairs={{0,2},{1,3},{6,4},{7,5},{8,10},{9,11},{14,12},{15,13},{16,18},{17,... | collective-permute-start | bytes 1572872 | tf_op jit(solution)/shard_map/ppermute | solution.py:172
  183.8 0.7 collective-permute-start.31
  184.5 1.9 collective-permute-start.27
  186.4 2.8 %collective-permute-start.28 = (bf16[64,4096]{1,0:T(8,128)(2,1)S(1)}, bf16[64,4096]{1,0:T(8,128)(2,1)S(1)}, u32[]{:S(2)}, u32[]{:S(2)}) collective-permute-start(bf16[64,4096]{1,0:T(8,128)(2,1)S(1)} %get-tuple-element.109), channel_id=1, source_target_pairs={{0,4},{1,5},{6,2},{7,3},{8,12},{9,13},{14,10},{15,11},{16,20},{17,... | collective-permute-start | bytes 1572872 | tf_op jit(solution)/shard_map/ppermute | solution.py:172
  189.3 5.1 %collective-permute-done.29 = bf16[64,4096]{1,0:T(8,128)(2,1)S(1)} collective-permute-done((bf16[64,4096]{1,0:T(8,128)(2,1)S(1)}, bf16[64,4096]{1,0:T(8,128)(2,1)S(1)}, u32[]{:S(2)}, u32[]{:S(2)}) %collective-permute-start.29) | collective-permute-done | bytes 524320 | tf_op jit(solution)/shard_map/ppermute | solution.py:172
  194.5 1.3 collective-permute-start.30
  195.8 0.7 collective-permute-start.32
  196.5 3.4 %late_out.1 = bf16[64,4096]{1,0:T(8,128)(2,1)S(1)} custom-call(bf16[64,1024]{1,0:T(8,128)(2,1)S(1)} %broadcast_select_fusion.before, bf16[512,4096]{1,0:T(8,128)(2,1)S(1)} %copy-done.1, bf16[512,4096]{1,0:T(8,128)(2,1)} %collective-permute-done.7.refs_5_.other_w), custom_call_target="tpu_custom_call" | custom-call | flops 536870912 | bytes 8388608 | tf_op jit(solution)/shard_map/late_out/pallas_call | solution.py:456
  199.9 5.7 %collective-permute-done.27 = bf16[64,4096]{1,0:T(8,128)(2,1)S(1)} collective-permute-done((bf16[64,4096]{1,0:T(8,128)(2,1)S(1)}, bf16[64,4096]{1,0:T(8,128)(2,1)S(1)}, u32[]{:S(2)}, u32[]{:S(2)}) %collective-permute-start.27) | collective-permute-done | bytes 524320 | tf_op jit(solution)/shard_map/ppermute | solution.py:172
  205.6 11.3 %collective-permute-done.28 = bf16[64,4096]{1,0:T(8,128)(2,1)S(1)} collective-permute-done((bf16[64,4096]{1,0:T(8,128)(2,1)S(1)}, bf16[64,4096]{1,0:T(8,128)(2,1)S(1)}, u32[]{:S(2)}, u32[]{:S(2)}) %collective-permute-start.28) | collective-permute-done | bytes 524320 | tf_op jit(solution)/shard_map/ppermute | solution.py:172
  217.3 6.3 %collective-permute-start.33 = (bf16[64,4096]{1,0:T(8,128)(2,1)S(1)}, bf16[64,4096]{1,0:T(8,128)(2,1)S(1)}, u32[]{:S(2)}, u32[]{:S(2)}) collective-permute-start(bf16[64,4096]{1,0:T(8,128)(2,1)S(1)} %add_convert_fusion), channel_id=1, source_target_pairs={{0,1},{1,0},{2,3},{3,2},{4,5},{5,4},{6,7},{7,6},{8,9},{9,8},{10,11... | collective-permute-start | bytes 1572872 | tf_op jit(solution)/shard_map/ppermute | solution.py:165
  223.7 0.8 copy.17
  224.5 0.6 collective-permute-done.33
  225.3 0.8 pad_maximum_fusion.3
  (81 shorter events, 4.5 us)
Async XLA Ops:
  0.6 6.7 %copy-start = (bf16[16,16,896]{2,1,0:T(8,128)(2,1)S(1)}, bf16[16,16,896]{2,1,0:T(8,128)(2,1)}, u32[]{:S(2)}) copy-start(bf16[16,16,896]{2,1,0:T(8,128)(2,1)} %param.11) | copy-start | bytes 1376260
  0.6 27.7 %collective-permute-start = (bf16[64,4096]{1,0:T(8,128)(2,1)}, bf16[64,4096]{1,0:T(8,128)(2,1)}, u32[]{:S(2)}, u32[]{:S(2)}) collective-permute-start(bf16[64,4096]{1,0:T(8,128)(2,1)} %param.10), channel_id=1, source_target_pairs={{0,4},{1,5},{2,6},{3,7},{4,0},{5,1},{6,2},{7,3},{8,12},{9,13},{10,... | collective-permute-start | bytes 1572872 | tf_op jit(solution)/shard_map/ppermute | solution.py:172
  4.7 23.7 %collective-permute-start.1 = (bf16[64,4096]{1,0:T(8,128)(2,1)}, bf16[64,4096]{1,0:T(8,128)(2,1)S(1)}, u32[]{:S(2)}, u32[]{:S(2)}) collective-permute-start(bf16[64,4096]{1,0:T(8,128)(2,1)} %param.10), channel_id=1, source_target_pairs={{0,2},{1,3},{2,0},{3,1},{4,6},{5,7},{6,4},{7,5},{8,10},{9,11},{10,... | collective-permute-start | bytes 1572872 | tf_op jit(solution)/shard_map/ppermute | solution.py:172
  8.0 1.6 collective-permute-start.2
  9.5 24.2 %copy-start.3 = (bf16[512,896]{1,0:T(8,128)(2,1)S(1)}, bf16[512,896]{1,0:T(8,128)(2,1)}, u32[]{:S(2)}) copy-start(bf16[512,896]{1,0:T(8,128)(2,1)} %refs_8_.3) | copy-start | bytes 2752516
  28.4 2.8 %copy-start.10 = (bf16[64,4096]{1,0:T(8,128)(2,1)}, bf16[64,4096]{1,0:T(8,128)(2,1)S(1)}, u32[]{:S(2)}) copy-start(bf16[64,4096]{1,0:T(8,128)(2,1)S(1)} %collective-permute-done.1) | copy-start | bytes 1572868
  28.4 20.9 %collective-permute-start.7 = (bf16[512,4096]{1,0:T(8,128)(2,1)}, bf16[512,4096]{1,0:T(8,128)(2,1)}, u32[]{:S(2)}, u32[]{:S(2)}) collective-permute-start(bf16[512,4096]{1,0:T(8,128)(2,1)} %own_w), channel_id=1, source_target_pairs={{0,1},{1,0},{2,3},{3,2},{4,5},{5,4},{6,7},{7,6},{8,9},{9,8},{10,11... | collective-permute-start | bytes 12582920 | tf_op jit(solution)/shard_map/ppermute | solution.py:165
  28.4 5.5 %collective-permute-start.3 = (bf16[64,4096]{1,0:T(8,128)(2,1)}, bf16[64,4096]{1,0:T(8,128)(2,1)}, u32[]{:S(2)}, u32[]{:S(2)}) collective-permute-start(bf16[64,4096]{1,0:T(8,128)(2,1)} %param.10), channel_id=1, source_target_pairs={{2,4},{3,5},{4,2},{5,3},{10,12},{11,13},{12,10},{13,11},{18,20},{1... | collective-permute-start | bytes 1572872 | tf_op jit(solution)/shard_map/ppermute | solution.py:172
  29.9 16.5 %collective-permute-start.4 = (bf16[64,4096]{1,0:T(8,128)(2,1)}, bf16[64,4096]{1,0:T(8,128)(2,1)}, u32[]{:S(2)}, u32[]{:S(2)}) collective-permute-start(bf16[64,4096]{1,0:T(8,128)(2,1)} %collective-permute-done), channel_id=1, source_target_pairs={{2,0},{3,1},{4,6},{5,7},{10,8},{11,9},{12,14},{13,15},{18,16},{19,... | collective-permute-start | bytes 1572872 | tf_op jit(solution)/shard_map/ppermute | solution.py:172
  33.2 16.1 %collective-permute-start.6 = (bf16[896,1024]{1,0:T(8,128)(2,1)S(1)}, bf16[896,1024]{1,0:T(8,128)(2,1)}, u32[]{:S(2)}, u32[]{:S(2)}) collective-permute-start(bf16[896,1024]{1,0:T(8,128)(2,1)S(1)} %bitcast.45), channel_id=1, source_target_pairs={{0,1},{1,0},{2,3},{3,2},{4,5},{5,4},{6,7},{7,6},{8,9},{9,8},{10,11... | collective-permute-start | bytes 5505032 | tf_op jit(solution)/shard_map/ppermute | solution.py:165
  33.8 15.5 %collective-permute-start.5 = (bf16[512,896]{1,0:T(8,128)(2,1)S(1)}, bf16[512,896]{1,0:T(8,128)(2,1)S(1)}, u32[]{:S(2)}, u32[]{:S(2)}) collective-permute-start(bf16[512,896]{1,0:T(8,128)(2,1)S(1)} %copy-done.3), channel_id=1, source_target_pairs={{0,1},{1,0},{2,3},{3,2},{4,5},{5,4},{6,7},{7,6},{8,9},{9,8},{10,11... | collective-permute-start | bytes 2752520 | tf_op jit(solution)/shard_map/ppermute | solution.py:165
  47.5 1.9 copy-start.2
  47.6 2.4 %copy-start.4 = (bf16[2,4,32,896]{3,2,1,0:T(8,128)(2,1)S(1)}, bf16[2,4,32,896]{3,2,1,0:T(8,128)(2,1)}, u32[]{:S(2)}) copy-start(bf16[2,4,32,896]{3,2,1,0:T(8,128)(2,1)} %pad_maximum_fusion.4.refs_0_) | copy-start | bytes 1376260
  49.3 4.6 %collective-permute-start.8 = (bf16[4,64,4096]{2,1,0:T(8,128)(2,1)S(1)}, bf16[4,64,4096]{2,1,0:T(8,128)(2,1)S(1)}, u32[]{:S(2)}, u32[]{:S(2)}) collective-permute-start(bf16[4,64,4096]{2,1,0:T(8,128)(2,1)S(1)} %pad_maximum_fusion.own), channel_id=1, source_target_pairs={{0,1},{1,0},{2,3},{3,2},{4,5},{5,4},{6,7},{7,6},{8,9},{9,8},{10,11... | collective-permute-start | bytes 6291464 | tf_op jit(solution)/shard_map/ppermute | solution.py:165
  49.4 24.8 %collective-permute-start.11 = (bf16[896,512]{1,0:T(8,128)(2,1)S(1)}, bf16[896,512]{1,0:T(8,128)(2,1)S(1)}, u32[]{:S(2)}, u32[]{:S(2)}) collective-permute-start(bf16[896,512]{1,0:T(8,128)(2,1)S(1)} %copy-done.2), channel_id=1, source_target_pairs={{0,1},{1,0},{2,3},{3,2},{4,5},{5,4},{6,7},{7,6},{8,9},{9,8},{10,11... | collective-permute-start | bytes 2752520 | tf_op jit(solution)/shard_map/ppermute | solution.py:165
  50.0 22.1 %collective-permute-start.10 = (bf16[2,4,32,896]{3,2,1,0:T(8,128)(2,1)S(1)}, bf16[2,4,32,896]{3,2,1,0:T(8,128)(2,1)S(1)}, u32[]{:S(2)}, u32[]{:S(2)}) collective-permute-start(bf16[2,4,32,896]{3,2,1,0:T(8,128)(2,1)S(1)} %copy-done.4), channel_id=1, source_target_pairs={{0,2},{1,3},{2,0},{3,1},{4,6},{5,7},{6,4},{7,5},{8,10},{9,11},{10,... | collective-permute-start | bytes 1376264 | tf_op jit(solution)/shard_map/ppermute | solution.py:172
  50.0 24.3 %collective-permute-start.9 = (bf16[2,4,32,896]{3,2,1,0:T(8,128)(2,1)S(1)}, bf16[2,4,32,896]{3,2,1,0:T(8,128)(2,1)S(1)}, u32[]{:S(2)}, u32[]{:S(2)}) collective-permute-start(bf16[2,4,32,896]{3,2,1,0:T(8,128)(2,1)S(1)} %copy-done.4), channel_id=1, source_target_pairs={{0,4},{1,5},{2,6},{3,7},{4,0},{5,1},{6,2},{7,3},{8,12},{9,13},{10,... | collective-permute-start | bytes 1376264 | tf_op jit(solution)/shard_map/ppermute | solution.py:172
  53.9 1.4 copy-start.12
  74.3 2.7 %collective-permute-start.14 = (bf16[4,64,1536]{2,1,0:T(8,128)(2,1)S(1)}, bf16[4,64,1536]{2,1,0:T(8,128)(2,1)S(1)}, u32[]{:S(2)}, u32[]{:S(2)}) collective-permute-start(bf16[4,64,1536]{2,1,0:T(8,128)(2,1)S(1)} %get-tuple-element.72), channel_id=1, source_target_pairs={{0,1},{1,0},{2,3},{3,2},{4,5},{5,4},{6,7},{7,6},{8,9},{9,8},{10,11... | collective-permute-start | bytes 2359304 | tf_op jit(solution)/shard_map/ppermute | solution.py:165
  74.3 2.6 %collective-permute-start.15 = (bf16[4,64,512]{2,1,0:T(8,128)(2,1)S(1)}, bf16[4,64,512]{2,1,0:T(8,128)(2,1)S(1)}, u32[]{:S(2)}, u32[]{:S(2)}) collective-permute-start(bf16[4,64,512]{2,1,0:T(8,128)(2,1)S(1)} %slice.35), channel_id=1, source_target_pairs={{0,1},{1,0},{2,3},{3,2},{4,5},{5,4},{6,7},{7,6},{8,9},{9,8},{10,11... | collective-permute-start | bytes 786440 | tf_op jit(solution)/shard_map/ppermute | solution.py:165
  74.9 3.9 %collective-permute-start.12 = (bf16[2,4,32,896]{3,2,1,0:T(8,128)(2,1)S(1)}, bf16[2,4,32,896]{3,2,1,0:T(8,128)(2,1)S(1)}, u32[]{:S(2)}, u32[]{:S(2)}) collective-permute-start(bf16[2,4,32,896]{3,2,1,0:T(8,128)(2,1)S(1)} %copy-done.4), channel_id=1, source_target_pairs={{2,4},{3,5},{4,2},{5,3},{10,12},{11,13},{12,10},{13,11},{18,20},{1... | collective-permute-start | bytes 1376264 | tf_op jit(solution)/shard_map/ppermute | solution.py:172
  75.6 14.3 %collective-permute-start.13 = (bf16[2,4,32,896]{3,2,1,0:T(8,128)(2,1)S(1)}, bf16[2,4,32,896]{3,2,1,0:T(8,128)(2,1)S(1)}, u32[]{:S(2)}, u32[]{:S(2)}) collective-permute-start(bf16[2,4,32,896]{3,2,1,0:T(8,128)(2,1)S(1)} %collective-permute-done.9.refs_2_), channel_id=1, source_target_pairs={{2,0},{3,1},{4,6},{5,7},{10,8},{11,9},{12,14},{13,15},{18,16},{19,... | collective-permute-start | bytes 1376264 | tf_op jit(solution)/shard_map/ppermute | solution.py:172
  77.1 0.7 collective-permute-start.16
  96.9 13.9 %copy-start.11 = (f32[896]{0:T(1024)S(1)}, f32[896]{0:T(1024)}, u32[]{:S(2)}) copy-start(f32[896]{0:T(1024)} %param.17) | copy-start | bytes 10756
  96.9 12.5 %collective-permute-start.19 = (bf16[256,896]{1,0:T(8,128)(2,1)S(1)}, bf16[256,896]{1,0:T(8,128)(2,1)S(1)}, u32[]{:S(2)}, u32[]{:S(2)}) collective-permute-start(bf16[256,896]{1,0:T(8,128)(2,1)S(1)} %encode.5), channel_id=1, source_target_pairs={{0,2},{1,3},{6,4},{7,5},{8,10},{9,11},{14,12},{15,13},{16,18},{17,... | collective-permute-start | bytes 1376264 | tf_op jit(solution)/shard_map/ppermute | solution.py:172
  98.5 28.8 %collective-permute-start.18 = (bf16[256,896]{1,0:T(8,128)(2,1)S(1)}, bf16[256,896]{1,0:T(8,128)(2,1)S(1)}, u32[]{:S(2)}, u32[]{:S(2)}) collective-permute-start(bf16[256,896]{1,0:T(8,128)(2,1)S(1)} %encode.4), channel_id=1, source_target_pairs={{0,4},{1,5},{6,2},{7,3},{8,12},{9,13},{14,10},{15,11},{16,20},{17,... | collective-permute-start | bytes 1376264 | tf_op jit(solution)/shard_map/ppermute | solution.py:172
  100.7 30.1 %collective-permute-start.21 = (bf16[256,896]{1,0:T(8,128)(2,1)S(1)}, bf16[256,896]{1,0:T(8,128)(2,1)S(1)}, u32[]{:S(2)}, u32[]{:S(2)}) collective-permute-start(bf16[256,896]{1,0:T(8,128)(2,1)S(1)} %encode.5), channel_id=1, source_target_pairs={{2,4},{3,5},{4,2},{5,3},{10,12},{11,13},{12,10},{13,11},{18,20},{1... | collective-permute-start | bytes 1376264 | tf_op jit(solution)/shard_map/ppermute | solution.py:172
  105.0 22.3 %collective-permute-start.17 = (bf16[256,896]{1,0:T(8,128)(2,1)S(1)}, bf16[256,896]{1,0:T(8,128)(2,1)S(1)}, u32[]{:S(2)}, u32[]{:S(2)}) collective-permute-start(bf16[256,896]{1,0:T(8,128)(2,1)S(1)} %encode.6), channel_id=1, source_target_pairs={{0,2},{1,3},{2,0},{3,1},{4,6},{5,7},{6,4},{7,5},{8,10},{9,11},{10,... | collective-permute-start | bytes 1376264 | tf_op jit(solution)/shard_map/ppermute | solution.py:172
  109.6 22.2 %collective-permute-start.20 = (bf16[256,896]{1,0:T(8,128)(2,1)S(1)}, bf16[256,896]{1,0:T(8,128)(2,1)S(1)}, u32[]{:S(2)}, u32[]{:S(2)}) collective-permute-start(bf16[256,896]{1,0:T(8,128)(2,1)S(1)} %add_convert_fusion.2), channel_id=1, source_target_pairs={{2,6},{3,7},{4,0},{5,1},{10,14},{11,15},{12,8},{13,9},{18,22},{19,... | collective-permute-start | bytes 1376264 | tf_op jit(solution)/shard_map/ppermute | solution.py:172
  130.8 4.5 %copy-start.13 = (s32[32]{0:T(128)S(1)}, s32[32]{0:T(128)}, u32[]{:S(2)}) copy-start(s32[32]{0:T(128)} %param.13) | copy-start | bytes 388
  130.8 4.8 %copy-start.5 = (bf16[5,64,1024]{2,1,0:T(8,128)(2,1)S(1)}, bf16[5,64,1024]{2,1,0:T(8,128)(2,1)}, u32[]{:S(2)}) copy-start(bf16[5,64,1024]{2,1,0:T(8,128)(2,1)} %pad_maximum_fusion.1.refs_3_.refs_4_.queries) | copy-start | bytes 1966084
  132.3 21.7 %collective-permute-start.22 = (bf16[256,896]{1,0:T(8,128)(2,1)S(1)}, bf16[256,896]{1,0:T(8,128)(2,1)}, u32[]{:S(2)}, u32[]{:S(2)}) collective-permute-start(bf16[256,896]{1,0:T(8,128)(2,1)S(1)} %normed.1.refs_0_), channel_id=1, source_target_pairs={{0,4},{1,5},{2,6},{3,7},{4,0},{5,1},{6,2},{7,3},{8,12},{9,13},{10,... | collective-permute-start | bytes 1376264 | tf_op jit(solution)/shard_map/ppermute | solution.py:172
  134.9 21.8 %collective-permute-start.25 = (bf16[256,896]{1,0:T(8,128)(2,1)S(1)}, bf16[256,896]{1,0:T(8,128)(2,1)}, u32[]{:S(2)}, u32[]{:S(2)}) collective-permute-start(bf16[256,896]{1,0:T(8,128)(2,1)S(1)} %normed.1.refs_0_), channel_id=1, source_target_pairs={{0,2},{1,3},{2,0},{3,1},{4,6},{5,7},{6,4},{7,5},{8,10},{9,11},{10,... | collective-permute-start | bytes 1376264 | tf_op jit(solution)/shard_map/ppermute | solution.py:172
  154.0 14.3 %collective-permute-start.23 = (bf16[256,896]{1,0:T(8,128)(2,1)S(1)}, bf16[256,896]{1,0:T(8,128)(2,1)}, u32[]{:S(2)}, u32[]{:S(2)}) collective-permute-start(bf16[256,896]{1,0:T(8,128)(2,1)S(1)} %normed.1.refs_0_), channel_id=1, source_target_pairs={{2,4},{3,5},{4,2},{5,3},{10,12},{11,13},{12,10},{13,11},{18,20},{1... | collective-permute-start | bytes 1376264 | tf_op jit(solution)/shard_map/ppermute | solution.py:172
  155.4 13.5 %collective-permute-start.24 = (bf16[256,896]{1,0:T(8,128)(2,1)}, bf16[256,896]{1,0:T(8,128)(2,1)}, u32[]{:S(2)}, u32[]{:S(2)}) collective-permute-start(bf16[256,896]{1,0:T(8,128)(2,1)} %collective-permute-done.22.refs_1_), channel_id=1, source_target_pairs={{2,0},{3,1},{4,6},{5,7},{10,8},{11,9},{12,14},{13,15},{18,16},{19,... | collective-permute-start | bytes 1376264 | tf_op jit(solution)/shard_map/ppermute | solution.py:172
  165.7 0.7 copy-start.6
  166.3 0.7 copy-start.8
  167.0 1.3 collective-permute-start.26
  169.0 0.9 copy-start.7
  169.9 0.9 copy-start.9
  170.8 25.7 %copy-start.1 = (bf16[512,4096]{1,0:T(8,128)(2,1)S(1)}, bf16[512,4096]{1,0:T(8,128)(2,1)}, u32[]{:S(2)}) copy-start(bf16[512,4096]{1,0:T(8,128)(2,1)} %own_w) | copy-start | bytes 12582916
  179.0 15.3 %collective-permute-start.29 = (bf16[64,4096]{1,0:T(8,128)(2,1)S(1)}, bf16[64,4096]{1,0:T(8,128)(2,1)S(1)}, u32[]{:S(2)}, u32[]{:S(2)}) collective-permute-start(bf16[64,4096]{1,0:T(8,128)(2,1)S(1)} %get-tuple-element.110), channel_id=1, source_target_pairs={{0,2},{1,3},{6,4},{7,5},{8,10},{9,11},{14,12},{15,13},{16,18},{17,... | collective-permute-start | bytes 1572872 | tf_op jit(solution)/shard_map/ppermute | solution.py:172
  183.8 33.0 %collective-permute-start.31 = (bf16[64,4096]{1,0:T(8,128)(2,1)S(1)}, bf16[64,4096]{1,0:T(8,128)(2,1)S(1)}, u32[]{:S(2)}, u32[]{:S(2)}) collective-permute-start(bf16[64,4096]{1,0:T(8,128)(2,1)S(1)} %get-tuple-element.110), channel_id=1, source_target_pairs={{2,4},{3,5},{4,2},{5,3},{10,12},{11,13},{12,10},{13,11},{18,20},{1... | collective-permute-start | bytes 1572872 | tf_op jit(solution)/shard_map/ppermute | solution.py:172
  184.5 21.1 %collective-permute-start.27 = (bf16[64,4096]{1,0:T(8,128)(2,1)S(1)}, bf16[64,4096]{1,0:T(8,128)(2,1)S(1)}, u32[]{:S(2)}, u32[]{:S(2)}) collective-permute-start(bf16[64,4096]{1,0:T(8,128)(2,1)S(1)} %get-tuple-element.108), channel_id=1, source_target_pairs={{0,2},{1,3},{2,0},{3,1},{4,6},{5,7},{6,4},{7,5},{8,10},{9,11},{10,... | collective-permute-start | bytes 1572872 | tf_op jit(solution)/shard_map/ppermute | solution.py:172
  186.4 30.4 %collective-permute-start.28 = (bf16[64,4096]{1,0:T(8,128)(2,1)S(1)}, bf16[64,4096]{1,0:T(8,128)(2,1)S(1)}, u32[]{:S(2)}, u32[]{:S(2)}) collective-permute-start(bf16[64,4096]{1,0:T(8,128)(2,1)S(1)} %get-tuple-element.109), channel_id=1, source_target_pairs={{0,4},{1,5},{6,2},{7,3},{8,12},{9,13},{14,10},{15,11},{16,20},{17,... | collective-permute-start | bytes 1572872 | tf_op jit(solution)/shard_map/ppermute | solution.py:172
  194.5 22.4 %collective-permute-start.30 = (bf16[64,4096]{1,0:T(8,128)(2,1)S(1)}, bf16[64,4096]{1,0:T(8,128)(2,1)S(1)}, u32[]{:S(2)}, u32[]{:S(2)}) collective-permute-start(bf16[64,4096]{1,0:T(8,128)(2,1)S(1)} %add_convert_fusion.1), channel_id=1, source_target_pairs={{2,6},{3,7},{4,0},{5,1},{10,14},{11,15},{12,8},{13,9},{18,22},{19,... | collective-permute-start | bytes 1572872 | tf_op jit(solution)/shard_map/ppermute | solution.py:172
  195.8 0.7 collective-permute-start.32
  217.3 7.9 %collective-permute-start.33 = (bf16[64,4096]{1,0:T(8,128)(2,1)S(1)}, bf16[64,4096]{1,0:T(8,128)(2,1)S(1)}, u32[]{:S(2)}, u32[]{:S(2)}) collective-permute-start(bf16[64,4096]{1,0:T(8,128)(2,1)S(1)} %add_convert_fusion), channel_id=1, source_target_pairs={{0,1},{1,0},{2,3},{3,2},{4,5},{5,4},{6,7},{7,6},{8,9},{9,8},{10,11... | collective-permute-start | bytes 1572872 | tf_op jit(solution)/shard_map/ppermute | solution.py:165

commit v3 on v2

--- a/solution.py
+++ b/solution.py
@@ -149,8 +149,8 @@
     return (cross_out, encoded_mine)
 
 
-def params(mib):
-    return pltpu.CompilerParams(vmem_limit_bytes=mib * 1024 * 1024)
+def params():
+    return pltpu.CompilerParams(vmem_limit_bytes=44 * 1024 * 1024)
 
 
 def dot(a, b):
@@ -173,14 +173,12 @@
 
 
 def scattered(part):
-    two = part(2)
+    two, three = part((2, 3))
     outer = hop(two, 2, ENDS)
-    three, two = part(3, two)
     passed, middle = hop(three, 1, ENDS), hop(three, 3, MIDDLE)
-    one, three = part(1, three)
+    one, own = part((1, 0))
     one = hop(one, 1)
     inner = hop((two.astype(F32) + passed.astype(F32)).astype(BF16), 2, MIDDLE)
-    own, one, outer = part(0, one, outer)
     return [own, one, outer, inner, middle]
 
 
@@ -236,7 +234,7 @@
         out_specs=[VMEM, VMEM],
         out_shape=[shape, shape],
         scratch_shapes=[pltpu.VMEM(w.shape, BF16), pltpu.SemaphoreType.DMA((pieces,))],
-        compiler_params=params(50),
+        compiler_params=params(),
         cost_estimate=pl.CostEstimate(
             flops=16 * rows * depth * width * pieces,
             bytes_accessed=2 * depth * (width * pieces + 8 * rows),
@@ -246,62 +244,68 @@
     )(pos, own, other, w)
 
 
-def enc_kernel(flip, pos, *refs):
+def enc_kernel(flips, pos, *refs):
     parts, weights, refs = refs[:5], (refs[5:9], refs[9:13]), refs[13:]
-    out, refs = refs[0], refs[1:]
-    if flip == 0:
-        raw, refs = refs[0], refs[1:]
-    rows, att, sems = refs
-    i = pos[0] ^ flip
-    jobs = fetches(pos, parts, lambda ref, j: [(ref.at[c, i], rows.at[j, c]) for c in range(2)], sems)
-    begin(jobs)
-    finish(jobs)
-    x = rows[...].reshape(out.shape)
-    if flip == 0:
-        raw[...] = x
-    here = pl.ds(pl.multiple_of(i * GROUP, GROUP), GROUP)
-    total = None
-    for wq, keys, values, wo in weights:
+    n = len(flips)
+    outs, (rows, att, sems) = refs[:n], refs[-3:]
+    for k, flip in enumerate(flips):
+        i = pos[0] ^ flip
+        place = lambda ref, j: [(ref.at[c, i], rows.at[k, j, c]) for c in range(2)]
+        begin(fetches(pos, parts, place, sems.at[k]))
+    for k, flip in enumerate(flips):
+        i = pos[0] ^ flip
+        place = lambda ref, j: [(ref.at[c, i], rows.at[k, j, c]) for c in range(2)]
+        finish(fetches(pos, parts, place, sems.at[k]))
+    each_rows, width = outs[0].shape
+    x = rows[...].reshape(n * each_rows, width)
+    if flips[-1] == 0:
+        refs[n][...] = x[(n - 1) * each_rows :]
+    heads = weights[0][0].shape[1]
+    for w, (wq, keys, values, _) in enumerate(weights):
         q = dot(x, wq[...]).astype(BF16)
-        for h in range(0, wq.shape[1], HEAD_DIM):
-            cols = pl.ds(h, HEAD_DIM)
-            scores = dot_t(keys[here, cols], q[:, h : h + HEAD_DIM]) * SCALE
-            raised = jnp.exp(scores - jnp.max(scores, axis=0, keepdims=True))
-            share = (raised / jnp.sum(raised, axis=0, keepdims=True)).astype(BF16)
-            att[:, cols] = lax.dot_general(
-                share, values[here, cols], (((0,), (0,)), ((), ())), preferred_element_type=F32
-            ).astype(BF16)
-        part = dot(att[...], wo[...])
-        total = part if total is None else total + part
-    out[...] = total.astype(BF16)
-
-
-def encode(pos, parts, flip, queries, projected, outs):
+        for k, flip in enumerate(flips):
+            here = pl.ds(pl.multiple_of((pos[0] ^ flip) * GROUP, GROUP), GROUP)
+            mine = pl.ds(k * each_rows, each_rows)
+            for h in range(0, heads, HEAD_DIM):
+                cols = pl.ds(h, HEAD_DIM)
+                scores = dot_t(keys[here, cols], q[k * each_rows : (k + 1) * each_rows, h : h + HEAD_DIM]) * SCALE
+                raised = jnp.exp(scores - jnp.max(scores, axis=0, keepdims=True))
+                share = (raised / jnp.sum(raised, axis=0, keepdims=True)).astype(BF16)
+                att[mine, pl.ds(w * heads + h, HEAD_DIM)] = lax.dot_general(
+                    share, values[here, cols], (((0,), (0,)), ((), ())), preferred_element_type=F32
+                ).astype(BF16)
+    total = dot(att[:, pl.ds(0, heads)], weights[0][3][...]) + dot(att[:, pl.ds(heads, heads)], weights[1][3][...])
+    for k, out in enumerate(outs):
+        out[...] = total[k * each_rows : (k + 1) * each_rows].astype(BF16)
+
+
+def encode(pos, parts, flips, queries, projected, outs):
     _, _, part, width = parts[0].shape
     tokens = projected[0].shape[0]
     heads = queries[0].shape[1]
     rows = 8 * part
+    n = len(flips)
     kv = [pl.BlockSpec((tokens, heads), lambda i: (0, 1)), pl.BlockSpec((tokens, heads), lambda i: (0, 2))]
-    shape = jax.ShapeDtypeStruct((rows, width), BF16)
     args = []
     for wq, proj, wo in zip(queries, projected, outs):
         args += [wq, proj, proj, wo]
+    results = n + (flips[-1] == 0)
     return pl.pallas_call(
-        functools.partial(enc_kernel, flip),
+        functools.partial(enc_kernel, flips),
         grid=(1,),
         in_specs=[SMEM] + [ANY] * 5 + ([VMEM] + kv + [VMEM]) * 2,
-        out_specs=[VMEM] * (1 if flip else 2),
-        out_shape=[shape] * (1 if flip else 2),
+        out_specs=[VMEM] * results,
+        out_shape=[jax.ShapeDtypeStruct((rows, width), BF16)] * results,
         scratch_shapes=[
-            pltpu.VMEM((4, 2, part, width), BF16),
-            pltpu.VMEM((rows, heads), BF16),
-            pltpu.SemaphoreType.DMA((10,)),
+            pltpu.VMEM((n, 4, 2, part, width), BF16),
+            pltpu.VMEM((n * rows, 2 * heads), BF16),
+            pltpu.SemaphoreType.DMA((n, 10)),
         ],
-        compiler_params=params(32),
+        compiler_params=params(),
         cost_estimate=pl.CostEstimate(
-            flops=2 * rows * heads * (4 * width + 4 * GROUP),
-            bytes_accessed=4 * rows * width + 8 * heads * width,
-            transcendentals=rows * heads,
+            flops=2 * n * rows * heads * (4 * width + 4 * GROUP),
+            bytes_accessed=4 * n * rows * width + 8 * heads * width,
+            transcendentals=n * rows * heads,
         ),
         name="encode",
     )(pos, *parts, *args)
@@ -320,7 +324,7 @@
         in_specs=[VMEM] * (len(parts) + 2),
         out_specs=VMEM,
         out_shape=jax.ShapeDtypeStruct(raw.shape, BF16),
-        compiler_params=params(8),
+        compiler_params=params(),
         name="normed",
     )(*parts, raw, gain)
 
@@ -342,27 +346,29 @@
             out[:, pl.ds(at, HEAD_DIM)] = dot(share, kv[:, heads + h : heads + h + HEAD_DIM]).astype(BF16)
 
 
-def attend_kernel(flips, pos, counts, *refs):
-    n = len(flips)
-    rows, (own_kv, other_kv, queries), refs = refs[:n], refs[n : n + 3], refs[n + 3 :]
-    outs = refs[-n:] if n == 1 else refs[1 : n + 1]
-    for flip, x, out in zip(flips, rows, outs):
-        attention(pos[0] ^ flip, pos[1], counts, x[...], (own_kv, other_kv), queries, out)
-    if n > 1:
-        z = pos[0]
-        refs[-1][...] = jnp.where(z == 3, refs[0][...], jnp.where(z == 2, outs[0][...], outs[1][...]))
-
-
-def attend(pos, counts, flips, rows, wkvs, queries, *earlier):
+def attend_kernel(pos, counts, rows, own_kv, other_kv, queries, out):
+    attention(pos[0], pos[1], counts, rows[...], (own_kv, other_kv), queries, out)
+
+
+def attend_more_kernel(pos, counts, one, two, own_kv, other_kv, queries, first, out):
+    out[0] = first[...]
+    for flip, x in (1, one), (2, two):
+        attention(pos[0] ^ flip, pos[1], counts, x[...], (own_kv, other_kv), queries, out.at[flip])
+    z = pos[0]
+    out[3] = jnp.where(z == 3, out[0], jnp.where(z == 2, out[1], out[2]))
+
+
+def attend(pos, counts, rows, wkvs, queries, *earlier):
     keys, width = rows[0].shape
     both = wkvs[0].shape[1]
-    n = len(flips)
+    n = len(rows)
+    shape = (4, GROUP, both) if earlier else (GROUP, both)
     return pl.pallas_call(
-        functools.partial(attend_kernel, flips),
+        attend_more_kernel if earlier else attend_kernel,
         in_specs=[SMEM, SMEM] + [VMEM] * (n + 3 + len(earlier)),
-        out_specs=[VMEM] * (n + len(earlier)),
-        out_shape=[jax.ShapeDtypeStruct((GROUP, both), BF16)] * (n + len(earlier)),
-        compiler_params=params(40),
+        out_specs=VMEM,
+        out_shape=jax.ShapeDtypeStruct(shape, BF16),
+        compiler_params=params(),
         cost_estimate=pl.CostEstimate(
             flops=4 * n * keys * both * (width + GROUP),
             bytes_accessed=2 * (2 * width * both + n * keys * width),
@@ -388,7 +394,7 @@
 
 
 def last_kernel(pos, counts, middle, far, own_kv, other_kv, queries, *refs):
-    atts, before, wos, outs, (got, held, loaded, sems) = refs[:3], refs[3], refs[4:6], refs[6:10], refs[10:]
+    atts, before, wos, outs, (got, held, loaded, sems) = refs[0], refs[1], refs[2:4], refs[4:8], refs[8:]
     loads = loads_of(wos, loaded, sems)
     for load in sum(loads, []):
         load.start()
@@ -396,8 +402,8 @@
     x = jnp.where((z == 1) | (z == 2), middle[...], far[...])
     attention(z ^ 3, core, counts, x, (own_kv, other_kv), queries, got)
     held[0] = before[...]
-    for flip, att in enumerate((*atts, got)):
-        held[(z ^ flip) + 1] = att[...]
+    for flip in range(4):
+        held[(z ^ flip) + 1] = got[...] if flip == 3 else atts[flip]
     first = lax.broadcasted_iota(jnp.int32, got.shape, 0) == 0
     rows = []
     for flip in range(4):
@@ -419,7 +425,7 @@
     pieces = 4
     return pl.pallas_call(
         last_kernel,
-        in_specs=[SMEM, SMEM] + [VMEM] * 9 + [HBM, ANY],
+        in_specs=[SMEM, SMEM] + [VMEM] * 7 + [HBM, ANY],
         out_specs=[VMEM] * 5,
         out_shape=[jax.ShapeDtypeStruct((GROUP, model), BF16)] * 4 + [jax.ShapeDtypeStruct(before.shape, BF16)],
         scratch_shapes=[
@@ -427,14 +433,14 @@
             pltpu.VMEM((pieces, 2 * heads, model // pieces), BF16),
             pltpu.SemaphoreType.DMA((2, pieces)),
         ],
-        compiler_params=params(48),
+        compiler_params=params(),
         cost_estimate=pl.CostEstimate(
             flops=16 * GROUP * heads * model + 8 * keys * heads * (width + GROUP),
             bytes_accessed=4 * heads * model + 8 * GROUP * model,
             transcendentals=2 * GROUP * keys * heads // HEAD_DIM,
         ),
         name="last_attend",
-    )(pos, counts, middle, far, *wkvs, queries, *atts, before, *wos)
+    )(pos, counts, middle, far, *wkvs, queries, atts, before, *wos)
 
 
 def late_kernel(before, own_w, other_w, out, loaded, sems):
@@ -462,7 +468,7 @@
             pltpu.VMEM((pieces, 2 * heads, model // pieces), BF16),
             pltpu.SemaphoreType.DMA((2, pieces)),
         ],
-        compiler_params=params(48),
+        compiler_params=params(),
         cost_estimate=pl.CostEstimate(
             flops=4 * GROUP * heads * model, bytes_accessed=4 * heads * model, transcendentals=0
         ),
@@ -506,16 +512,15 @@
         (two, one, tokens, nbr_own, enc_query, enc_out, nbr_proj, out_proj)
     )
     far, middle = hop(two, 1, MIDDLE), hop(own, 3, MIDDLE)
-    nbr_two, nbr_one = hop(nbr_own, 2), hop(nbr_own, 1)
-    encqs = (enc_query, swapped(enc_query, nz))
-    column = jnp.stack([own, one, two, jnp.where((z == 1) | (z == 2), middle, far)])
     wkv = nbr_proj.reshape(enc_width, 2 * width)
     encos, wkvs, outps = [(w, swapped(w, nz)) for w in (enc_out, wkv, out_proj)]
+    column = jnp.stack([own, one, two, jnp.where((z == 1) | (z == 2), middle, far)])
     column, encos, wkvs, outps = held((column, encos, wkvs, outps))
-    mine, theirs = project(pos, column, swapped(column, nz), dec_proj.transpose(1, 0, 2))
-    mine, theirs, nbr_two, nbr_one, nbr_own, encqs, enc_out, nbr_proj, out_proj = held(
-        (mine, theirs, nbr_two, nbr_one, nbr_own, encqs, enc_out, nbr_proj, out_proj)
-    )
+    other = swapped(column, nz)
+    encqs = (enc_query, swapped(enc_query, nz))
+    nbr_two, nbr_one = hop(nbr_own, 2), hop(nbr_own, 1)
+    mine, theirs = project(pos, column, other, dec_proj.transpose(1, 0, 2))
+    mine, theirs, nbr_two, nbr_one, nbr_own, encqs = held((mine, theirs, nbr_two, nbr_one, nbr_own, encqs))
     nbrs = (nbr_own, nbr_one, nbr_two, hop(nbr_own, 3, MIDDLE), hop(nbr_two, 1, MIDDLE))
     projected = [p.reshape(nz * GROUP, 3 * width) for p in (mine, swapped(theirs, nz))]
 
@@ -529,32 +534,30 @@
         lax.dynamic_slice_in_dim(valid_counts, seq_index * ch_grp, ch_grp, 0).reshape(nz, 2), core, 1, False
     )
 
-    nbrs, queries, encos, wkvs, outps = held((nbrs, queries, encos, wkvs, outps))
+    nbrs, queries = held((nbrs, queries))
     raws = []
 
-    def part(flip, *after):
-        after, here = held((after, pos))
-        got = encode(here, nbrs, flip, encqs, projected, encos)
-        raws.extend(got[1:])
-        return [got[0], *after] if after else got[0]
+    def part(flips):
+        got = encode(pos, nbrs, flips, encqs, projected, encos)
+        raws.extend(got[len(flips) :])
+        return got[: len(flips)]
 
     arrived = scattered(part)
     enc_own = normed(arrived, raws[0], enc_gain.reshape(1, -1))
     enc_two, enc_one = hop(enc_own, 2), hop(enc_own, 1)
-    atts = list(attend(pos, counts, (0,), (enc_own,), wkvs, queries))
-    enc_two, enc_mine, atts[0] = lax.optimization_barrier((enc_two, enc_own, atts[0]))
+    first = attend(pos, counts, (enc_own,), wkvs, queries)
+    enc_two, enc_mine, first = held((enc_two, enc_own, first))
     enc_middle, enc_far = hop(enc_mine, 3, MIDDLE), hop(enc_two, 1, MIDDLE)
-    *more, before = attend(pos, counts, (1, 2), (enc_one, enc_two), wkvs, queries, atts[0])
-    atts += more
+    atts = attend(pos, counts, (enc_one, enc_two), wkvs, queries, first)
 
     def onward(x, chips):
         route = [(q * 2 * nz + 2 * i + 1, (q + 1) * 2 * nz + 2 * i + 1) for q in range(n_seq - 1) for i in chips]
         got = lax.ppermute(x, ("seq", "nbr"), route)
         return jnp.where((seq_index * ch_grp * GROUP) % SEQ_LEN == 0, 0, got).astype(BF16)
 
-    before = onward(before, (1, 2, 3))
+    before = onward(atts[3], (1, 2, 3))
     *outs, last = last_attend(pos, counts, enc_middle, enc_far, wkvs, queries, atts, before, outps)
-    arrived = scattered(lambda flip, *after: [outs[flip], *after] if after else outs[flip])
+    arrived = scattered(lambda flips: [outs[flip] for flip in flips])
     arrived.append(late_out(onward(last, (0,)), outps))
     mine = sum(part.astype(F32) for part in arrived).astype(BF16)
     theirs = swapped(mine, nz)

time: 227 us -> 221 us (0.974)
  waiting for transfers between devices: 108 us -> 118 us
  starting transfers between devices: 49.3 us -> 41.2 us
  Pallas kernels: 50.8 us -> 46.3 us
    ppermute x22, waiting for transfers between devices: 107 us -> 117 us  [hop(): lax.ppermute(x, 'nbr', [(2 * z + c, 2 * (z ^ flip) + c) for z in chips fo...]
    ppermute x9, starting transfers between devices: 8.2 us -> 3.79 us  [swapped(): return lax.ppermute(x, 'nbr', [(n, n ^ 1) for n in range(2 * nz)])]
    pallas_call x7 -> x5, Pallas kernels: 36.1 us -> 32.7 us  [the longest x2 13.1 us: attend(): pl.pallas_call(attend_more_kernel if earlier else attend_kernel, in_specs...]
    ppermute x22, starting transfers between devices: 38.4 us -> 35.2 us  [hop(): lax.ppermute(x, 'nbr', [(2 * z + c, 2 * (z ^ flip) + c) for z in chips fo...]
    unnamed x29 -> x19, local copies, waits for them, and re-layouts: 6.52 us -> 3.86 us
  transfers between devices with their start and end apart: 34 -> 34, of which waited for: 16 -> 19; matrix products, arithmetic and copies ran while one was open for 5% -> 4% of each run, Pallas kernels for 16% -> 14%
where the time goes in v3:
time: 221 us; the launch traced here: 220 us
  waiting for transfers between devices  118 us (53%)
  Pallas kernels  46.3 us (21%)
  starting transfers between devices  41.2 us (19%)
  local copies, waits for them, and re-layouts  7.64 us (3%)
  other arithmetic  5.49 us (2%)
    ppermute x22, waiting for transfers between devices, hop(): lax.ppermute(x, 'nbr', [(2 * z + c, 2 * (z ^ flip) + c) for z in chips fo...  117 us
    ppermute x22, starting transfers between devices, hop(): lax.ppermute(x, 'nbr', [(2 * z + c, 2 * (z ^ flip) + c) for z in chips fo...  35.2 us
    pallas_call x2, Pallas kernels, attend(): pl.pallas_call(attend_more_kernel if earlier else attend_kernel, in_specs...  13.1 us
    pallas_call x2, Pallas kernels, encode(): pl.pallas_call(functools.partial(enc_kernel, flips), grid=(1,), in_specs=...  11 us
    pallas_call x1, Pallas kernels, project(): pl.pallas_call(proj_kernel, in_specs=[SMEM, VMEM, VMEM, HBM], out_specs=[...  9.73 us
    pallas_call x1, Pallas kernels, last_attend(): pl.pallas_call(last_kernel, in_specs=[SMEM, SMEM] + [VMEM] * 7 + [HBM, AN...  8.63 us
  transfers between devices with their start and end apart: 34, of which 19 were waited for; matrix products, arithmetic and copies ran while one was open for 4% of the time, Pallas kernels for 14%

profile of v3, /device:TPU:0, one launch (start us, length us, event | category | flops | bytes accessed | tf_op | source)
XLA Modules:
  0.0 220.4 jit_solution(11622028439080253026)
XLA Ops:
  0.6 4.1 %collective-permute-start = (bf16[64,4096]{1,0:T(8,128)(2,1)}, bf16[64,4096]{1,0:T(8,128)(2,1)}, u32[]{:S(2)}, u32[]{:S(2)}) collective-permute-start(bf16[64,4096]{1,0:T(8,128)(2,1)} %param.10), channel_id=1, source_target_pairs={{0,4},{1,5},{2,6},{3,7},{4,0},{5,1},{6,2},{7,3},{8,12},{9,13},{10,... | collective-permute-start | bytes 1572872 | tf_op jit(solution)/shard_map/ppermute | solution.py:172
  4.7 1.6 collective-permute-start.1
  6.3 0.7 broadcast_subtract_fusion
  7.4 0.6 gather_fusion.1
  8.3 0.6 gather_fusion
  8.8 0.7 collective-permute-done.2
  9.6 18.8 %collective-permute-done = bf16[64,4096]{1,0:T(8,128)(2,1)} collective-permute-done((bf16[64,4096]{1,0:T(8,128)(2,1)}, bf16[64,4096]{1,0:T(8,128)(2,1)}, u32[]{:S(2)}, u32[]{:S(2)}) %collective-permute-start) | collective-permute-done | bytes 524320 | tf_op jit(solution)/shard_map/ppermute | solution.py:172
  28.4 0.7 collective-permute-start.3
  29.1 1.3 collective-permute-start.4
  30.4 2.0 copy.18
  32.4 0.6 collective-permute-start.6
  33.1 13.1 %collective-permute-done.4 = bf16[64,4096]{1,0:T(8,128)(2,1)} collective-permute-done((bf16[64,4096]{1,0:T(8,128)(2,1)}, bf16[64,4096]{1,0:T(8,128)(2,1)}, u32[]{:S(2)}, u32[]{:S(2)}) %collective-permute-start.4) | collective-permute-done | bytes 524320 | tf_op jit(solution)/shard_map/ppermute | solution.py:172
  46.2 1.1 select_bitcast_fusion
  47.3 1.7 pad_maximum_fusion.own
  49.1 0.5 collective-permute-start.11
  49.7 3.4 %collective-permute-start.10 = (bf16[2,4,32,896]{3,2,1,0:T(8,128)(2,1)S(1)}, bf16[2,4,32,896]{3,2,1,0:T(8,128)(2,1)S(1)}, u32[]{:S(2)}, u32[]{:S(2)}) collective-permute-start(bf16[2,4,32,896]{3,2,1,0:T(8,128)(2,1)S(1)} %pad_maximum_fusion.4.refs_0_), channel_id=1, source_target_pairs={{0,2},{1,3},{2,0},{3,1},{4,6},{5,7},{6,4},{7,5},{8,10},{9,11},{10,... | collective-permute-start | bytes 1376264 | tf_op jit(solution)/shard_map/ppermute | solution.py:172
  53.1 0.2 collective-permute-done.8.other
  53.2 9.7 %project.1 = (bf16[4,64,1536]{2,1,0:T(8,128)(2,1)S(1)}, bf16[4,64,1536]{2,1,0:T(8,128)(2,1)S(1)}) custom-call(s32[2]{0:T(128)S(1)} %pad_add_fusion.pos, bf16[4,64,4096]{2,1,0:T(8,128)(2,1)S(1)} %pad_maximum_fusion.own, bf16[4,64,4096]{2,1,0:T(8,128)(2,1)S(1)} %collective-permute-done.8.other, bf16[3,4096,512]{2,1,0:T(8,128)(2,1)} %bitcast.53), custom_call_target="tpu_custom_call" | custom-call | flops 6442450944 | bytes 16777216 | tf_op jit(solution)/shard_map/project/pallas_call | solution.py:231
  63.0 10.0 %collective-permute-done.9.refs_2_ = bf16[2,4,32,896]{3,2,1,0:T(8,128)(2,1)S(1)} collective-permute-done((bf16[2,4,32,896]{3,2,1,0:T(8,128)(2,1)S(1)}, bf16[2,4,32,896]{3,2,1,0:T(8,128)(2,1)S(1)}, u32[]{:S(2)}, u32[]{:S(2)}) %collective-permute-start.9) | collective-permute-done | bytes 458784 | tf_op jit(solution)/shard_map/ppermute | solution.py:172
  73.1 0.6 collective-permute-start.15
  73.7 0.8 collective-permute-start.12
  74.6 1.3 collective-permute-start.13
  76.1 0.7 collective-permute-start.16
  76.8 0.2 pad_maximum_fusion.1.queries
  77.0 11.9 %collective-permute-done.13.refs_4_ = bf16[2,4,32,896]{3,2,1,0:T(8,128)(2,1)S(1)} collective-permute-done((bf16[2,4,32,896]{3,2,1,0:T(8,128)(2,1)S(1)}, bf16[2,4,32,896]{3,2,1,0:T(8,128)(2,1)S(1)}, u32[]{:S(2)}, u32[]{:S(2)}) %collective-permute-start.13) | collective-permute-done | bytes 458784 | tf_op jit(solution)/shard_map/ppermute | solution.py:172
  88.9 5.4 %encode.3 = (bf16[256,896]{1,0:T(8,128)(2,1)S(1)}, bf16[256,896]{1,0:T(8,128)(2,1)S(1)}) custom-call(s32[2]{0:T(128)S(1)} %pad_add_fusion.pos, bf16[2,4,32,896]{3,2,1,0:T(8,128)(2,1)S(1)} %pad_maximum_fusion.4.refs_0_, bf16[2,4,32,896]{3,2,1,0:T(8,128)(2,1)S(1)} %collective-permute-done.10.refs_1_, ...), custom_call_target="tpu_custom_call" | custom-call | flops 2013265920 | bytes 5505024 | tf_op jit(solution)/shard_map/encode/pallas_call | solution.py:293
  94.3 1.5 collective-permute-start.19
  95.8 0.7 collective-permute-start.21
  96.5 5.6 %encode.2 = (bf16[256,896]{1,0:T(8,128)(2,1)S(1)}, bf16[256,896]{1,0:T(8,128)(2,1)S(1)}, bf16[256,896]{1,0:T(8,128)(2,1)S(1)}) custom-call(s32[2]{0:T(128)S(1)} %pad_add_fusion.pos, bf16[2,4,32,896]{3,2,1,0:T(8,128)(2,1)S(1)} %pad_maximum_fusion.4.refs_0_, bf16[2,4,32,896]{3,2,1,0:T(8,128)(2,1)S(1)} %collective-permute-done.10.refs_1_, ...), custom_call_target="tpu_custom_call" | custom-call | flops 2013265920 | bytes 5505024 | tf_op jit(solution)/shard_map/encode/pallas_call | solution.py:293
  102.1 1.6 collective-permute-start.17
  103.7 2.9 %collective-permute-start.18 = (bf16[256,896]{1,0:T(8,128)(2,1)S(1)}, bf16[256,896]{1,0:T(8,128)(2,1)S(1)}, u32[]{:S(2)}, u32[]{:S(2)}) collective-permute-start(bf16[256,896]{1,0:T(8,128)(2,1)S(1)} %get-tuple-element.72), channel_id=1, source_target_pairs={{0,4},{1,5},{6,2},{7,3},{8,12},{9,13},{14,10},{15,11},{16,20},{17,... | collective-permute-start | bytes 1376264 | tf_op jit(solution)/shard_map/ppermute | solution.py:172
  106.8 1.3 collective-permute-start.20
  108.2 12.0 %collective-permute-done.17.refs_1_ = bf16[256,896]{1,0:T(8,128)(2,1)S(1)} collective-permute-done((bf16[256,896]{1,0:T(8,128)(2,1)S(1)}, bf16[256,896]{1,0:T(8,128)(2,1)S(1)}, u32[]{:S(2)}, u32[]{:S(2)}) %collective-permute-start.17) | collective-permute-done | bytes 458784 | tf_op jit(solution)/shard_map/ppermute | solution.py:172
  120.2 4.5 %collective-permute-done.18.refs_2_ = bf16[256,896]{1,0:T(8,128)(2,1)S(1)} collective-permute-done((bf16[256,896]{1,0:T(8,128)(2,1)S(1)}, bf16[256,896]{1,0:T(8,128)(2,1)S(1)}, u32[]{:S(2)}, u32[]{:S(2)}) %collective-permute-start.18) | collective-permute-done | bytes 458784 | tf_op jit(solution)/shard_map/ppermute | solution.py:172
  124.7 5.6 %collective-permute-done.20.refs_3_ = bf16[256,896]{1,0:T(8,128)(2,1)S(1)} collective-permute-done((bf16[256,896]{1,0:T(8,128)(2,1)S(1)}, bf16[256,896]{1,0:T(8,128)(2,1)S(1)}, u32[]{:S(2)}, u32[]{:S(2)}) %collective-permute-start.20) | collective-permute-done | bytes 458784 | tf_op jit(solution)/shard_map/ppermute | solution.py:172
  130.3 0.5 normed.1.rows
  130.9 2.5 %collective-permute-start.25 = (bf16[256,896]{1,0:T(8,128)(2,1)S(1)}, bf16[256,896]{1,0:T(8,128)(2,1)}, u32[]{:S(2)}, u32[]{:S(2)}) collective-permute-start(bf16[256,896]{1,0:T(8,128)(2,1)S(1)} %normed.1.rows), channel_id=1, source_target_pairs={{0,2},{1,3},{2,0},{3,1},{4,6},{5,7},{6,4},{7,5},{8,10},{9,11},{10,... | collective-permute-start | bytes 1376264 | tf_op jit(solution)/shard_map/ppermute | solution.py:172
  133.6 0.2 dynamic-slice_reduce_fusion.counts
  133.8 4.8 %attend.2.first = bf16[64,1024]{1,0:T(8,128)(2,1)S(1)} custom-call(s32[2]{0:T(128)S(1)} %pad_add_fusion.pos, s32[4]{0:T(128)S(1)} %dynamic-slice_reduce_fusion.counts, bf16[256,896]{1,0:T(8,128)(2,1)S(1)} %normed.1.rows, bf16[896,1024]{1,0:T(8,128)(2,1)S(1)} %bitcast.35, bf16[896,1024]{1,0:T(8,128)(2,1)} %collective-permute-done.6.other_kv, ...), custom_call_target="tpu_custom_call" | custom-call | flops 1006632960 | bytes 4128768 | tf_op jit(solution)/shard_map/attend/pallas_call | solution.py:366
  138.6 12.6 %collective-permute-done.22.two = bf16[256,896]{1,0:T(8,128)(2,1)} collective-permute-done((bf16[256,896]{1,0:T(8,128)(2,1)S(1)}, bf16[256,896]{1,0:T(8,128)(2,1)}, u32[]{:S(2)}, u32[]{:S(2)}) %collective-permute-start.22) | collective-permute-done | bytes 458784 | tf_op jit(solution)/shard_map/ppermute | solution.py:172
  151.2 1.4 collective-permute-start.23
  152.6 1.3 collective-permute-start.24
  153.9 8.3 %attend.3.refs_0_ = bf16[4,64,1024]{2,1,0:T(8,128)(2,1)S(1)} custom-call(s32[2]{0:T(128)S(1)} %pad_add_fusion.pos, s32[4]{0:T(128)S(1)} %dynamic-slice_reduce_fusion.counts, bf16[256,896]{1,0:T(8,128)(2,1)} %collective-permute-done.25.one, bf16[256,896]{1,0:T(8,128)(2,1)} %collective-permute-done.22.two, bf16[896,1024]{1,0:T(8,128)(2,1)S(1)} %bitcast.36, ...), custom_call_target="tpu_custom_call" | custom-call | flops 2013265920 | bytes 4587520 | tf_op jit(solution)/shard_map/attend/pallas_call | solution.py:366
  162.2 0.7 slice_bitcast_fusion
  162.9 0.8 copy-done.4
  163.6 0.9 collective-permute-start.26
  164.6 2.6 %collective-permute-done.24.far = bf16[256,896]{1,0:T(8,128)(2,1)} collective-permute-done((bf16[256,896]{1,0:T(8,128)(2,1)}, bf16[256,896]{1,0:T(8,128)(2,1)}, u32[]{:S(2)}, u32[]{:S(2)}) %collective-permute-start.24) | collective-permute-done | bytes 458784 | tf_op jit(solution)/shard_map/ppermute | solution.py:172
  167.2 1.0 copy-done.5
  168.2 8.6 %last_attend.1 = (bf16[64,4096]{1,0:T(8,128)(2,1)S(1)}, bf16[64,4096]{1,0:T(8,128)(2,1)S(1)}, bf16[64,4096]{1,0:T(8,128)(2,1)S(1)}, bf16[64,4096]{1,0:T(8,128)(2,1)S(1)}, bf16[64,1024]{1,0:T(8,128)(2,1)S(1)}) custom-call(s32[2]{0:T(128)S(1)} %pad_add_fusion.pos, s32[4]{0:T(128)S(1)} %dynamic-slice_reduce_fusion.counts, ...), custom_call_target="tpu_custom_call" | custom-call | flops 3154116608 | bytes 10485760 | tf_op jit(solution)/shard_map/last_attend/pallas_call | solution.py:426
  176.9 2.7 %collective-permute-start.29 = (bf16[64,4096]{1,0:T(8,128)(2,1)S(1)}, bf16[64,4096]{1,0:T(8,128)(2,1)S(1)}, u32[]{:S(2)}, u32[]{:S(2)}) collective-permute-start(bf16[64,4096]{1,0:T(8,128)(2,1)S(1)} %get-tuple-element.86), channel_id=1, source_target_pairs={{0,2},{1,3},{6,4},{7,5},{8,10},{9,11},{14,12},{15,13},{16,18},{17,... | collective-permute-start | bytes 1572872 | tf_op jit(solution)/shard_map/ppermute | solution.py:172
  179.6 0.7 collective-permute-start.31
  180.3 4.0 %collective-permute-start.28 = (bf16[64,4096]{1,0:T(8,128)(2,1)S(1)}, bf16[64,4096]{1,0:T(8,128)(2,1)S(1)}, u32[]{:S(2)}, u32[]{:S(2)}) collective-permute-start(bf16[64,4096]{1,0:T(8,128)(2,1)S(1)} %get-tuple-element.85), channel_id=1, source_target_pairs={{0,4},{1,5},{6,2},{7,3},{8,12},{9,13},{14,10},{15,11},{16,20},{17,... | collective-permute-start | bytes 1572872 | tf_op jit(solution)/shard_map/ppermute | solution.py:172
  184.4 4.3 %collective-permute-done.29 = bf16[64,4096]{1,0:T(8,128)(2,1)S(1)} collective-permute-done((bf16[64,4096]{1,0:T(8,128)(2,1)S(1)}, bf16[64,4096]{1,0:T(8,128)(2,1)S(1)}, u32[]{:S(2)}, u32[]{:S(2)}) %collective-permute-start.29) | collective-permute-done | bytes 524320 | tf_op jit(solution)/shard_map/ppermute | solution.py:172
  188.8 1.3 collective-permute-start.30
  190.1 0.7 collective-permute-start.32
  190.8 3.4 %late_out.1 = bf16[64,4096]{1,0:T(8,128)(2,1)S(1)} custom-call(bf16[64,1024]{1,0:T(8,128)(2,1)S(1)} %broadcast_select_fusion.before, bf16[512,4096]{1,0:T(8,128)(2,1)S(1)} %copy-done.1, bf16[512,4096]{1,0:T(8,128)(2,1)} %collective-permute-done.7.refs_3_.other_w), custom_call_target="tpu_custom_call" | custom-call | flops 536870912 | bytes 8388608 | tf_op jit(solution)/shard_map/late_out/pallas_call | solution.py:462
  194.3 5.7 %collective-permute-done.28 = bf16[64,4096]{1,0:T(8,128)(2,1)S(1)} collective-permute-done((bf16[64,4096]{1,0:T(8,128)(2,1)S(1)}, bf16[64,4096]{1,0:T(8,128)(2,1)S(1)}, u32[]{:S(2)}, u32[]{:S(2)}) %collective-permute-start.28) | collective-permute-done | bytes 524320 | tf_op jit(solution)/shard_map/ppermute | solution.py:172
  200.0 11.2 %collective-permute-done.27 = bf16[64,4096]{1,0:T(8,128)(2,1)S(1)} collective-permute-done((bf16[64,4096]{1,0:T(8,128)(2,1)S(1)}, bf16[64,4096]{1,0:T(8,128)(2,1)S(1)}, u32[]{:S(2)}, u32[]{:S(2)}) %collective-permute-start.27) | collective-permute-done | bytes 524320 | tf_op jit(solution)/shard_map/ppermute | solution.py:172
  211.2 4.3 %collective-permute-done.30 = bf16[64,4096]{1,0:T(8,128)(2,1)S(1)} collective-permute-done((bf16[64,4096]{1,0:T(8,128)(2,1)S(1)}, bf16[64,4096]{1,0:T(8,128)(2,1)S(1)}, u32[]{:S(2)}, u32[]{:S(2)}) %collective-permute-start.30) | collective-permute-done | bytes 524320 | tf_op jit(solution)/shard_map/ppermute | solution.py:172
  215.5 0.4 add_convert_fusion
  216.0 1.9 collective-permute-start.33
  218.0 0.8 copy.17
  218.8 0.6 collective-permute-done.33
  219.6 0.8 pad_maximum_fusion.3
  (70 shorter events, 2.3 us)
Async XLA Ops:
  0.6 6.7 %copy-start = (bf16[16,16,896]{2,1,0:T(8,128)(2,1)S(1)}, bf16[16,16,896]{2,1,0:T(8,128)(2,1)}, u32[]{:S(2)}) copy-start(bf16[16,16,896]{2,1,0:T(8,128)(2,1)} %param.11) | copy-start | bytes 1376260
  0.6 27.7 %collective-permute-start = (bf16[64,4096]{1,0:T(8,128)(2,1)}, bf16[64,4096]{1,0:T(8,128)(2,1)}, u32[]{:S(2)}, u32[]{:S(2)}) collective-permute-start(bf16[64,4096]{1,0:T(8,128)(2,1)} %param.10), channel_id=1, source_target_pairs={{0,4},{1,5},{2,6},{3,7},{4,0},{5,1},{6,2},{7,3},{8,12},{9,13},{10,... | collective-permute-start | bytes 1572872 | tf_op jit(solution)/shard_map/ppermute | solution.py:172
  4.7 23.7 %collective-permute-start.1 = (bf16[64,4096]{1,0:T(8,128)(2,1)}, bf16[64,4096]{1,0:T(8,128)(2,1)S(1)}, u32[]{:S(2)}, u32[]{:S(2)}) collective-permute-start(bf16[64,4096]{1,0:T(8,128)(2,1)} %param.10), channel_id=1, source_target_pairs={{0,2},{1,3},{2,0},{3,1},{4,6},{5,7},{6,4},{7,5},{8,10},{9,11},{10,... | collective-permute-start | bytes 1572872 | tf_op jit(solution)/shard_map/ppermute | solution.py:172
  8.0 1.6 collective-permute-start.2
  28.4 2.0 copy-start.6
  28.4 20.6 %collective-permute-start.7 = (bf16[512,4096]{1,0:T(8,128)(2,1)}, bf16[512,4096]{1,0:T(8,128)(2,1)}, u32[]{:S(2)}, u32[]{:S(2)}) collective-permute-start(bf16[512,4096]{1,0:T(8,128)(2,1)} %own_w), channel_id=1, source_target_pairs={{0,1},{1,0},{2,3},{3,2},{4,5},{5,4},{6,7},{7,6},{8,9},{9,8},{10,11... | collective-permute-start | bytes 12582920 | tf_op jit(solution)/shard_map/ppermute | solution.py:165
  28.4 4.7 %collective-permute-start.3 = (bf16[64,4096]{1,0:T(8,128)(2,1)}, bf16[64,4096]{1,0:T(8,128)(2,1)S(1)}, u32[]{:S(2)}, u32[]{:S(2)}) collective-permute-start(bf16[64,4096]{1,0:T(8,128)(2,1)} %param.10), channel_id=1, source_target_pairs={{2,4},{3,5},{4,2},{5,3},{10,12},{11,13},{12,10},{13,11},{18,20},{1... | collective-permute-start | bytes 1572872 | tf_op jit(solution)/shard_map/ppermute | solution.py:172
  29.1 17.1 %collective-permute-start.4 = (bf16[64,4096]{1,0:T(8,128)(2,1)}, bf16[64,4096]{1,0:T(8,128)(2,1)}, u32[]{:S(2)}, u32[]{:S(2)}) collective-permute-start(bf16[64,4096]{1,0:T(8,128)(2,1)} %collective-permute-done), channel_id=1, source_target_pairs={{2,0},{3,1},{4,6},{5,7},{10,8},{11,9},{12,14},{13,15},{18,16},{19,... | collective-permute-start | bytes 1572872 | tf_op jit(solution)/shard_map/ppermute | solution.py:172
  32.4 16.6 %collective-permute-start.6 = (bf16[896,1024]{1,0:T(8,128)(2,1)S(1)}, bf16[896,1024]{1,0:T(8,128)(2,1)}, u32[]{:S(2)}, u32[]{:S(2)}) collective-permute-start(bf16[896,1024]{1,0:T(8,128)(2,1)S(1)} %bitcast.34), channel_id=1, source_target_pairs={{0,1},{1,0},{2,3},{3,2},{4,5},{5,4},{6,7},{7,6},{8,9},{9,8},{10,11... | collective-permute-start | bytes 5505032 | tf_op jit(solution)/shard_map/ppermute | solution.py:165
  33.0 16.0 %collective-permute-start.5 = (bf16[512,896]{1,0:T(8,128)(2,1)}, bf16[512,896]{1,0:T(8,128)(2,1)S(1)}, u32[]{:S(2)}, u32[]{:S(2)}) collective-permute-start(bf16[512,896]{1,0:T(8,128)(2,1)} %refs_8_.1), channel_id=1, source_target_pairs={{0,1},{1,0},{2,3},{3,2},{4,5},{5,4},{6,7},{7,6},{8,9},{9,8},{10,11... | collective-permute-start | bytes 2752520 | tf_op jit(solution)/shard_map/ppermute | solution.py:165
  47.3 1.8 copy-start.2
  49.0 4.2 %collective-permute-start.8 = (bf16[4,64,4096]{2,1,0:T(8,128)(2,1)S(1)}, bf16[4,64,4096]{2,1,0:T(8,128)(2,1)S(1)}, u32[]{:S(2)}, u32[]{:S(2)}) collective-permute-start(bf16[4,64,4096]{2,1,0:T(8,128)(2,1)S(1)} %pad_maximum_fusion.own), channel_id=1, source_target_pairs={{0,1},{1,0},{2,3},{3,2},{4,5},{5,4},{6,7},{7,6},{8,9},{9,8},{10,11... | collective-permute-start | bytes 6291464 | tf_op jit(solution)/shard_map/ppermute | solution.py:165
  49.1 24.0 %collective-permute-start.11 = (bf16[896,512]{1,0:T(8,128)(2,1)S(1)}, bf16[896,512]{1,0:T(8,128)(2,1)S(1)}, u32[]{:S(2)}, u32[]{:S(2)}) collective-permute-start(bf16[896,512]{1,0:T(8,128)(2,1)S(1)} %copy-done.2), channel_id=1, source_target_pairs={{0,1},{1,0},{2,3},{3,2},{4,5},{5,4},{6,7},{7,6},{8,9},{9,8},{10,11... | collective-permute-start | bytes 2752520 | tf_op jit(solution)/shard_map/ppermute | solution.py:165
  49.7 23.3 %collective-permute-start.9 = (bf16[2,4,32,896]{3,2,1,0:T(8,128)(2,1)S(1)}, bf16[2,4,32,896]{3,2,1,0:T(8,128)(2,1)S(1)}, u32[]{:S(2)}, u32[]{:S(2)}) collective-permute-start(bf16[2,4,32,896]{3,2,1,0:T(8,128)(2,1)S(1)} %pad_maximum_fusion.4.refs_0_), channel_id=1, source_target_pairs={{0,4},{1,5},{2,6},{3,7},{4,0},{5,1},{6,2},{7,3},{8,12},{9,13},{10,... | collective-permute-start | bytes 1376264 | tf_op jit(solution)/shard_map/ppermute | solution.py:172
  49.7 23.4 %collective-permute-start.10 = (bf16[2,4,32,896]{3,2,1,0:T(8,128)(2,1)S(1)}, bf16[2,4,32,896]{3,2,1,0:T(8,128)(2,1)S(1)}, u32[]{:S(2)}, u32[]{:S(2)}) collective-permute-start(bf16[2,4,32,896]{3,2,1,0:T(8,128)(2,1)S(1)} %pad_maximum_fusion.4.refs_0_), channel_id=1, source_target_pairs={{0,2},{1,3},{2,0},{3,1},{4,6},{5,7},{6,4},{7,5},{8,10},{9,11},{10,... | collective-permute-start | bytes 1376264 | tf_op jit(solution)/shard_map/ppermute | solution.py:172
  73.1 2.9 %collective-permute-start.14 = (bf16[4,64,1536]{2,1,0:T(8,128)(2,1)S(1)}, bf16[4,64,1536]{2,1,0:T(8,128)(2,1)S(1)}, u32[]{:S(2)}, u32[]{:S(2)}) collective-permute-start(bf16[4,64,1536]{2,1,0:T(8,128)(2,1)S(1)} %get-tuple-element.60), channel_id=1, source_target_pairs={{0,1},{1,0},{2,3},{3,2},{4,5},{5,4},{6,7},{7,6},{8,9},{9,8},{10,11... | collective-permute-start | bytes 2359304 | tf_op jit(solution)/shard_map/ppermute | solution.py:165
  73.1 2.8 %collective-permute-start.15 = (bf16[4,64,512]{2,1,0:T(8,128)(2,1)S(1)}, bf16[4,64,512]{2,1,0:T(8,128)(2,1)S(1)}, u32[]{:S(2)}, u32[]{:S(2)}) collective-permute-start(bf16[4,64,512]{2,1,0:T(8,128)(2,1)S(1)} %slice.38), channel_id=1, source_target_pairs={{0,1},{1,0},{2,3},{3,2},{4,5},{5,4},{6,7},{7,6},{8,9},{9,8},{10,11... | collective-permute-start | bytes 786440 | tf_op jit(solution)/shard_map/ppermute | solution.py:165
  73.7 15.2 %copy-start.3 = (bf16[512,896]{1,0:T(8,128)(2,1)S(1)}, bf16[512,896]{1,0:T(8,128)(2,1)}, u32[]{:S(2)}) copy-start(bf16[512,896]{1,0:T(8,128)(2,1)} %refs_8_.1) | copy-start | bytes 2752516
  73.7 3.2 %collective-permute-start.12 = (bf16[2,4,32,896]{3,2,1,0:T(8,128)(2,1)S(1)}, bf16[2,4,32,896]{3,2,1,0:T(8,128)(2,1)S(1)}, u32[]{:S(2)}, u32[]{:S(2)}) collective-permute-start(bf16[2,4,32,896]{3,2,1,0:T(8,128)(2,1)S(1)} %pad_maximum_fusion.4.refs_0_), channel_id=1, source_target_pairs={{2,4},{3,5},{4,2},{5,3},{10,12},{11,13},{12,10},{13,11},{18,20},{1... | collective-permute-start | bytes 1376264 | tf_op jit(solution)/shard_map/ppermute | solution.py:172
  74.6 14.3 %collective-permute-start.13 = (bf16[2,4,32,896]{3,2,1,0:T(8,128)(2,1)S(1)}, bf16[2,4,32,896]{3,2,1,0:T(8,128)(2,1)S(1)}, u32[]{:S(2)}, u32[]{:S(2)}) collective-permute-start(bf16[2,4,32,896]{3,2,1,0:T(8,128)(2,1)S(1)} %collective-permute-done.9.refs_2_), channel_id=1, source_target_pairs={{2,0},{3,1},{4,6},{5,7},{10,8},{11,9},{12,14},{13,15},{18,16},{19,... | collective-permute-start | bytes 1376264 | tf_op jit(solution)/shard_map/ppermute | solution.py:172
  76.1 0.7 collective-permute-start.16
  94.3 13.8 %copy-start.7 = (f32[896]{0:T(1024)S(1)}, f32[896]{0:T(1024)}, u32[]{:S(2)}) copy-start(f32[896]{0:T(1024)} %param.17) | copy-start | bytes 10756
  94.3 12.4 %collective-permute-start.19 = (bf16[256,896]{1,0:T(8,128)(2,1)S(1)}, bf16[256,896]{1,0:T(8,128)(2,1)S(1)}, u32[]{:S(2)}, u32[]{:S(2)}) collective-permute-start(bf16[256,896]{1,0:T(8,128)(2,1)S(1)} %get-tuple-element.73), channel_id=1, source_target_pairs={{0,2},{1,3},{6,4},{7,5},{8,10},{9,11},{14,12},{15,13},{16,18},{17,... | collective-permute-start | bytes 1376264 | tf_op jit(solution)/shard_map/ppermute | solution.py:172
  95.8 28.9 %collective-permute-start.21 = (bf16[256,896]{1,0:T(8,128)(2,1)S(1)}, bf16[256,896]{1,0:T(8,128)(2,1)S(1)}, u32[]{:S(2)}, u32[]{:S(2)}) collective-permute-start(bf16[256,896]{1,0:T(8,128)(2,1)S(1)} %get-tuple-element.73), channel_id=1, source_target_pairs={{2,4},{3,5},{4,2},{5,3},{10,12},{11,13},{12,10},{13,11},{18,20},{1... | collective-permute-start | bytes 1376264 | tf_op jit(solution)/shard_map/ppermute | solution.py:172
  102.1 18.1 %collective-permute-start.17 = (bf16[256,896]{1,0:T(8,128)(2,1)S(1)}, bf16[256,896]{1,0:T(8,128)(2,1)S(1)}, u32[]{:S(2)}, u32[]{:S(2)}) collective-permute-start(bf16[256,896]{1,0:T(8,128)(2,1)S(1)} %get-tuple-element.71), channel_id=1, source_target_pairs={{0,2},{1,3},{2,0},{3,1},{4,6},{5,7},{6,4},{7,5},{8,10},{9,11},{10,... | collective-permute-start | bytes 1376264 | tf_op jit(solution)/shard_map/ppermute | solution.py:172
  103.7 29.8 %copy-start.8 = (s32[32]{0:T(128)S(1)}, s32[32]{0:T(128)}, u32[]{:S(2)}) copy-start(s32[32]{0:T(128)} %param.13) | copy-start | bytes 388
  103.7 21.0 %collective-permute-start.18 = (bf16[256,896]{1,0:T(8,128)(2,1)S(1)}, bf16[256,896]{1,0:T(8,128)(2,1)S(1)}, u32[]{:S(2)}, u32[]{:S(2)}) collective-permute-start(bf16[256,896]{1,0:T(8,128)(2,1)S(1)} %get-tuple-element.72), channel_id=1, source_target_pairs={{0,4},{1,5},{6,2},{7,3},{8,12},{9,13},{14,10},{15,11},{16,20},{17,... | collective-permute-start | bytes 1376264 | tf_op jit(solution)/shard_map/ppermute | solution.py:172
  106.8 23.4 %collective-permute-start.20 = (bf16[256,896]{1,0:T(8,128)(2,1)S(1)}, bf16[256,896]{1,0:T(8,128)(2,1)S(1)}, u32[]{:S(2)}, u32[]{:S(2)}) collective-permute-start(bf16[256,896]{1,0:T(8,128)(2,1)S(1)} %add_convert_fusion.2), channel_id=1, source_target_pairs={{2,6},{3,7},{4,0},{5,1},{10,14},{11,15},{12,8},{13,9},{18,22},{19,... | collective-permute-start | bytes 1376264 | tf_op jit(solution)/shard_map/ppermute | solution.py:172
  130.8 20.4 %collective-permute-start.22 = (bf16[256,896]{1,0:T(8,128)(2,1)S(1)}, bf16[256,896]{1,0:T(8,128)(2,1)}, u32[]{:S(2)}, u32[]{:S(2)}) collective-permute-start(bf16[256,896]{1,0:T(8,128)(2,1)S(1)} %normed.1.rows), channel_id=1, source_target_pairs={{0,4},{1,5},{2,6},{3,7},{4,0},{5,1},{6,2},{7,3},{8,12},{9,13},{10,... | collective-permute-start | bytes 1376264 | tf_op jit(solution)/shard_map/ppermute | solution.py:172
  130.9 23.0 %collective-permute-start.25 = (bf16[256,896]{1,0:T(8,128)(2,1)S(1)}, bf16[256,896]{1,0:T(8,128)(2,1)}, u32[]{:S(2)}, u32[]{:S(2)}) collective-permute-start(bf16[256,896]{1,0:T(8,128)(2,1)S(1)} %normed.1.rows), channel_id=1, source_target_pairs={{0,2},{1,3},{2,0},{3,1},{4,6},{5,7},{6,4},{7,5},{8,10},{9,11},{10,... | collective-permute-start | bytes 1376264 | tf_op jit(solution)/shard_map/ppermute | solution.py:172
  151.2 13.4 %collective-permute-start.23 = (bf16[256,896]{1,0:T(8,128)(2,1)S(1)}, bf16[256,896]{1,0:T(8,128)(2,1)}, u32[]{:S(2)}, u32[]{:S(2)}) collective-permute-start(bf16[256,896]{1,0:T(8,128)(2,1)S(1)} %normed.1.rows), channel_id=1, source_target_pairs={{2,4},{3,5},{4,2},{5,3},{10,12},{11,13},{12,10},{13,11},{18,20},{1... | collective-permute-start | bytes 1376264 | tf_op jit(solution)/shard_map/ppermute | solution.py:172
  152.6 14.6 %collective-permute-start.24 = (bf16[256,896]{1,0:T(8,128)(2,1)}, bf16[256,896]{1,0:T(8,128)(2,1)}, u32[]{:S(2)}, u32[]{:S(2)}) collective-permute-start(bf16[256,896]{1,0:T(8,128)(2,1)} %collective-permute-done.22.two), channel_id=1, source_target_pairs={{2,0},{3,1},{4,6},{5,7},{10,8},{11,9},{12,14},{13,15},{18,16},{19,... | collective-permute-start | bytes 1376264 | tf_op jit(solution)/shard_map/ppermute | solution.py:172
  162.8 0.8 copy-start.4
  163.6 0.9 collective-permute-start.26
  167.2 1.0 copy-start.5
  168.2 22.6 %copy-start.1 = (bf16[512,4096]{1,0:T(8,128)(2,1)S(1)}, bf16[512,4096]{1,0:T(8,128)(2,1)}, u32[]{:S(2)}) copy-start(bf16[512,4096]{1,0:T(8,128)(2,1)} %own_w) | copy-start | bytes 12582916
  176.9 11.8 %collective-permute-start.29 = (bf16[64,4096]{1,0:T(8,128)(2,1)S(1)}, bf16[64,4096]{1,0:T(8,128)(2,1)S(1)}, u32[]{:S(2)}, u32[]{:S(2)}) collective-permute-start(bf16[64,4096]{1,0:T(8,128)(2,1)S(1)} %get-tuple-element.86), channel_id=1, source_target_pairs={{0,2},{1,3},{6,4},{7,5},{8,10},{9,11},{14,12},{15,13},{16,18},{17,... | collective-permute-start | bytes 1572872 | tf_op jit(solution)/shard_map/ppermute | solution.py:172
  179.6 14.6 %collective-permute-start.31 = (bf16[64,4096]{1,0:T(8,128)(2,1)S(1)}, bf16[64,4096]{1,0:T(8,128)(2,1)S(1)}, u32[]{:S(2)}, u32[]{:S(2)}) collective-permute-start(bf16[64,4096]{1,0:T(8,128)(2,1)S(1)} %get-tuple-element.86), channel_id=1, source_target_pairs={{2,4},{3,5},{4,2},{5,3},{10,12},{11,13},{12,10},{13,11},{18,20},{1... | collective-permute-start | bytes 1572872 | tf_op jit(solution)/shard_map/ppermute | solution.py:172
  180.3 19.7 %collective-permute-start.28 = (bf16[64,4096]{1,0:T(8,128)(2,1)S(1)}, bf16[64,4096]{1,0:T(8,128)(2,1)S(1)}, u32[]{:S(2)}, u32[]{:S(2)}) collective-permute-start(bf16[64,4096]{1,0:T(8,128)(2,1)S(1)} %get-tuple-element.85), channel_id=1, source_target_pairs={{0,4},{1,5},{6,2},{7,3},{8,12},{9,13},{14,10},{15,11},{16,20},{17,... | collective-permute-start | bytes 1572872 | tf_op jit(solution)/shard_map/ppermute | solution.py:172
  184.3 26.9 %collective-permute-start.27 = (bf16[64,4096]{1,0:T(8,128)(2,1)S(1)}, bf16[64,4096]{1,0:T(8,128)(2,1)S(1)}, u32[]{:S(2)}, u32[]{:S(2)}) collective-permute-start(bf16[64,4096]{1,0:T(8,128)(2,1)S(1)} %get-tuple-element.84), channel_id=1, source_target_pairs={{0,2},{1,3},{2,0},{3,1},{4,6},{5,7},{6,4},{7,5},{8,10},{9,11},{10,... | collective-permute-start | bytes 1572872 | tf_op jit(solution)/shard_map/ppermute | solution.py:172
  188.8 26.7 %collective-permute-start.30 = (bf16[64,4096]{1,0:T(8,128)(2,1)S(1)}, bf16[64,4096]{1,0:T(8,128)(2,1)S(1)}, u32[]{:S(2)}, u32[]{:S(2)}) collective-permute-start(bf16[64,4096]{1,0:T(8,128)(2,1)S(1)} %add_convert_fusion.1), channel_id=1, source_target_pairs={{2,6},{3,7},{4,0},{5,1},{10,14},{11,15},{12,8},{13,9},{18,22},{19,... | collective-permute-start | bytes 1572872 | tf_op jit(solution)/shard_map/ppermute | solution.py:172
  190.1 0.7 collective-permute-start.32
  216.0 3.4 %collective-permute-start.33 = (bf16[64,4096]{1,0:T(8,128)(2,1)S(1)}, bf16[64,4096]{1,0:T(8,128)(2,1)S(1)}, u32[]{:S(2)}, u32[]{:S(2)}) collective-permute-start(bf16[64,4096]{1,0:T(8,128)(2,1)S(1)} %add_convert_fusion), channel_id=1, source_target_pairs={{0,1},{1,0},{2,3},{3,2},{4,5},{5,4},{6,7},{7,6},{8,9},{9,8},{10,11... | collective-permute-start | bytes 1572872 | tf_op jit(solution)/shard_map/ppermute | solution.py:165

commit v4 on v3

--- a/solution.py
+++ b/solution.py
@@ -261,19 +261,23 @@
     if flips[-1] == 0:
         refs[n][...] = x[(n - 1) * each_rows :]
     heads = weights[0][0].shape[1]
-    for w, (wq, keys, values, _) in enumerate(weights):
-        q = dot(x, wq[...]).astype(BF16)
-        for k, flip in enumerate(flips):
-            here = pl.ds(pl.multiple_of((pos[0] ^ flip) * GROUP, GROUP), GROUP)
-            mine = pl.ds(k * each_rows, each_rows)
-            for h in range(0, heads, HEAD_DIM):
-                cols = pl.ds(h, HEAD_DIM)
-                scores = dot_t(keys[here, cols], q[k * each_rows : (k + 1) * each_rows, h : h + HEAD_DIM]) * SCALE
-                raised = jnp.exp(scores - jnp.max(scores, axis=0, keepdims=True))
-                share = (raised / jnp.sum(raised, axis=0, keepdims=True)).astype(BF16)
-                att[mine, pl.ds(w * heads + h, HEAD_DIM)] = lax.dot_general(
-                    share, values[here, cols], (((0,), (0,)), ((), ())), preferred_element_type=F32
-                ).astype(BF16)
+    qs = [dot(x, wq[...]).astype(BF16) for wq, *_ in weights]
+    chains = [(w, k, h) for w in range(2) for k in range(n) for h in range(0, heads, HEAD_DIM)]
+    here = [pl.ds(pl.multiple_of((pos[0] ^ flip) * GROUP, GROUP), GROUP) for flip in flips]
+    scores = []
+    for w, k, h in chains:
+        ask = qs[w][k * each_rows : (k + 1) * each_rows, h : h + HEAD_DIM]
+        scores.append(dot_t(weights[w][1][here[k], pl.ds(h, HEAD_DIM)], ask)[None])
+    scores = jnp.concatenate(scores, axis=0) * SCALE
+    raised = jnp.exp(scores - jnp.max(scores, axis=1, keepdims=True))
+    share = (raised / jnp.sum(raised, axis=1, keepdims=True)).astype(BF16)
+    for c, (w, k, h) in enumerate(chains):
+        att[pl.ds(k * each_rows, each_rows), pl.ds(w * heads + h, HEAD_DIM)] = lax.dot_general(
+            share[c],
+            weights[w][2][here[k], pl.ds(h, HEAD_DIM)],
+            (((0,), (0,)), ((), ())),
+            preferred_element_type=F32,
+        ).astype(BF16)
     total = dot(att[:, pl.ds(0, heads)], weights[0][3][...]) + dot(att[:, pl.ds(heads, heads)], weights[1][3][...])
     for k, out in enumerate(outs):
         out[...] = total[k * each_rows : (k + 1) * each_rows].astype(BF16)
@@ -335,15 +339,19 @@
     first = lax.broadcasted_iota(jnp.int32, (GROUP, 2 * heads), 0) == 0
     allowed = slot < counts[i]
     q = jnp.where(first, queries[i], queries[i + core])
-    for w, wkv in enumerate(wkvs):
-        kv = dot(x, wkv[...]).astype(BF16)
-        for h in range(0, heads, HEAD_DIM):
-            at = heads * w + h
-            scores = dot_t(q[:, at : at + HEAD_DIM], kv[:, h : h + HEAD_DIM]) * SCALE
-            scores = jnp.where(allowed, scores, -1e30)
-            raised = jnp.where(allowed, jnp.exp(scores - jnp.max(scores, axis=-1, keepdims=True)), 0.0)
-            share = (raised / jnp.sum(raised, axis=-1, keepdims=True)).astype(BF16)
-            out[:, pl.ds(at, HEAD_DIM)] = dot(share, kv[:, heads + h : heads + h + HEAD_DIM]).astype(BF16)
+    kvs = [dot(x, wkv[...]).astype(BF16) for wkv in wkvs]
+    each_head = [(w, h) for w in range(2) for h in range(0, heads, HEAD_DIM)]
+    scores = [
+        dot_t(q[:, heads * w + h : heads * w + h + HEAD_DIM], kvs[w][:, h : h + HEAD_DIM]) for w, h in each_head
+    ]
+    scores = jnp.concatenate(scores, axis=0) * SCALE
+    allowed = jnp.concatenate([allowed] * len(each_head), axis=0)
+    scores = jnp.where(allowed, scores, -1e30)
+    raised = jnp.where(allowed, jnp.exp(scores - jnp.max(scores, axis=-1, keepdims=True)), 0.0)
+    share = (raised / jnp.sum(raised, axis=-1, keepdims=True)).astype(BF16)
+    for k, (w, h) in enumerate(each_head):
+        value = kvs[w][:, heads + h : heads + h + HEAD_DIM]
+        out[:, pl.ds(heads * w + h, HEAD_DIM)] = dot(share[k * GROUP : (k + 1) * GROUP], value).astype(BF16)
 
 
 def attend_kernel(pos, counts, rows, own_kv, other_kv, queries, out):

time: 221 us -> 209 us (0.946)
  Pallas kernels: 46.3 us -> 39.7 us
  waiting for transfers between devices: 118 us -> 114 us
    ppermute x22, waiting for transfers between devices: 117 us -> 112 us  [hop(): lax.ppermute(x, 'nbr', [(2 * z + c, 2 * (z ^ flip) + c) for z in chips fo...]
    pallas_call x2, Pallas kernels: 13.1 us -> 8.39 us  [attend(): pl.pallas_call(attend_more_kernel if earlier else attend_kernel, in_specs...]
  transfers between devices with their start and end apart: 34 -> 34, of which waited for: 19 -> 19; matrix products, arithmetic and copies ran while one was open for 4% -> 5% of each run, Pallas kernels for 14% -> 13%
where the time goes in v4:
time: 209 us; the launch traced here: 208 us
  waiting for transfers between devices  114 us (55%)
  starting transfers between devices  40.1 us (19%)
  Pallas kernels  39.7 us (19%)
  local copies, waits for them, and re-layouts  7.64 us (4%)
  other arithmetic  5.49 us (3%)
    ppermute x22, waiting for transfers between devices, hop(): lax.ppermute(x, 'nbr', [(2 * z + c, 2 * (z ^ flip) + c) for z in chips fo...  112 us
    ppermute x22, starting transfers between devices, hop(): lax.ppermute(x, 'nbr', [(2 * z + c, 2 * (z ^ flip) + c) for z in chips fo...  36.2 us
    pallas_call x2, Pallas kernels, encode(): pl.pallas_call(functools.partial(enc_kernel, flips), grid=(1,), in_specs=...  10.1 us
    pallas_call x1, Pallas kernels, project(): pl.pallas_call(proj_kernel, in_specs=[SMEM, VMEM, VMEM, HBM], out_specs=[...  9.73 us
    pallas_call x2, Pallas kernels, attend(): pl.pallas_call(attend_more_kernel if earlier else attend_kernel, in_specs...  8.39 us
    pallas_call x1, Pallas kernels, last_attend(): pl.pallas_call(last_kernel, in_specs=[SMEM, SMEM] + [VMEM] * 7 + [HBM, AN...  7.55 us
  transfers between devices with their start and end apart: 34, of which 19 were waited for; matrix products, arithmetic and copies ran while one was open for 5% of the time, Pallas kernels for 13%

profile of v4, /device:TPU:0, one launch (start us, length us, event | category | flops | bytes accessed | tf_op | source)
XLA Modules:
  0.0 207.9 jit_solution(664839029427267873)
XLA Ops:
  0.6 4.1 %collective-permute-start = (bf16[64,4096]{1,0:T(8,128)(2,1)}, bf16[64,4096]{1,0:T(8,128)(2,1)}, u32[]{:S(2)}, u32[]{:S(2)}) collective-permute-start(bf16[64,4096]{1,0:T(8,128)(2,1)} %param.10), channel_id=1, source_target_pairs={{0,4},{1,5},{2,6},{3,7},{4,0},{5,1},{6,2},{7,3},{8,12},{9,13},{10,... | collective-permute-start | bytes 1572872 | tf_op jit(solution)/shard_map/ppermute | solution.py:172
  4.7 1.6 collective-permute-start.1
  6.3 0.7 broadcast_subtract_fusion
  7.4 0.6 gather_fusion.1
  8.3 0.6 gather_fusion
  8.8 0.7 collective-permute-done.2
  9.6 18.8 %collective-permute-done = bf16[64,4096]{1,0:T(8,128)(2,1)} collective-permute-done((bf16[64,4096]{1,0:T(8,128)(2,1)}, bf16[64,4096]{1,0:T(8,128)(2,1)}, u32[]{:S(2)}, u32[]{:S(2)}) %collective-permute-start) | collective-permute-done | bytes 524320 | tf_op jit(solution)/shard_map/ppermute | solution.py:172
  28.4 0.7 collective-permute-start.3
  29.1 1.3 collective-permute-start.4
  30.4 2.0 copy.18
  32.4 0.6 collective-permute-start.6
  33.1 13.1 %collective-permute-done.4 = bf16[64,4096]{1,0:T(8,128)(2,1)} collective-permute-done((bf16[64,4096]{1,0:T(8,128)(2,1)}, bf16[64,4096]{1,0:T(8,128)(2,1)}, u32[]{:S(2)}, u32[]{:S(2)}) %collective-permute-start.4) | collective-permute-done | bytes 524320 | tf_op jit(solution)/shard_map/ppermute | solution.py:172
  46.2 1.1 select_bitcast_fusion
  47.3 1.7 pad_maximum_fusion.own
  49.1 0.5 collective-permute-start.11
  49.7 3.4 %collective-permute-start.10 = (bf16[2,4,32,896]{3,2,1,0:T(8,128)(2,1)S(1)}, bf16[2,4,32,896]{3,2,1,0:T(8,128)(2,1)S(1)}, u32[]{:S(2)}, u32[]{:S(2)}) collective-permute-start(bf16[2,4,32,896]{3,2,1,0:T(8,128)(2,1)S(1)} %pad_maximum_fusion.4.refs_0_), channel_id=1, source_target_pairs={{0,2},{1,3},{2,0},{3,1},{4,6},{5,7},{6,4},{7,5},{8,10},{9,11},{10,... | collective-permute-start | bytes 1376264 | tf_op jit(solution)/shard_map/ppermute | solution.py:172
  53.1 0.2 collective-permute-done.8.other
  53.2 9.7 %project.1 = (bf16[4,64,1536]{2,1,0:T(8,128)(2,1)S(1)}, bf16[4,64,1536]{2,1,0:T(8,128)(2,1)S(1)}) custom-call(s32[2]{0:T(128)S(1)} %pad_add_fusion.pos, bf16[4,64,4096]{2,1,0:T(8,128)(2,1)S(1)} %pad_maximum_fusion.own, bf16[4,64,4096]{2,1,0:T(8,128)(2,1)S(1)} %collective-permute-done.8.other, bf16[3,4096,512]{2,1,0:T(8,128)(2,1)} %bitcast.53), custom_call_target="tpu_custom_call" | custom-call | flops 6442450944 | bytes 16777216 | tf_op jit(solution)/shard_map/project/pallas_call | solution.py:231
  63.0 10.0 %collective-permute-done.9.refs_2_ = bf16[2,4,32,896]{3,2,1,0:T(8,128)(2,1)S(1)} collective-permute-done((bf16[2,4,32,896]{3,2,1,0:T(8,128)(2,1)S(1)}, bf16[2,4,32,896]{3,2,1,0:T(8,128)(2,1)S(1)}, u32[]{:S(2)}, u32[]{:S(2)}) %collective-permute-start.9) | collective-permute-done | bytes 458784 | tf_op jit(solution)/shard_map/ppermute | solution.py:172
  73.1 0.6 collective-permute-start.15
  73.7 0.8 collective-permute-start.12
  74.6 1.3 collective-permute-start.13
  76.1 0.7 collective-permute-start.16
  76.8 0.2 pad_maximum_fusion.1.queries
  77.0 11.9 %collective-permute-done.13.refs_4_ = bf16[2,4,32,896]{3,2,1,0:T(8,128)(2,1)S(1)} collective-permute-done((bf16[2,4,32,896]{3,2,1,0:T(8,128)(2,1)S(1)}, bf16[2,4,32,896]{3,2,1,0:T(8,128)(2,1)S(1)}, u32[]{:S(2)}, u32[]{:S(2)}) %collective-permute-start.13) | collective-permute-done | bytes 458784 | tf_op jit(solution)/shard_map/ppermute | solution.py:172
  88.9 5.0 %encode.3 = (bf16[256,896]{1,0:T(8,128)(2,1)S(1)}, bf16[256,896]{1,0:T(8,128)(2,1)S(1)}) custom-call(s32[2]{0:T(128)S(1)} %pad_add_fusion.pos, bf16[2,4,32,896]{3,2,1,0:T(8,128)(2,1)S(1)} %pad_maximum_fusion.4.refs_0_, bf16[2,4,32,896]{3,2,1,0:T(8,128)(2,1)S(1)} %collective-permute-done.10.refs_1_, ...), custom_call_target="tpu_custom_call" | custom-call | flops 2013265920 | bytes 5505024 | tf_op jit(solution)/shard_map/encode/pallas_call | solution.py:297
  94.0 1.5 collective-permute-start.19
  95.4 0.7 collective-permute-start.21
  96.1 5.0 %encode.2 = (bf16[256,896]{1,0:T(8,128)(2,1)S(1)}, bf16[256,896]{1,0:T(8,128)(2,1)S(1)}, bf16[256,896]{1,0:T(8,128)(2,1)S(1)}) custom-call(s32[2]{0:T(128)S(1)} %pad_add_fusion.pos, bf16[2,4,32,896]{3,2,1,0:T(8,128)(2,1)S(1)} %pad_maximum_fusion.4.refs_0_, bf16[2,4,32,896]{3,2,1,0:T(8,128)(2,1)S(1)} %collective-permute-done.10.refs_1_, ...), custom_call_target="tpu_custom_call" | custom-call | flops 2013265920 | bytes 5505024 | tf_op jit(solution)/shard_map/encode/pallas_call | solution.py:297
  101.2 1.6 collective-permute-start.17
  102.8 2.9 %collective-permute-start.18 = (bf16[256,896]{1,0:T(8,128)(2,1)S(1)}, bf16[256,896]{1,0:T(8,128)(2,1)S(1)}, u32[]{:S(2)}, u32[]{:S(2)}) collective-permute-start(bf16[256,896]{1,0:T(8,128)(2,1)S(1)} %get-tuple-element.72), channel_id=1, source_target_pairs={{0,4},{1,5},{6,2},{7,3},{8,12},{9,13},{14,10},{15,11},{16,20},{17,... | collective-permute-start | bytes 1376264 | tf_op jit(solution)/shard_map/ppermute | solution.py:172
  105.7 0.7 collective-permute-done.19
  106.5 1.5 collective-permute-start.20
  108.0 11.8 %collective-permute-done.17.refs_1_ = bf16[256,896]{1,0:T(8,128)(2,1)S(1)} collective-permute-done((bf16[256,896]{1,0:T(8,128)(2,1)S(1)}, bf16[256,896]{1,0:T(8,128)(2,1)S(1)}, u32[]{:S(2)}, u32[]{:S(2)}) %collective-permute-start.17) | collective-permute-done | bytes 458784 | tf_op jit(solution)/shard_map/ppermute | solution.py:172
  119.8 4.5 %collective-permute-done.18.refs_2_ = bf16[256,896]{1,0:T(8,128)(2,1)S(1)} collective-permute-done((bf16[256,896]{1,0:T(8,128)(2,1)S(1)}, bf16[256,896]{1,0:T(8,128)(2,1)S(1)}, u32[]{:S(2)}, u32[]{:S(2)}) %collective-permute-start.18) | collective-permute-done | bytes 458784 | tf_op jit(solution)/shard_map/ppermute | solution.py:172
  124.3 11.7 %collective-permute-done.20.refs_3_ = bf16[256,896]{1,0:T(8,128)(2,1)S(1)} collective-permute-done((bf16[256,896]{1,0:T(8,128)(2,1)S(1)}, bf16[256,896]{1,0:T(8,128)(2,1)S(1)}, u32[]{:S(2)}, u32[]{:S(2)}) %collective-permute-start.20) | collective-permute-done | bytes 458784 | tf_op jit(solution)/shard_map/ppermute | solution.py:172
  136.0 0.5 normed.1.rows
  136.6 2.7 %collective-permute-start.25 = (bf16[256,896]{1,0:T(8,128)(2,1)S(1)}, bf16[256,896]{1,0:T(8,128)(2,1)}, u32[]{:S(2)}, u32[]{:S(2)}) collective-permute-start(bf16[256,896]{1,0:T(8,128)(2,1)S(1)} %normed.1.rows), channel_id=1, source_target_pairs={{0,2},{1,3},{2,0},{3,1},{4,6},{5,7},{6,4},{7,5},{8,10},{9,11},{10,... | collective-permute-start | bytes 1376264 | tf_op jit(solution)/shard_map/ppermute | solution.py:172
  139.5 0.2 dynamic-slice_reduce_fusion.counts
  139.7 3.2 %attend.2.first = bf16[64,1024]{1,0:T(8,128)(2,1)S(1)} custom-call(s32[2]{0:T(128)S(1)} %pad_add_fusion.pos, s32[4]{0:T(128)S(1)} %dynamic-slice_reduce_fusion.counts, bf16[256,896]{1,0:T(8,128)(2,1)S(1)} %normed.1.rows, bf16[896,1024]{1,0:T(8,128)(2,1)S(1)} %bitcast.35, bf16[896,1024]{1,0:T(8,128)(2,1)} %collective-permute-done.6.other_kv, ...), custom_call_target="tpu_custom_call" | custom-call | flops 1006632960 | bytes 4128768 | tf_op jit(solution)/shard_map/attend/pallas_call | solution.py:374
  143.0 12.1 %collective-permute-done.22.two = bf16[256,896]{1,0:T(8,128)(2,1)} collective-permute-done((bf16[256,896]{1,0:T(8,128)(2,1)S(1)}, bf16[256,896]{1,0:T(8,128)(2,1)}, u32[]{:S(2)}, u32[]{:S(2)}) %collective-permute-start.22) | collective-permute-done | bytes 458784 | tf_op jit(solution)/shard_map/ppermute | solution.py:172
  155.1 1.4 collective-permute-start.23
  156.5 1.3 collective-permute-start.24
  157.8 5.1 %attend.3.refs_0_ = bf16[4,64,1024]{2,1,0:T(8,128)(2,1)S(1)} custom-call(s32[2]{0:T(128)S(1)} %pad_add_fusion.pos, s32[4]{0:T(128)S(1)} %dynamic-slice_reduce_fusion.counts, bf16[256,896]{1,0:T(8,128)(2,1)} %collective-permute-done.25.one, bf16[256,896]{1,0:T(8,128)(2,1)} %collective-permute-done.22.two, bf16[896,1024]{1,0:T(8,128)(2,1)S(1)} %bitcast.36, ...), custom_call_target="tpu_custom_call" | custom-call | flops 2013265920 | bytes 4587520 | tf_op jit(solution)/shard_map/attend/pallas_call | solution.py:374
  163.0 0.7 slice_bitcast_fusion
  163.7 0.8 copy-done.4
  164.5 0.7 collective-permute-start.26
  165.2 2.0 collective-permute-done.24.far
  167.2 1.0 copy-done.5
  168.3 7.5 %last_attend.1 = (bf16[64,4096]{1,0:T(8,128)(2,1)S(1)}, bf16[64,4096]{1,0:T(8,128)(2,1)S(1)}, bf16[64,4096]{1,0:T(8,128)(2,1)S(1)}, bf16[64,4096]{1,0:T(8,128)(2,1)S(1)}, bf16[64,1024]{1,0:T(8,128)(2,1)S(1)}) custom-call(s32[2]{0:T(128)S(1)} %pad_add_fusion.pos, s32[4]{0:T(128)S(1)} %dynamic-slice_reduce_fusion.counts, ...), custom_call_target="tpu_custom_call" | custom-call | flops 3154116608 | bytes 10485760 | tf_op jit(solution)/shard_map/last_attend/pallas_call | solution.py:434
  175.8 3.3 %collective-permute-start.29 = (bf16[64,4096]{1,0:T(8,128)(2,1)S(1)}, bf16[64,4096]{1,0:T(8,128)(2,1)S(1)}, u32[]{:S(2)}, u32[]{:S(2)}) collective-permute-start(bf16[64,4096]{1,0:T(8,128)(2,1)S(1)} %get-tuple-element.86), channel_id=1, source_target_pairs={{0,2},{1,3},{6,4},{7,5},{8,10},{9,11},{14,12},{15,13},{16,18},{17,... | collective-permute-start | bytes 1572872 | tf_op jit(solution)/shard_map/ppermute | solution.py:172
  179.1 0.7 collective-permute-start.31
  179.8 4.0 %collective-permute-start.28 = (bf16[64,4096]{1,0:T(8,128)(2,1)S(1)}, bf16[64,4096]{1,0:T(8,128)(2,1)S(1)}, u32[]{:S(2)}, u32[]{:S(2)}) collective-permute-start(bf16[64,4096]{1,0:T(8,128)(2,1)S(1)} %get-tuple-element.85), channel_id=1, source_target_pairs={{0,4},{1,5},{6,2},{7,3},{8,12},{9,13},{14,10},{15,11},{16,20},{17,... | collective-permute-start | bytes 1572872 | tf_op jit(solution)/shard_map/ppermute | solution.py:172
  183.9 6.2 %collective-permute-done.29 = bf16[64,4096]{1,0:T(8,128)(2,1)S(1)} collective-permute-done((bf16[64,4096]{1,0:T(8,128)(2,1)S(1)}, bf16[64,4096]{1,0:T(8,128)(2,1)S(1)}, u32[]{:S(2)}, u32[]{:S(2)}) %collective-permute-start.29) | collective-permute-done | bytes 524320 | tf_op jit(solution)/shard_map/ppermute | solution.py:172
  190.1 0.1 add_convert_fusion.1
  190.2 1.3 collective-permute-start.30
  191.5 0.7 collective-permute-start.32
  192.2 3.4 %late_out.1 = bf16[64,4096]{1,0:T(8,128)(2,1)S(1)} custom-call(bf16[64,1024]{1,0:T(8,128)(2,1)S(1)} %broadcast_select_fusion.before, bf16[512,4096]{1,0:T(8,128)(2,1)S(1)} %copy-done.1, bf16[512,4096]{1,0:T(8,128)(2,1)} %collective-permute-done.7.refs_3_.other_w), custom_call_target="tpu_custom_call" | custom-call | flops 536870912 | bytes 8388608 | tf_op jit(solution)/shard_map/late_out/pallas_call | solution.py:470
  195.7 5.6 %collective-permute-done.27 = bf16[64,4096]{1,0:T(8,128)(2,1)S(1)} collective-permute-done((bf16[64,4096]{1,0:T(8,128)(2,1)S(1)}, bf16[64,4096]{1,0:T(8,128)(2,1)S(1)}, u32[]{:S(2)}, u32[]{:S(2)}) %collective-permute-start.27) | collective-permute-done | bytes 524320 | tf_op jit(solution)/shard_map/ppermute | solution.py:172
  201.4 3.1 %collective-permute-done.30 = bf16[64,4096]{1,0:T(8,128)(2,1)S(1)} collective-permute-done((bf16[64,4096]{1,0:T(8,128)(2,1)S(1)}, bf16[64,4096]{1,0:T(8,128)(2,1)S(1)}, u32[]{:S(2)}, u32[]{:S(2)}) %collective-permute-start.30) | collective-permute-done | bytes 524320 | tf_op jit(solution)/shard_map/ppermute | solution.py:172
  204.5 0.4 add_convert_fusion
  205.1 0.8 copy.17
  205.9 1.0 collective-permute-done.33
  207.0 0.8 pad_maximum_fusion.3
  (70 shorter events, 2.2 us)
Async XLA Ops:
  0.6 6.7 %copy-start = (bf16[16,16,896]{2,1,0:T(8,128)(2,1)S(1)}, bf16[16,16,896]{2,1,0:T(8,128)(2,1)}, u32[]{:S(2)}) copy-start(bf16[16,16,896]{2,1,0:T(8,128)(2,1)} %param.11) | copy-start | bytes 1376260
  0.6 27.7 %collective-permute-start = (bf16[64,4096]{1,0:T(8,128)(2,1)}, bf16[64,4096]{1,0:T(8,128)(2,1)}, u32[]{:S(2)}, u32[]{:S(2)}) collective-permute-start(bf16[64,4096]{1,0:T(8,128)(2,1)} %param.10), channel_id=1, source_target_pairs={{0,4},{1,5},{2,6},{3,7},{4,0},{5,1},{6,2},{7,3},{8,12},{9,13},{10,... | collective-permute-start | bytes 1572872 | tf_op jit(solution)/shard_map/ppermute | solution.py:172
  4.7 23.7 %collective-permute-start.1 = (bf16[64,4096]{1,0:T(8,128)(2,1)}, bf16[64,4096]{1,0:T(8,128)(2,1)S(1)}, u32[]{:S(2)}, u32[]{:S(2)}) collective-permute-start(bf16[64,4096]{1,0:T(8,128)(2,1)} %param.10), channel_id=1, source_target_pairs={{0,2},{1,3},{2,0},{3,1},{4,6},{5,7},{6,4},{7,5},{8,10},{9,11},{10,... | collective-permute-start | bytes 1572872 | tf_op jit(solution)/shard_map/ppermute | solution.py:172
  8.0 1.6 collective-permute-start.2
  28.4 2.0 copy-start.6
  28.4 20.6 %collective-permute-start.7 = (bf16[512,4096]{1,0:T(8,128)(2,1)}, bf16[512,4096]{1,0:T(8,128)(2,1)}, u32[]{:S(2)}, u32[]{:S(2)}) collective-permute-start(bf16[512,4096]{1,0:T(8,128)(2,1)} %own_w), channel_id=1, source_target_pairs={{0,1},{1,0},{2,3},{3,2},{4,5},{5,4},{6,7},{7,6},{8,9},{9,8},{10,11... | collective-permute-start | bytes 12582920 | tf_op jit(solution)/shard_map/ppermute | solution.py:165
  28.4 4.7 %collective-permute-start.3 = (bf16[64,4096]{1,0:T(8,128)(2,1)}, bf16[64,4096]{1,0:T(8,128)(2,1)S(1)}, u32[]{:S(2)}, u32[]{:S(2)}) collective-permute-start(bf16[64,4096]{1,0:T(8,128)(2,1)} %param.10), channel_id=1, source_target_pairs={{2,4},{3,5},{4,2},{5,3},{10,12},{11,13},{12,10},{13,11},{18,20},{1... | collective-permute-start | bytes 1572872 | tf_op jit(solution)/shard_map/ppermute | solution.py:172
  29.1 17.1 %collective-permute-start.4 = (bf16[64,4096]{1,0:T(8,128)(2,1)}, bf16[64,4096]{1,0:T(8,128)(2,1)}, u32[]{:S(2)}, u32[]{:S(2)}) collective-permute-start(bf16[64,4096]{1,0:T(8,128)(2,1)} %collective-permute-done), channel_id=1, source_target_pairs={{2,0},{3,1},{4,6},{5,7},{10,8},{11,9},{12,14},{13,15},{18,16},{19,... | collective-permute-start | bytes 1572872 | tf_op jit(solution)/shard_map/ppermute | solution.py:172
  32.4 16.6 %collective-permute-start.6 = (bf16[896,1024]{1,0:T(8,128)(2,1)S(1)}, bf16[896,1024]{1,0:T(8,128)(2,1)}, u32[]{:S(2)}, u32[]{:S(2)}) collective-permute-start(bf16[896,1024]{1,0:T(8,128)(2,1)S(1)} %bitcast.34), channel_id=1, source_target_pairs={{0,1},{1,0},{2,3},{3,2},{4,5},{5,4},{6,7},{7,6},{8,9},{9,8},{10,11... | collective-permute-start | bytes 5505032 | tf_op jit(solution)/shard_map/ppermute | solution.py:165
  33.0 16.0 %collective-permute-start.5 = (bf16[512,896]{1,0:T(8,128)(2,1)}, bf16[512,896]{1,0:T(8,128)(2,1)S(1)}, u32[]{:S(2)}, u32[]{:S(2)}) collective-permute-start(bf16[512,896]{1,0:T(8,128)(2,1)} %refs_8_.1), channel_id=1, source_target_pairs={{0,1},{1,0},{2,3},{3,2},{4,5},{5,4},{6,7},{7,6},{8,9},{9,8},{10,11... | collective-permute-start | bytes 2752520 | tf_op jit(solution)/shard_map/ppermute | solution.py:165
  47.3 1.8 copy-start.2
  49.0 4.2 %collective-permute-start.8 = (bf16[4,64,4096]{2,1,0:T(8,128)(2,1)S(1)}, bf16[4,64,4096]{2,1,0:T(8,128)(2,1)S(1)}, u32[]{:S(2)}, u32[]{:S(2)}) collective-permute-start(bf16[4,64,4096]{2,1,0:T(8,128)(2,1)S(1)} %pad_maximum_fusion.own), channel_id=1, source_target_pairs={{0,1},{1,0},{2,3},{3,2},{4,5},{5,4},{6,7},{7,6},{8,9},{9,8},{10,11... | collective-permute-start | bytes 6291464 | tf_op jit(solution)/shard_map/ppermute | solution.py:165
  49.1 24.0 %collective-permute-start.11 = (bf16[896,512]{1,0:T(8,128)(2,1)S(1)}, bf16[896,512]{1,0:T(8,128)(2,1)S(1)}, u32[]{:S(2)}, u32[]{:S(2)}) collective-permute-start(bf16[896,512]{1,0:T(8,128)(2,1)S(1)} %copy-done.2), channel_id=1, source_target_pairs={{0,1},{1,0},{2,3},{3,2},{4,5},{5,4},{6,7},{7,6},{8,9},{9,8},{10,11... | collective-permute-start | bytes 2752520 | tf_op jit(solution)/shard_map/ppermute | solution.py:165
  49.7 23.3 %collective-permute-start.9 = (bf16[2,4,32,896]{3,2,1,0:T(8,128)(2,1)S(1)}, bf16[2,4,32,896]{3,2,1,0:T(8,128)(2,1)S(1)}, u32[]{:S(2)}, u32[]{:S(2)}) collective-permute-start(bf16[2,4,32,896]{3,2,1,0:T(8,128)(2,1)S(1)} %pad_maximum_fusion.4.refs_0_), channel_id=1, source_target_pairs={{0,4},{1,5},{2,6},{3,7},{4,0},{5,1},{6,2},{7,3},{8,12},{9,13},{10,... | collective-permute-start | bytes 1376264 | tf_op jit(solution)/shard_map/ppermute | solution.py:172
  49.7 23.4 %collective-permute-start.10 = (bf16[2,4,32,896]{3,2,1,0:T(8,128)(2,1)S(1)}, bf16[2,4,32,896]{3,2,1,0:T(8,128)(2,1)S(1)}, u32[]{:S(2)}, u32[]{:S(2)}) collective-permute-start(bf16[2,4,32,896]{3,2,1,0:T(8,128)(2,1)S(1)} %pad_maximum_fusion.4.refs_0_), channel_id=1, source_target_pairs={{0,2},{1,3},{2,0},{3,1},{4,6},{5,7},{6,4},{7,5},{8,10},{9,11},{10,... | collective-permute-start | bytes 1376264 | tf_op jit(solution)/shard_map/ppermute | solution.py:172
  73.1 2.9 %collective-permute-start.14 = (bf16[4,64,1536]{2,1,0:T(8,128)(2,1)S(1)}, bf16[4,64,1536]{2,1,0:T(8,128)(2,1)S(1)}, u32[]{:S(2)}, u32[]{:S(2)}) collective-permute-start(bf16[4,64,1536]{2,1,0:T(8,128)(2,1)S(1)} %get-tuple-element.60), channel_id=1, source_target_pairs={{0,1},{1,0},{2,3},{3,2},{4,5},{5,4},{6,7},{7,6},{8,9},{9,8},{10,11... | collective-permute-start | bytes 2359304 | tf_op jit(solution)/shard_map/ppermute | solution.py:165
  73.1 2.8 %collective-permute-start.15 = (bf16[4,64,512]{2,1,0:T(8,128)(2,1)S(1)}, bf16[4,64,512]{2,1,0:T(8,128)(2,1)S(1)}, u32[]{:S(2)}, u32[]{:S(2)}) collective-permute-start(bf16[4,64,512]{2,1,0:T(8,128)(2,1)S(1)} %slice.38), channel_id=1, source_target_pairs={{0,1},{1,0},{2,3},{3,2},{4,5},{5,4},{6,7},{7,6},{8,9},{9,8},{10,11... | collective-permute-start | bytes 786440 | tf_op jit(solution)/shard_map/ppermute | solution.py:165
  73.7 15.2 %copy-start.3 = (bf16[512,896]{1,0:T(8,128)(2,1)S(1)}, bf16[512,896]{1,0:T(8,128)(2,1)}, u32[]{:S(2)}) copy-start(bf16[512,896]{1,0:T(8,128)(2,1)} %refs_8_.1) | copy-start | bytes 2752516
  73.7 3.2 %collective-permute-start.12 = (bf16[2,4,32,896]{3,2,1,0:T(8,128)(2,1)S(1)}, bf16[2,4,32,896]{3,2,1,0:T(8,128)(2,1)S(1)}, u32[]{:S(2)}, u32[]{:S(2)}) collective-permute-start(bf16[2,4,32,896]{3,2,1,0:T(8,128)(2,1)S(1)} %pad_maximum_fusion.4.refs_0_), channel_id=1, source_target_pairs={{2,4},{3,5},{4,2},{5,3},{10,12},{11,13},{12,10},{13,11},{18,20},{1... | collective-permute-start | bytes 1376264 | tf_op jit(solution)/shard_map/ppermute | solution.py:172
  74.6 14.3 %collective-permute-start.13 = (bf16[2,4,32,896]{3,2,1,0:T(8,128)(2,1)S(1)}, bf16[2,4,32,896]{3,2,1,0:T(8,128)(2,1)S(1)}, u32[]{:S(2)}, u32[]{:S(2)}) collective-permute-start(bf16[2,4,32,896]{3,2,1,0:T(8,128)(2,1)S(1)} %collective-permute-done.9.refs_2_), channel_id=1, source_target_pairs={{2,0},{3,1},{4,6},{5,7},{10,8},{11,9},{12,14},{13,15},{18,16},{19,... | collective-permute-start | bytes 1376264 | tf_op jit(solution)/shard_map/ppermute | solution.py:172
  76.1 0.7 collective-permute-start.16
  93.9 14.0 %copy-start.7 = (f32[896]{0:T(1024)S(1)}, f32[896]{0:T(1024)}, u32[]{:S(2)}) copy-start(f32[896]{0:T(1024)} %param.17) | copy-start | bytes 10756
  94.0 12.4 %collective-permute-start.19 = (bf16[256,896]{1,0:T(8,128)(2,1)S(1)}, bf16[256,896]{1,0:T(8,128)(2,1)S(1)}, u32[]{:S(2)}, u32[]{:S(2)}) collective-permute-start(bf16[256,896]{1,0:T(8,128)(2,1)S(1)} %get-tuple-element.73), channel_id=1, source_target_pairs={{0,2},{1,3},{6,4},{7,5},{8,10},{9,11},{14,12},{15,13},{16,18},{17,... | collective-permute-start | bytes 1376264 | tf_op jit(solution)/shard_map/ppermute | solution.py:172
  95.4 28.9 %collective-permute-start.21 = (bf16[256,896]{1,0:T(8,128)(2,1)S(1)}, bf16[256,896]{1,0:T(8,128)(2,1)S(1)}, u32[]{:S(2)}, u32[]{:S(2)}) collective-permute-start(bf16[256,896]{1,0:T(8,128)(2,1)S(1)} %get-tuple-element.73), channel_id=1, source_target_pairs={{2,4},{3,5},{4,2},{5,3},{10,12},{11,13},{12,10},{13,11},{18,20},{1... | collective-permute-start | bytes 1376264 | tf_op jit(solution)/shard_map/ppermute | solution.py:172
  101.2 18.6 %collective-permute-start.17 = (bf16[256,896]{1,0:T(8,128)(2,1)S(1)}, bf16[256,896]{1,0:T(8,128)(2,1)S(1)}, u32[]{:S(2)}, u32[]{:S(2)}) collective-permute-start(bf16[256,896]{1,0:T(8,128)(2,1)S(1)} %get-tuple-element.71), channel_id=1, source_target_pairs={{0,2},{1,3},{2,0},{3,1},{4,6},{5,7},{6,4},{7,5},{8,10},{9,11},{10,... | collective-permute-start | bytes 1376264 | tf_op jit(solution)/shard_map/ppermute | solution.py:172
  102.8 36.6 %copy-start.8 = (s32[32]{0:T(128)S(1)}, s32[32]{0:T(128)}, u32[]{:S(2)}) copy-start(s32[32]{0:T(128)} %param.13) | copy-start | bytes 388
  102.8 21.6 %collective-permute-start.18 = (bf16[256,896]{1,0:T(8,128)(2,1)S(1)}, bf16[256,896]{1,0:T(8,128)(2,1)S(1)}, u32[]{:S(2)}, u32[]{:S(2)}) collective-permute-start(bf16[256,896]{1,0:T(8,128)(2,1)S(1)} %get-tuple-element.72), channel_id=1, source_target_pairs={{0,4},{1,5},{6,2},{7,3},{8,12},{9,13},{14,10},{15,11},{16,20},{17,... | collective-permute-start | bytes 1376264 | tf_op jit(solution)/shard_map/ppermute | solution.py:172
  106.5 29.6 %collective-permute-start.20 = (bf16[256,896]{1,0:T(8,128)(2,1)S(1)}, bf16[256,896]{1,0:T(8,128)(2,1)S(1)}, u32[]{:S(2)}, u32[]{:S(2)}) collective-permute-start(bf16[256,896]{1,0:T(8,128)(2,1)S(1)} %add_convert_fusion.2), channel_id=1, source_target_pairs={{2,6},{3,7},{4,0},{5,1},{10,14},{11,15},{12,8},{13,9},{18,22},{19,... | collective-permute-start | bytes 1376264 | tf_op jit(solution)/shard_map/ppermute | solution.py:172
  136.6 18.5 %collective-permute-start.22 = (bf16[256,896]{1,0:T(8,128)(2,1)S(1)}, bf16[256,896]{1,0:T(8,128)(2,1)}, u32[]{:S(2)}, u32[]{:S(2)}) collective-permute-start(bf16[256,896]{1,0:T(8,128)(2,1)S(1)} %normed.1.rows), channel_id=1, source_target_pairs={{0,4},{1,5},{2,6},{3,7},{4,0},{5,1},{6,2},{7,3},{8,12},{9,13},{10,... | collective-permute-start | bytes 1376264 | tf_op jit(solution)/shard_map/ppermute | solution.py:172
  136.6 21.2 %collective-permute-start.25 = (bf16[256,896]{1,0:T(8,128)(2,1)S(1)}, bf16[256,896]{1,0:T(8,128)(2,1)}, u32[]{:S(2)}, u32[]{:S(2)}) collective-permute-start(bf16[256,896]{1,0:T(8,128)(2,1)S(1)} %normed.1.rows), channel_id=1, source_target_pairs={{0,2},{1,3},{2,0},{3,1},{4,6},{5,7},{6,4},{7,5},{8,10},{9,11},{10,... | collective-permute-start | bytes 1376264 | tf_op jit(solution)/shard_map/ppermute | solution.py:172
  155.1 10.1 %collective-permute-start.23 = (bf16[256,896]{1,0:T(8,128)(2,1)S(1)}, bf16[256,896]{1,0:T(8,128)(2,1)}, u32[]{:S(2)}, u32[]{:S(2)}) collective-permute-start(bf16[256,896]{1,0:T(8,128)(2,1)S(1)} %normed.1.rows), channel_id=1, source_target_pairs={{2,4},{3,5},{4,2},{5,3},{10,12},{11,13},{12,10},{13,11},{18,20},{1... | collective-permute-start | bytes 1376264 | tf_op jit(solution)/shard_map/ppermute | solution.py:172
  156.5 10.7 %collective-permute-start.24 = (bf16[256,896]{1,0:T(8,128)(2,1)}, bf16[256,896]{1,0:T(8,128)(2,1)}, u32[]{:S(2)}, u32[]{:S(2)}) collective-permute-start(bf16[256,896]{1,0:T(8,128)(2,1)} %collective-permute-done.22.two), channel_id=1, source_target_pairs={{2,0},{3,1},{4,6},{5,7},{10,8},{11,9},{12,14},{13,15},{18,16},{19,... | collective-permute-start | bytes 1376264 | tf_op jit(solution)/shard_map/ppermute | solution.py:172
  163.7 0.8 copy-start.4
  164.5 0.7 collective-permute-start.26
  167.2 1.0 copy-start.5
  168.3 24.0 %copy-start.1 = (bf16[512,4096]{1,0:T(8,128)(2,1)S(1)}, bf16[512,4096]{1,0:T(8,128)(2,1)}, u32[]{:S(2)}) copy-start(bf16[512,4096]{1,0:T(8,128)(2,1)} %own_w) | copy-start | bytes 12582916
  175.8 14.3 %collective-permute-start.29 = (bf16[64,4096]{1,0:T(8,128)(2,1)S(1)}, bf16[64,4096]{1,0:T(8,128)(2,1)S(1)}, u32[]{:S(2)}, u32[]{:S(2)}) collective-permute-start(bf16[64,4096]{1,0:T(8,128)(2,1)S(1)} %get-tuple-element.86), channel_id=1, source_target_pairs={{0,2},{1,3},{6,4},{7,5},{8,10},{9,11},{14,12},{15,13},{16,18},{17,... | collective-permute-start | bytes 1572872 | tf_op jit(solution)/shard_map/ppermute | solution.py:172
  179.1 16.5 %collective-permute-start.31 = (bf16[64,4096]{1,0:T(8,128)(2,1)S(1)}, bf16[64,4096]{1,0:T(8,128)(2,1)S(1)}, u32[]{:S(2)}, u32[]{:S(2)}) collective-permute-start(bf16[64,4096]{1,0:T(8,128)(2,1)S(1)} %get-tuple-element.86), channel_id=1, source_target_pairs={{2,4},{3,5},{4,2},{5,3},{10,12},{11,13},{12,10},{13,11},{18,20},{1... | collective-permute-start | bytes 1572872 | tf_op jit(solution)/shard_map/ppermute | solution.py:172
  179.8 15.9 %collective-permute-start.28 = (bf16[64,4096]{1,0:T(8,128)(2,1)S(1)}, bf16[64,4096]{1,0:T(8,128)(2,1)S(1)}, u32[]{:S(2)}, u32[]{:S(2)}) collective-permute-start(bf16[64,4096]{1,0:T(8,128)(2,1)S(1)} %get-tuple-element.85), channel_id=1, source_target_pairs={{0,4},{1,5},{6,2},{7,3},{8,12},{9,13},{14,10},{15,11},{16,20},{17,... | collective-permute-start | bytes 1572872 | tf_op jit(solution)/shard_map/ppermute | solution.py:172
  183.8 17.6 %collective-permute-start.27 = (bf16[64,4096]{1,0:T(8,128)(2,1)S(1)}, bf16[64,4096]{1,0:T(8,128)(2,1)S(1)}, u32[]{:S(2)}, u32[]{:S(2)}) collective-permute-start(bf16[64,4096]{1,0:T(8,128)(2,1)S(1)} %get-tuple-element.84), channel_id=1, source_target_pairs={{0,2},{1,3},{2,0},{3,1},{4,6},{5,7},{6,4},{7,5},{8,10},{9,11},{10,... | collective-permute-start | bytes 1572872 | tf_op jit(solution)/shard_map/ppermute | solution.py:172
  190.2 14.3 %collective-permute-start.30 = (bf16[64,4096]{1,0:T(8,128)(2,1)S(1)}, bf16[64,4096]{1,0:T(8,128)(2,1)S(1)}, u32[]{:S(2)}, u32[]{:S(2)}) collective-permute-start(bf16[64,4096]{1,0:T(8,128)(2,1)S(1)} %add_convert_fusion.1), channel_id=1, source_target_pairs={{2,6},{3,7},{4,0},{5,1},{10,14},{11,15},{12,8},{13,9},{18,22},{19,... | collective-permute-start | bytes 1572872 | tf_op jit(solution)/shard_map/ppermute | solution.py:172
  191.5 0.7 collective-permute-start.32
  204.9 2.0 collective-permute-start.33

commit v5 on v4

--- a/solution.py
+++ b/solution.py
@@ -244,75 +244,83 @@
     )(pos, own, other, w)
 
 
-def enc_kernel(flips, pos, *refs):
+def enc_kernel(ahead, pos, *refs):
     parts, weights, refs = refs[:5], (refs[5:9], refs[9:13]), refs[13:]
-    n = len(flips)
-    outs, (rows, att, sems) = refs[:n], refs[-3:]
-    for k, flip in enumerate(flips):
-        i = pos[0] ^ flip
-        place = lambda ref, j: [(ref.at[c, i], rows.at[k, j, c]) for c in range(2)]
-        begin(fetches(pos, parts, place, sems.at[k]))
-    for k, flip in enumerate(flips):
-        i = pos[0] ^ flip
-        place = lambda ref, j: [(ref.at[c, i], rows.at[k, j, c]) for c in range(2)]
-        finish(fetches(pos, parts, place, sems.at[k]))
-    each_rows, width = outs[0].shape
-    x = rows[...].reshape(n * each_rows, width)
-    if flips[-1] == 0:
-        refs[n][...] = x[(n - 1) * each_rows :]
-    heads = weights[0][0].shape[1]
-    qs = [dot(x, wq[...]).astype(BF16) for wq, *_ in weights]
-    chains = [(w, k, h) for w in range(2) for k in range(n) for h in range(0, heads, HEAD_DIM)]
-    here = [pl.ds(pl.multiple_of((pos[0] ^ flip) * GROUP, GROUP), GROUP) for flip in flips]
-    scores = []
-    for w, k, h in chains:
-        ask = qs[w][k * each_rows : (k + 1) * each_rows, h : h + HEAD_DIM]
-        scores.append(dot_t(weights[w][1][here[k], pl.ds(h, HEAD_DIM)], ask)[None])
-    scores = jnp.concatenate(scores, axis=0) * SCALE
-    raised = jnp.exp(scores - jnp.max(scores, axis=1, keepdims=True))
-    share = (raised / jnp.sum(raised, axis=1, keepdims=True)).astype(BF16)
-    for c, (w, k, h) in enumerate(chains):
-        att[pl.ds(k * each_rows, each_rows), pl.ds(w * heads + h, HEAD_DIM)] = lax.dot_general(
-            share[c],
-            weights[w][2][here[k], pl.ds(h, HEAD_DIM)],
-            (((0,), (0,)), ((), ())),
-            preferred_element_type=F32,
-        ).astype(BF16)
-    total = dot(att[:, pl.ds(0, heads)], weights[0][3][...]) + dot(att[:, pl.ds(heads, heads)], weights[1][3][...])
-    for k, out in enumerate(outs):
-        out[...] = total[k * each_rows : (k + 1) * each_rows].astype(BF16)
-
-
-def encode(pos, parts, flips, queries, projected, outs):
+    if ahead:
+        (two, three, one, own, raw), refs = refs[:5], refs[5:]
+    else:
+        (one, own, raw), refs = refs[3:6], refs[6:]
+    rows, att, sems = refs
+    shape = own.shape
+
+    def work(flips, outs):
+        n = len(flips)
+        for act in begin, finish:
+            for k, flip in enumerate(flips):
+                i = pos[0] ^ flip
+                place = lambda ref, j: [(ref.at[c, i], rows.at[k, j, c]) for c in range(2)]
+                act(fetches(pos, parts, place, sems.at[k]))
+        x = rows[...].reshape(n * shape[0], shape[1])
+        if flips[-1] == 0:
+            raw[...] = x[(n - 1) * shape[0] :]
+        heads = weights[0][0].shape[1]
+        qs = [dot(x, wq[...]).astype(BF16) for wq, *_ in weights]
+        chains = [(w, c, h) for w in range(2) for c in range(n) for h in range(0, heads, HEAD_DIM)]
+        here = [pl.ds(pl.multiple_of((pos[0] ^ flip) * GROUP, GROUP), GROUP) for flip in flips]
+        scores = []
+        for w, c, h in chains:
+            ask = qs[w][c * shape[0] : (c + 1) * shape[0], h : h + HEAD_DIM]
+            scores.append(dot_t(weights[w][1][here[c], pl.ds(h, HEAD_DIM)], ask)[None])
+        scores = jnp.concatenate(scores, axis=0) * SCALE
+        raised = jnp.exp(scores - jnp.max(scores, axis=1, keepdims=True))
+        share = (raised / jnp.sum(raised, axis=1, keepdims=True)).astype(BF16)
+        for m, (w, c, h) in enumerate(chains):
+            att[pl.ds(c * shape[0], shape[0]), pl.ds(w * heads + h, HEAD_DIM)] = lax.dot_general(
+                share[m],
+                weights[w][2][here[c], pl.ds(h, HEAD_DIM)],
+                (((0,), (0,)), ((), ())),
+                preferred_element_type=F32,
+            ).astype(BF16)
+        total = dot(att[:, pl.ds(0, heads)], weights[0][3][...]) + dot(att[:, pl.ds(heads, heads)], weights[1][3][...])
+        for k, out in enumerate(outs):
+            out[...] = total[k * shape[0] : (k + 1) * shape[0]].astype(BF16)
+
+    if ahead:
+        work((2, 3), (two, three))
+    pl.when(pos[1] == (0 if ahead else 1))(lambda: work((1, 0), (one, own)))
+
+
+def encode(pos, parts, queries, projected, outs, *results):
     _, _, part, width = parts[0].shape
     tokens = projected[0].shape[0]
     heads = queries[0].shape[1]
     rows = 8 * part
-    n = len(flips)
     kv = [pl.BlockSpec((tokens, heads), lambda i: (0, 1)), pl.BlockSpec((tokens, heads), lambda i: (0, 2))]
     args = []
     for wq, proj, wo in zip(queries, projected, outs):
         args += [wq, proj, proj, wo]
-    results = n + (flips[-1] == 0)
+    ahead = not results
+    n = 5 if ahead else 3
     return pl.pallas_call(
-        functools.partial(enc_kernel, flips),
+        functools.partial(enc_kernel, ahead),
         grid=(1,),
-        in_specs=[SMEM] + [ANY] * 5 + ([VMEM] + kv + [VMEM]) * 2,
-        out_specs=[VMEM] * results,
-        out_shape=[jax.ShapeDtypeStruct((rows, width), BF16)] * results,
+        in_specs=[SMEM] + [ANY] * 5 + ([VMEM] + kv + [VMEM]) * 2 + [VMEM] * len(results),
+        out_specs=[VMEM] * n,
+        out_shape=[jax.ShapeDtypeStruct((rows, width), BF16)] * n,
+        input_output_aliases={14 + i: i for i in range(len(results))},
         scratch_shapes=[
-            pltpu.VMEM((n, 4, 2, part, width), BF16),
-            pltpu.VMEM((n * rows, 2 * heads), BF16),
-            pltpu.SemaphoreType.DMA((n, 10)),
+            pltpu.VMEM((2, 4, 2, part, width), BF16),
+            pltpu.VMEM((2 * rows, 2 * heads), BF16),
+            pltpu.SemaphoreType.DMA((2, 10)),
         ],
         compiler_params=params(),
         cost_estimate=pl.CostEstimate(
-            flops=2 * n * rows * heads * (4 * width + 4 * GROUP),
-            bytes_accessed=4 * n * rows * width + 8 * heads * width,
-            transcendentals=n * rows * heads,
+            flops=4 * rows * heads * (4 * width + 4 * GROUP),
+            bytes_accessed=8 * rows * width + 8 * heads * width,
+            transcendentals=2 * rows * heads,
         ),
         name="encode",
-    )(pos, *parts, *args)
+    )(pos, *parts, *args, *results)
 
 
 def norm_kernel(nz, *refs):
@@ -358,24 +366,24 @@
     attention(pos[0], pos[1], counts, rows[...], (own_kv, other_kv), queries, out)
 
 
-def attend_more_kernel(pos, counts, one, two, own_kv, other_kv, queries, first, out):
+def attend_more_kernel(pos, counts, one, two, own_kv, other_kv, queries, first, out, pick):
     out[0] = first[...]
     for flip, x in (1, one), (2, two):
         attention(pos[0] ^ flip, pos[1], counts, x[...], (own_kv, other_kv), queries, out.at[flip])
     z = pos[0]
-    out[3] = jnp.where(z == 3, out[0], jnp.where(z == 2, out[1], out[2]))
+    pick[...] = jnp.where(z == 3, out[0], jnp.where(z == 2, out[1], out[2]))
 
 
 def attend(pos, counts, rows, wkvs, queries, *earlier):
     keys, width = rows[0].shape
     both = wkvs[0].shape[1]
     n = len(rows)
-    shape = (4, GROUP, both) if earlier else (GROUP, both)
+    single = jax.ShapeDtypeStruct((GROUP, both), BF16)
     return pl.pallas_call(
         attend_more_kernel if earlier else attend_kernel,
         in_specs=[SMEM, SMEM] + [VMEM] * (n + 3 + len(earlier)),
-        out_specs=VMEM,
-        out_shape=jax.ShapeDtypeStruct(shape, BF16),
+        out_specs=[VMEM, VMEM] if earlier else VMEM,
+        out_shape=[jax.ShapeDtypeStruct((3, GROUP, both), BF16), single] if earlier else single,
         compiler_params=params(),
         cost_estimate=pl.CostEstimate(
             flops=4 * n * keys * both * (width + GROUP),
@@ -534,21 +542,24 @@
 
     last = jnp.concatenate([p[:, :width].reshape(nz, GROUP, width)[:, GROUP - 1 :] for p in projected], axis=2)
     others = jnp.concatenate([theirs[:, :, :width], swapped(mine[:, :, :width], nz)], axis=2)
+    counts = lax.dynamic_index_in_dim(
+        lax.dynamic_slice_in_dim(valid_counts, seq_index * ch_grp, ch_grp, 0).reshape(nz, 2), core, 1, False
+    )
+
+    nbrs, others, last = held((nbrs, others, last))
     queries = jnp.concatenate([last, others[:, : GROUP - 1]], axis=1)
     odd = range(1, 2 * nz, 2)
     back = [((q + 1) * 2 * nz + n, q * 2 * nz + n) for q in range(n_seq - 1) for n in odd]
     queries = jnp.concatenate([queries, lax.ppermute(queries[:1], ("seq", "nbr"), back)])
-    counts = lax.dynamic_index_in_dim(
-        lax.dynamic_slice_in_dim(valid_counts, seq_index * ch_grp, ch_grp, 0).reshape(nz, 2), core, 1, False
-    )
-
-    nbrs, queries = held((nbrs, queries))
+    two, three, *rest = encode(pos, nbrs, encqs, projected, encos)
     raws = []
 
     def part(flips):
-        got = encode(pos, nbrs, flips, encqs, projected, encos)
-        raws.extend(got[len(flips) :])
-        return got[: len(flips)]
+        if flips == (2, 3):
+            return two, three
+        one, own, raw = encode(pos, nbrs, encqs, projected, encos, *rest)
+        raws.append(raw)
+        return one, own
 
     arrived = scattered(part)
     enc_own = normed(arrived, raws[0], enc_gain.reshape(1, -1))
@@ -556,14 +567,14 @@
     first = attend(pos, counts, (enc_own,), wkvs, queries)
     enc_two, enc_mine, first = held((enc_two, enc_own, first))
     enc_middle, enc_far = hop(enc_mine, 3, MIDDLE), hop(enc_two, 1, MIDDLE)
-    atts = attend(pos, counts, (enc_one, enc_two), wkvs, queries, first)
+    atts, pick = attend(pos, counts, (enc_one, enc_two), wkvs, queries, first)
 
     def onward(x, chips):
         route = [(q * 2 * nz + 2 * i + 1, (q + 1) * 2 * nz + 2 * i + 1) for q in range(n_seq - 1) for i in chips]
         got = lax.ppermute(x, ("seq", "nbr"), route)
         return jnp.where((seq_index * ch_grp * GROUP) % SEQ_LEN == 0, 0, got).astype(BF16)
 
-    before = onward(atts[3], (1, 2, 3))
+    before = onward(pick, (1, 2, 3))
     *outs, last = last_attend(pos, counts, enc_middle, enc_far, wkvs, queries, atts, before, outps)
     arrived = scattered(lambda flips: [outs[flip] for flip in flips])
     arrived.append(late_out(onward(last, (0,)), outps))

time: 209 us -> 209 us (level)
  transfers between devices with their start and end apart: 34 -> 34, of which waited for: 19 -> 19; matrix products, arithmetic and copies ran while one was open for 5% -> 5% of each run, Pallas kernels for 13% -> 11%
where the time goes in v5:
time: 209 us; the launch traced here: 207 us
  waiting for transfers between devices  112 us (54%)
  starting transfers between devices  40.2 us (19%)
  Pallas kernels  39.9 us (19%)
  local copies, waits for them, and re-layouts  6.89 us (3%)
  other arithmetic  6.62 us (3%)
    ppermute x22, waiting for transfers between devices, hop(): lax.ppermute(x, 'nbr', [(2 * z + c, 2 * (z ^ flip) + c) for z in chips fo...  110 us
    ppermute x22, starting transfers between devices, hop(): lax.ppermute(x, 'nbr', [(2 * z + c, 2 * (z ^ flip) + c) for z in chips fo...  34.9 us
    pallas_call x2, Pallas kernels, encode(): pl.pallas_call(functools.partial(enc_kernel, ahead), grid=(1,), in_specs=...  10.2 us
    pallas_call x1, Pallas kernels, project(): pl.pallas_call(proj_kernel, in_specs=[SMEM, VMEM, VMEM, HBM], out_specs=[...  9.73 us
    pallas_call x2, Pallas kernels, attend(): pl.pallas_call(attend_more_kernel if earlier else attend_kernel, in_specs...  8.41 us
    pallas_call x1, Pallas kernels, last_attend(): pl.pallas_call(last_kernel, in_specs=[SMEM, SMEM] + [VMEM] * 7 + [HBM, AN...  7.55 us
  transfers between devices with their start and end apart: 34, of which 19 were waited for; matrix products, arithmetic and copies ran while one was open for 5% of the time, Pallas kernels for 11%

profile of v5, /device:TPU:0, one launch (start us, length us, event | category | flops | bytes accessed | tf_op | source)
XLA Modules:
  0.0 207.1 jit_solution(13999806534252722040)
XLA Ops:
  0.6 4.1 %collective-permute-start = (bf16[64,4096]{1,0:T(8,128)(2,1)}, bf16[64,4096]{1,0:T(8,128)(2,1)}, u32[]{:S(2)}, u32[]{:S(2)}) collective-permute-start(bf16[64,4096]{1,0:T(8,128)(2,1)} %param.10), channel_id=1, source_target_pairs={{0,4},{1,5},{2,6},{3,7},{4,0},{5,1},{6,2},{7,3},{8,12},{9,13},{10,... | collective-permute-start | bytes 1572872 | tf_op jit(solution)/shard_map/ppermute | solution.py:172
  4.7 1.6 collective-permute-start.1
  6.3 0.7 broadcast_subtract_fusion
  7.4 0.6 gather_fusion.1
  8.3 0.6 gather_fusion
  8.8 0.7 collective-permute-done.2
  9.6 18.8 %collective-permute-done = bf16[64,4096]{1,0:T(8,128)(2,1)} collective-permute-done((bf16[64,4096]{1,0:T(8,128)(2,1)}, bf16[64,4096]{1,0:T(8,128)(2,1)}, u32[]{:S(2)}, u32[]{:S(2)}) %collective-permute-start) | collective-permute-done | bytes 524320 | tf_op jit(solution)/shard_map/ppermute | solution.py:172
  28.4 0.7 collective-permute-start.3
  29.1 1.3 collective-permute-start.4
  30.4 2.0 copy.21
  32.4 0.6 collective-permute-start.6
  33.1 13.1 %collective-permute-done.4 = bf16[64,4096]{1,0:T(8,128)(2,1)} collective-permute-done((bf16[64,4096]{1,0:T(8,128)(2,1)}, bf16[64,4096]{1,0:T(8,128)(2,1)}, u32[]{:S(2)}, u32[]{:S(2)}) %collective-permute-start.4) | collective-permute-done | bytes 524320 | tf_op jit(solution)/shard_map/ppermute | solution.py:172
  46.2 1.1 select_bitcast_fusion
  47.3 1.7 pad_maximum_fusion.own
  49.1 0.5 collective-permute-start.11
  49.7 3.4 %collective-permute-start.10 = (bf16[2,4,32,896]{3,2,1,0:T(8,128)(2,1)S(1)}, bf16[2,4,32,896]{3,2,1,0:T(8,128)(2,1)S(1)}, u32[]{:S(2)}, u32[]{:S(2)}) collective-permute-start(bf16[2,4,32,896]{3,2,1,0:T(8,128)(2,1)S(1)} %pad_maximum_fusion.4.refs_0_), channel_id=1, source_target_pairs={{0,2},{1,3},{2,0},{3,1},{4,6},{5,7},{6,4},{7,5},{8,10},{9,11},{10,... | collective-permute-start | bytes 1376264 | tf_op jit(solution)/shard_map/ppermute | solution.py:172
  53.1 0.2 collective-permute-done.8.other
  53.2 9.7 %project.1 = (bf16[4,64,1536]{2,1,0:T(8,128)(2,1)S(1)}, bf16[4,64,1536]{2,1,0:T(8,128)(2,1)S(1)}) custom-call(s32[2]{0:T(128)S(1)} %pad_add_fusion.pos, bf16[4,64,4096]{2,1,0:T(8,128)(2,1)S(1)} %pad_maximum_fusion.own, bf16[4,64,4096]{2,1,0:T(8,128)(2,1)S(1)} %collective-permute-done.8.other, bf16[3,4096,512]{2,1,0:T(8,128)(2,1)} %bitcast.54), custom_call_target="tpu_custom_call" | custom-call | flops 6442450944 | bytes 16777216 | tf_op jit(solution)/shard_map/project/pallas_call | solution.py:231
  63.0 10.0 %collective-permute-done.9.refs_2_ = bf16[2,4,32,896]{3,2,1,0:T(8,128)(2,1)S(1)} collective-permute-done((bf16[2,4,32,896]{3,2,1,0:T(8,128)(2,1)S(1)}, bf16[2,4,32,896]{3,2,1,0:T(8,128)(2,1)S(1)}, u32[]{:S(2)}, u32[]{:S(2)}) %collective-permute-start.9) | collective-permute-done | bytes 458784 | tf_op jit(solution)/shard_map/ppermute | solution.py:172
  73.1 0.6 collective-permute-start.14
  73.7 0.7 collective-permute-start.12
  74.4 1.3 collective-permute-start.13
  75.9 12.8 %collective-permute-done.13.refs_4_ = bf16[2,4,32,896]{3,2,1,0:T(8,128)(2,1)S(1)} collective-permute-done((bf16[2,4,32,896]{3,2,1,0:T(8,128)(2,1)S(1)}, bf16[2,4,32,896]{3,2,1,0:T(8,128)(2,1)S(1)}, u32[]{:S(2)}, u32[]{:S(2)}) %collective-permute-start.13) | collective-permute-done | bytes 458784 | tf_op jit(solution)/shard_map/ppermute | solution.py:172
  88.7 9.3 %encode.2 = (bf16[256,896]{1,0:T(8,128)(2,1)S(1)}, bf16[256,896]{1,0:T(8,128)(2,1)S(1)}, bf16[256,896]{1,0:T(8,128)(2,1)S(1)}, bf16[256,896]{1,0:T(8,128)(2,1)S(1)}, bf16[256,896]{1,0:T(8,128)(2,1)S(1)}) custom-call(s32[2]{0:T(128)S(1)} %pad_add_fusion.pos, bf16[2,4,32,896]{3,2,1,0:T(8,128)(2,1)S(1)} %pad_maximum_fusion.4.refs_0_, ...), custom_call_target="tpu_custom_call" | custom-call | flops 2013265920 | bytes 5505024 | tf_op jit(solution)/shard_map/encode/pallas_call | solution.py:304
  98.1 1.5 collective-permute-start.18
  99.6 0.7 collective-permute-start.20
  100.3 0.9 encode.3
  101.2 1.6 collective-permute-start.16
  102.8 2.8 %collective-permute-start.17 = (bf16[256,896]{1,0:T(8,128)(2,1)S(1)}, bf16[256,896]{1,0:T(8,128)(2,1)S(1)}, u32[]{:S(2)}, u32[]{:S(2)}) collective-permute-start(bf16[256,896]{1,0:T(8,128)(2,1)S(1)} %get-tuple-element.81), channel_id=1, source_target_pairs={{0,4},{1,5},{6,2},{7,3},{8,12},{9,13},{14,10},{15,11},{16,20},{17,... | collective-permute-start | bytes 1376264 | tf_op jit(solution)/shard_map/ppermute | solution.py:172
  105.6 3.6 %collective-permute-done.18 = bf16[256,896]{1,0:T(8,128)(2,1)S(1)} collective-permute-done((bf16[256,896]{1,0:T(8,128)(2,1)S(1)}, bf16[256,896]{1,0:T(8,128)(2,1)S(1)}, u32[]{:S(2)}, u32[]{:S(2)}) %collective-permute-start.18) | collective-permute-done | bytes 458784 | tf_op jit(solution)/shard_map/ppermute | solution.py:172
  109.3 1.3 collective-permute-start.19
  110.7 8.9 %collective-permute-done.16.refs_1_ = bf16[256,896]{1,0:T(8,128)(2,1)S(1)} collective-permute-done((bf16[256,896]{1,0:T(8,128)(2,1)S(1)}, bf16[256,896]{1,0:T(8,128)(2,1)S(1)}, u32[]{:S(2)}, u32[]{:S(2)}) %collective-permute-start.16) | collective-permute-done | bytes 458784 | tf_op jit(solution)/shard_map/ppermute | solution.py:172
  119.6 5.7 %collective-permute-done.17.refs_2_ = bf16[256,896]{1,0:T(8,128)(2,1)S(1)} collective-permute-done((bf16[256,896]{1,0:T(8,128)(2,1)S(1)}, bf16[256,896]{1,0:T(8,128)(2,1)S(1)}, u32[]{:S(2)}, u32[]{:S(2)}) %collective-permute-start.17) | collective-permute-done | bytes 458784 | tf_op jit(solution)/shard_map/ppermute | solution.py:172
  125.2 11.4 %collective-permute-done.19.refs_3_ = bf16[256,896]{1,0:T(8,128)(2,1)S(1)} collective-permute-done((bf16[256,896]{1,0:T(8,128)(2,1)S(1)}, bf16[256,896]{1,0:T(8,128)(2,1)S(1)}, u32[]{:S(2)}, u32[]{:S(2)}) %collective-permute-start.19) | collective-permute-done | bytes 458784 | tf_op jit(solution)/shard_map/ppermute | solution.py:172
  136.6 0.5 normed.1.rows
  137.2 2.0 collective-permute-start.25
  139.3 1.3 collective-permute-start.22
  140.8 0.2 dynamic-slice_reduce_fusion.counts
  141.0 1.3 pad_maximum_fusion.1.queries
  142.2 3.3 %attend.2.first = bf16[64,1024]{1,0:T(8,128)(2,1)S(1)} custom-call(s32[2]{0:T(128)S(1)} %pad_add_fusion.pos, s32[4]{0:T(128)S(1)} %dynamic-slice_reduce_fusion.counts, bf16[256,896]{1,0:T(8,128)(2,1)S(1)} %normed.1.rows, bf16[896,1024]{1,0:T(8,128)(2,1)S(1)} %bitcast.34, bf16[896,1024]{1,0:T(8,128)(2,1)} %collective-permute-done.6.other_kv, ...), custom_call_target="tpu_custom_call" | custom-call | flops 1006632960 | bytes 4128768 | tf_op jit(solution)/shard_map/attend/pallas_call | solution.py:382
  145.5 9.5 %collective-permute-done.21.two = bf16[256,896]{1,0:T(8,128)(2,1)} collective-permute-done((bf16[256,896]{1,0:T(8,128)(2,1)S(1)}, bf16[256,896]{1,0:T(8,128)(2,1)}, u32[]{:S(2)}, u32[]{:S(2)}) %collective-permute-start.21) | collective-permute-done | bytes 458784 | tf_op jit(solution)/shard_map/ppermute | solution.py:172
  155.0 1.4 collective-permute-start.23
  156.4 1.3 collective-permute-start.24
  157.7 5.2 %attend.3 = (bf16[3,64,1024]{2,1,0:T(8,128)(2,1)S(1)}, bf16[64,1024]{1,0:T(8,128)(2,1)S(1)}) custom-call(s32[2]{0:T(128)S(1)} %pad_add_fusion.pos, s32[4]{0:T(128)S(1)} %dynamic-slice_reduce_fusion.counts, bf16[256,896]{1,0:T(8,128)(2,1)} %collective-permute-done.25.one, bf16[256,896]{1,0:T(8,128)(2,1)} %collective-permute-done.21.two, ...), custom_call_target="tpu_custom_call" | custom-call | flops 2013265920 | bytes 4587520 | tf_op jit(solution)/shard_map/attend/pallas_call | solution.py:382
  162.9 0.7 copy-done.4
  163.6 1.3 collective-permute-start.26
  165.0 2.1 %collective-permute-done.24.far = bf16[256,896]{1,0:T(8,128)(2,1)} collective-permute-done((bf16[256,896]{1,0:T(8,128)(2,1)}, bf16[256,896]{1,0:T(8,128)(2,1)}, u32[]{:S(2)}, u32[]{:S(2)}) %collective-permute-start.24) | collective-permute-done | bytes 458784 | tf_op jit(solution)/shard_map/ppermute | solution.py:172
  167.1 1.0 copy-done.5
  168.1 7.5 %last_attend.1 = (bf16[64,4096]{1,0:T(8,128)(2,1)S(1)}, bf16[64,4096]{1,0:T(8,128)(2,1)S(1)}, bf16[64,4096]{1,0:T(8,128)(2,1)S(1)}, bf16[64,4096]{1,0:T(8,128)(2,1)S(1)}, bf16[64,1024]{1,0:T(8,128)(2,1)S(1)}) custom-call(s32[2]{0:T(128)S(1)} %pad_add_fusion.pos, s32[4]{0:T(128)S(1)} %dynamic-slice_reduce_fusion.counts, ...), custom_call_target="tpu_custom_call" | custom-call | flops 3154116608 | bytes 10485760 | tf_op jit(solution)/shard_map/last_attend/pallas_call | solution.py:442
  175.6 3.2 %collective-permute-start.29 = (bf16[64,4096]{1,0:T(8,128)(2,1)S(1)}, bf16[64,4096]{1,0:T(8,128)(2,1)S(1)}, u32[]{:S(2)}, u32[]{:S(2)}) collective-permute-start(bf16[64,4096]{1,0:T(8,128)(2,1)S(1)} %get-tuple-element.98), channel_id=1, source_target_pairs={{0,2},{1,3},{6,4},{7,5},{8,10},{9,11},{14,12},{15,13},{16,18},{17,... | collective-permute-start | bytes 1572872 | tf_op jit(solution)/shard_map/ppermute | solution.py:172
  178.9 0.7 collective-permute-start.31
  179.6 4.0 %collective-permute-start.28 = (bf16[64,4096]{1,0:T(8,128)(2,1)S(1)}, bf16[64,4096]{1,0:T(8,128)(2,1)S(1)}, u32[]{:S(2)}, u32[]{:S(2)}) collective-permute-start(bf16[64,4096]{1,0:T(8,128)(2,1)S(1)} %get-tuple-element.97), channel_id=1, source_target_pairs={{0,4},{1,5},{6,2},{7,3},{8,12},{9,13},{14,10},{15,11},{16,20},{17,... | collective-permute-start | bytes 1572872 | tf_op jit(solution)/shard_map/ppermute | solution.py:172
  183.6 5.7 %collective-permute-done.29 = bf16[64,4096]{1,0:T(8,128)(2,1)S(1)} collective-permute-done((bf16[64,4096]{1,0:T(8,128)(2,1)S(1)}, bf16[64,4096]{1,0:T(8,128)(2,1)S(1)}, u32[]{:S(2)}, u32[]{:S(2)}) %collective-permute-start.29) | collective-permute-done | bytes 524320 | tf_op jit(solution)/shard_map/ppermute | solution.py:172
  189.3 0.1 add_convert_fusion.1
  189.4 1.3 collective-permute-start.30
  190.7 0.7 collective-permute-start.32
  191.4 3.4 %late_out.1 = bf16[64,4096]{1,0:T(8,128)(2,1)S(1)} custom-call(bf16[64,1024]{1,0:T(8,128)(2,1)S(1)} %broadcast_select_fusion.before, bf16[512,4096]{1,0:T(8,128)(2,1)S(1)} %copy-done.1, bf16[512,4096]{1,0:T(8,128)(2,1)} %collective-permute-done.7.refs_3_.other_w), custom_call_target="tpu_custom_call" | custom-call | flops 536870912 | bytes 8388608 | tf_op jit(solution)/shard_map/late_out/pallas_call | solution.py:478
  194.9 5.6 %collective-permute-done.27 = bf16[64,4096]{1,0:T(8,128)(2,1)S(1)} collective-permute-done((bf16[64,4096]{1,0:T(8,128)(2,1)S(1)}, bf16[64,4096]{1,0:T(8,128)(2,1)S(1)}, u32[]{:S(2)}, u32[]{:S(2)}) %collective-permute-start.27) | collective-permute-done | bytes 524320 | tf_op jit(solution)/shard_map/ppermute | solution.py:172
  200.6 3.1 %collective-permute-done.30 = bf16[64,4096]{1,0:T(8,128)(2,1)S(1)} collective-permute-done((bf16[64,4096]{1,0:T(8,128)(2,1)S(1)}, bf16[64,4096]{1,0:T(8,128)(2,1)S(1)}, u32[]{:S(2)}, u32[]{:S(2)}) %collective-permute-start.30) | collective-permute-done | bytes 524320 | tf_op jit(solution)/shard_map/ppermute | solution.py:172
  203.7 0.4 add_convert_fusion
  204.3 0.8 copy.20
  205.1 1.0 collective-permute-done.33
  206.1 0.1 slice.48
  206.2 0.8 pad_maximum_fusion.3
  (72 shorter events, 2.1 us)
Async XLA Ops:
  0.6 6.7 %copy-start = (bf16[16,16,896]{2,1,0:T(8,128)(2,1)S(1)}, bf16[16,16,896]{2,1,0:T(8,128)(2,1)}, u32[]{:S(2)}) copy-start(bf16[16,16,896]{2,1,0:T(8,128)(2,1)} %param.11) | copy-start | bytes 1376260
  0.6 27.7 %collective-permute-start = (bf16[64,4096]{1,0:T(8,128)(2,1)}, bf16[64,4096]{1,0:T(8,128)(2,1)}, u32[]{:S(2)}, u32[]{:S(2)}) collective-permute-start(bf16[64,4096]{1,0:T(8,128)(2,1)} %param.10), channel_id=1, source_target_pairs={{0,4},{1,5},{2,6},{3,7},{4,0},{5,1},{6,2},{7,3},{8,12},{9,13},{10,... | collective-permute-start | bytes 1572872 | tf_op jit(solution)/shard_map/ppermute | solution.py:172
  4.7 23.7 %collective-permute-start.1 = (bf16[64,4096]{1,0:T(8,128)(2,1)}, bf16[64,4096]{1,0:T(8,128)(2,1)S(1)}, u32[]{:S(2)}, u32[]{:S(2)}) collective-permute-start(bf16[64,4096]{1,0:T(8,128)(2,1)} %param.10), channel_id=1, source_target_pairs={{0,2},{1,3},{2,0},{3,1},{4,6},{5,7},{6,4},{7,5},{8,10},{9,11},{10,... | collective-permute-start | bytes 1572872 | tf_op jit(solution)/shard_map/ppermute | solution.py:172
  8.0 1.6 collective-permute-start.2
  28.4 2.0 copy-start.7
  28.4 20.6 %collective-permute-start.7 = (bf16[512,4096]{1,0:T(8,128)(2,1)}, bf16[512,4096]{1,0:T(8,128)(2,1)}, u32[]{:S(2)}, u32[]{:S(2)}) collective-permute-start(bf16[512,4096]{1,0:T(8,128)(2,1)} %own_w), channel_id=1, source_target_pairs={{0,1},{1,0},{2,3},{3,2},{4,5},{5,4},{6,7},{7,6},{8,9},{9,8},{10,11... | collective-permute-start | bytes 12582920 | tf_op jit(solution)/shard_map/ppermute | solution.py:165
  28.4 4.7 %collective-permute-start.3 = (bf16[64,4096]{1,0:T(8,128)(2,1)}, bf16[64,4096]{1,0:T(8,128)(2,1)S(1)}, u32[]{:S(2)}, u32[]{:S(2)}) collective-permute-start(bf16[64,4096]{1,0:T(8,128)(2,1)} %param.10), channel_id=1, source_target_pairs={{2,4},{3,5},{4,2},{5,3},{10,12},{11,13},{12,10},{13,11},{18,20},{1... | collective-permute-start | bytes 1572872 | tf_op jit(solution)/shard_map/ppermute | solution.py:172
  29.1 17.1 %collective-permute-start.4 = (bf16[64,4096]{1,0:T(8,128)(2,1)}, bf16[64,4096]{1,0:T(8,128)(2,1)}, u32[]{:S(2)}, u32[]{:S(2)}) collective-permute-start(bf16[64,4096]{1,0:T(8,128)(2,1)} %collective-permute-done), channel_id=1, source_target_pairs={{2,0},{3,1},{4,6},{5,7},{10,8},{11,9},{12,14},{13,15},{18,16},{19,... | collective-permute-start | bytes 1572872 | tf_op jit(solution)/shard_map/ppermute | solution.py:172
  32.4 16.6 %collective-permute-start.6 = (bf16[896,1024]{1,0:T(8,128)(2,1)S(1)}, bf16[896,1024]{1,0:T(8,128)(2,1)}, u32[]{:S(2)}, u32[]{:S(2)}) collective-permute-start(bf16[896,1024]{1,0:T(8,128)(2,1)S(1)} %bitcast.33), channel_id=1, source_target_pairs={{0,1},{1,0},{2,3},{3,2},{4,5},{5,4},{6,7},{7,6},{8,9},{9,8},{10,11... | collective-permute-start | bytes 5505032 | tf_op jit(solution)/shard_map/ppermute | solution.py:165
  33.0 16.0 %collective-permute-start.5 = (bf16[512,896]{1,0:T(8,128)(2,1)}, bf16[512,896]{1,0:T(8,128)(2,1)S(1)}, u32[]{:S(2)}, u32[]{:S(2)}) collective-permute-start(bf16[512,896]{1,0:T(8,128)(2,1)} %refs_8_.1), channel_id=1, source_target_pairs={{0,1},{1,0},{2,3},{3,2},{4,5},{5,4},{6,7},{7,6},{8,9},{9,8},{10,11... | collective-permute-start | bytes 2752520 | tf_op jit(solution)/shard_map/ppermute | solution.py:165
  47.3 1.8 copy-start.2
  49.0 4.2 %collective-permute-start.8 = (bf16[4,64,4096]{2,1,0:T(8,128)(2,1)S(1)}, bf16[4,64,4096]{2,1,0:T(8,128)(2,1)S(1)}, u32[]{:S(2)}, u32[]{:S(2)}) collective-permute-start(bf16[4,64,4096]{2,1,0:T(8,128)(2,1)S(1)} %pad_maximum_fusion.own), channel_id=1, source_target_pairs={{0,1},{1,0},{2,3},{3,2},{4,5},{5,4},{6,7},{7,6},{8,9},{9,8},{10,11... | collective-permute-start | bytes 6291464 | tf_op jit(solution)/shard_map/ppermute | solution.py:165
  49.1 24.0 %collective-permute-start.11 = (bf16[896,512]{1,0:T(8,128)(2,1)S(1)}, bf16[896,512]{1,0:T(8,128)(2,1)S(1)}, u32[]{:S(2)}, u32[]{:S(2)}) collective-permute-start(bf16[896,512]{1,0:T(8,128)(2,1)S(1)} %copy-done.2), channel_id=1, source_target_pairs={{0,1},{1,0},{2,3},{3,2},{4,5},{5,4},{6,7},{7,6},{8,9},{9,8},{10,11... | collective-permute-start | bytes 2752520 | tf_op jit(solution)/shard_map/ppermute | solution.py:165
  49.7 23.3 %collective-permute-start.9 = (bf16[2,4,32,896]{3,2,1,0:T(8,128)(2,1)S(1)}, bf16[2,4,32,896]{3,2,1,0:T(8,128)(2,1)S(1)}, u32[]{:S(2)}, u32[]{:S(2)}) collective-permute-start(bf16[2,4,32,896]{3,2,1,0:T(8,128)(2,1)S(1)} %pad_maximum_fusion.4.refs_0_), channel_id=1, source_target_pairs={{0,4},{1,5},{2,6},{3,7},{4,0},{5,1},{6,2},{7,3},{8,12},{9,13},{10,... | collective-permute-start | bytes 1376264 | tf_op jit(solution)/shard_map/ppermute | solution.py:172
  49.7 23.4 %collective-permute-start.10 = (bf16[2,4,32,896]{3,2,1,0:T(8,128)(2,1)S(1)}, bf16[2,4,32,896]{3,2,1,0:T(8,128)(2,1)S(1)}, u32[]{:S(2)}, u32[]{:S(2)}) collective-permute-start(bf16[2,4,32,896]{3,2,1,0:T(8,128)(2,1)S(1)} %pad_maximum_fusion.4.refs_0_), channel_id=1, source_target_pairs={{0,2},{1,3},{2,0},{3,1},{4,6},{5,7},{6,4},{7,5},{8,10},{9,11},{10,... | collective-permute-start | bytes 1376264 | tf_op jit(solution)/shard_map/ppermute | solution.py:172
  63.0 25.7 %copy-start.3 = (bf16[512,896]{1,0:T(8,128)(2,1)S(1)}, bf16[512,896]{1,0:T(8,128)(2,1)}, u32[]{:S(2)}) copy-start(bf16[512,896]{1,0:T(8,128)(2,1)} %refs_8_.1) | copy-start | bytes 2752516
  73.1 2.7 %collective-permute-start.15 = (bf16[4,64,1536]{2,1,0:T(8,128)(2,1)S(1)}, bf16[4,64,1536]{2,1,0:T(8,128)(2,1)S(1)}, u32[]{:S(2)}, u32[]{:S(2)}) collective-permute-start(bf16[4,64,1536]{2,1,0:T(8,128)(2,1)S(1)} %get-tuple-element.65), channel_id=1, source_target_pairs={{0,1},{1,0},{2,3},{3,2},{4,5},{5,4},{6,7},{7,6},{8,9},{9,8},{10,11... | collective-permute-start | bytes 2359304 | tf_op jit(solution)/shard_map/ppermute | solution.py:165
  73.1 2.6 %collective-permute-start.14 = (bf16[4,64,512]{2,1,0:T(8,128)(2,1)S(1)}, bf16[4,64,512]{2,1,0:T(8,128)(2,1)S(1)}, u32[]{:S(2)}, u32[]{:S(2)}) collective-permute-start(bf16[4,64,512]{2,1,0:T(8,128)(2,1)S(1)} %slice.31), channel_id=1, source_target_pairs={{0,1},{1,0},{2,3},{3,2},{4,5},{5,4},{6,7},{7,6},{8,9},{9,8},{10,11... | collective-permute-start | bytes 786440 | tf_op jit(solution)/shard_map/ppermute | solution.py:165
  73.7 2.2 %collective-permute-start.12 = (bf16[2,4,32,896]{3,2,1,0:T(8,128)(2,1)S(1)}, bf16[2,4,32,896]{3,2,1,0:T(8,128)(2,1)S(1)}, u32[]{:S(2)}, u32[]{:S(2)}) collective-permute-start(bf16[2,4,32,896]{3,2,1,0:T(8,128)(2,1)S(1)} %pad_maximum_fusion.4.refs_0_), channel_id=1, source_target_pairs={{2,4},{3,5},{4,2},{5,3},{10,12},{11,13},{12,10},{13,11},{18,20},{1... | collective-permute-start | bytes 1376264 | tf_op jit(solution)/shard_map/ppermute | solution.py:172
  74.4 14.3 %collective-permute-start.13 = (bf16[2,4,32,896]{3,2,1,0:T(8,128)(2,1)S(1)}, bf16[2,4,32,896]{3,2,1,0:T(8,128)(2,1)S(1)}, u32[]{:S(2)}, u32[]{:S(2)}) collective-permute-start(bf16[2,4,32,896]{3,2,1,0:T(8,128)(2,1)S(1)} %collective-permute-done.9.refs_2_), channel_id=1, source_target_pairs={{2,0},{3,1},{4,6},{5,7},{10,8},{11,9},{12,14},{13,15},{18,16},{19,... | collective-permute-start | bytes 1376264 | tf_op jit(solution)/shard_map/ppermute | solution.py:172
  75.8 63.4 %copy-start.6 = (bf16[4,64,1024]{2,1,0:T(8,128)(2,1)}, bf16[4,64,1024]{2,1,0:T(8,128)(2,1)S(1)}, u32[]{:S(2)}) copy-start(bf16[4,64,1024]{2,1,0:T(8,128)(2,1)S(1)} %pad_maximum_fusion.2) | copy-start | bytes 1572868
  98.1 11.1 %collective-permute-start.18 = (bf16[256,896]{1,0:T(8,128)(2,1)S(1)}, bf16[256,896]{1,0:T(8,128)(2,1)S(1)}, u32[]{:S(2)}, u32[]{:S(2)}) collective-permute-start(bf16[256,896]{1,0:T(8,128)(2,1)S(1)} %get-tuple-element.82), channel_id=1, source_target_pairs={{0,2},{1,3},{6,4},{7,5},{8,10},{9,11},{14,12},{15,13},{16,18},{17,... | collective-permute-start | bytes 1376264 | tf_op jit(solution)/shard_map/ppermute | solution.py:172
  99.6 25.7 %collective-permute-start.20 = (bf16[256,896]{1,0:T(8,128)(2,1)S(1)}, bf16[256,896]{1,0:T(8,128)(2,1)S(1)}, u32[]{:S(2)}, u32[]{:S(2)}) collective-permute-start(bf16[256,896]{1,0:T(8,128)(2,1)S(1)} %get-tuple-element.82), channel_id=1, source_target_pairs={{2,4},{3,5},{4,2},{5,3},{10,12},{11,13},{12,10},{13,11},{18,20},{1... | collective-permute-start | bytes 1376264 | tf_op jit(solution)/shard_map/ppermute | solution.py:172
  100.3 10.4 %copy-start.8 = (f32[896]{0:T(1024)S(1)}, f32[896]{0:T(1024)}, u32[]{:S(2)}) copy-start(f32[896]{0:T(1024)} %param.17) | copy-start | bytes 10756
  101.2 18.4 %collective-permute-start.16 = (bf16[256,896]{1,0:T(8,128)(2,1)S(1)}, bf16[256,896]{1,0:T(8,128)(2,1)S(1)}, u32[]{:S(2)}, u32[]{:S(2)}) collective-permute-start(bf16[256,896]{1,0:T(8,128)(2,1)S(1)} %get-tuple-element.80), channel_id=1, source_target_pairs={{0,2},{1,3},{2,0},{3,1},{4,6},{5,7},{6,4},{7,5},{8,10},{9,11},{10,... | collective-permute-start | bytes 1376264 | tf_op jit(solution)/shard_map/ppermute | solution.py:172
  102.8 22.4 %collective-permute-start.17 = (bf16[256,896]{1,0:T(8,128)(2,1)S(1)}, bf16[256,896]{1,0:T(8,128)(2,1)S(1)}, u32[]{:S(2)}, u32[]{:S(2)}) collective-permute-start(bf16[256,896]{1,0:T(8,128)(2,1)S(1)} %get-tuple-element.81), channel_id=1, source_target_pairs={{0,4},{1,5},{6,2},{7,3},{8,12},{9,13},{14,10},{15,11},{16,20},{17,... | collective-permute-start | bytes 1376264 | tf_op jit(solution)/shard_map/ppermute | solution.py:172
  109.3 31.3 %copy-start.9 = (s32[32]{0:T(128)S(1)}, s32[32]{0:T(128)}, u32[]{:S(2)}) copy-start(s32[32]{0:T(128)} %param.13) | copy-start | bytes 388
  109.3 27.2 %collective-permute-start.19 = (bf16[256,896]{1,0:T(8,128)(2,1)S(1)}, bf16[256,896]{1,0:T(8,128)(2,1)S(1)}, u32[]{:S(2)}, u32[]{:S(2)}) collective-permute-start(bf16[256,896]{1,0:T(8,128)(2,1)S(1)} %add_convert_fusion.2), channel_id=1, source_target_pairs={{2,6},{3,7},{4,0},{5,1},{10,14},{11,15},{12,8},{13,9},{18,22},{19,... | collective-permute-start | bytes 1376264 | tf_op jit(solution)/shard_map/ppermute | solution.py:172
  137.1 17.9 %collective-permute-start.21 = (bf16[256,896]{1,0:T(8,128)(2,1)S(1)}, bf16[256,896]{1,0:T(8,128)(2,1)}, u32[]{:S(2)}, u32[]{:S(2)}) collective-permute-start(bf16[256,896]{1,0:T(8,128)(2,1)S(1)} %normed.1.rows), channel_id=1, source_target_pairs={{0,4},{1,5},{2,6},{3,7},{4,0},{5,1},{6,2},{7,3},{8,12},{9,13},{10,... | collective-permute-start | bytes 1376264 | tf_op jit(solution)/shard_map/ppermute | solution.py:172
  137.2 20.5 %collective-permute-start.25 = (bf16[256,896]{1,0:T(8,128)(2,1)S(1)}, bf16[256,896]{1,0:T(8,128)(2,1)}, u32[]{:S(2)}, u32[]{:S(2)}) collective-permute-start(bf16[256,896]{1,0:T(8,128)(2,1)S(1)} %normed.1.rows), channel_id=1, source_target_pairs={{0,2},{1,3},{2,0},{3,1},{4,6},{5,7},{6,4},{7,5},{8,10},{9,11},{10,... | collective-permute-start | bytes 1376264 | tf_op jit(solution)/shard_map/ppermute | solution.py:172
  139.3 1.7 collective-permute-start.22
  155.0 10.0 %collective-permute-start.23 = (bf16[256,896]{1,0:T(8,128)(2,1)S(1)}, bf16[256,896]{1,0:T(8,128)(2,1)}, u32[]{:S(2)}, u32[]{:S(2)}) collective-permute-start(bf16[256,896]{1,0:T(8,128)(2,1)S(1)} %normed.1.rows), channel_id=1, source_target_pairs={{2,4},{3,5},{4,2},{5,3},{10,12},{11,13},{12,10},{13,11},{18,20},{1... | collective-permute-start | bytes 1376264 | tf_op jit(solution)/shard_map/ppermute | solution.py:172
  156.4 10.7 %collective-permute-start.24 = (bf16[256,896]{1,0:T(8,128)(2,1)}, bf16[256,896]{1,0:T(8,128)(2,1)}, u32[]{:S(2)}, u32[]{:S(2)}) collective-permute-start(bf16[256,896]{1,0:T(8,128)(2,1)} %collective-permute-done.21.two), channel_id=1, source_target_pairs={{2,0},{3,1},{4,6},{5,7},{10,8},{11,9},{12,14},{13,15},{18,16},{19,... | collective-permute-start | bytes 1376264 | tf_op jit(solution)/shard_map/ppermute | solution.py:172
  162.9 0.7 copy-start.4
  163.6 1.3 collective-permute-start.26
  167.1 1.0 copy-start.5
  168.1 23.3 %copy-start.1 = (bf16[512,4096]{1,0:T(8,128)(2,1)S(1)}, bf16[512,4096]{1,0:T(8,128)(2,1)}, u32[]{:S(2)}) copy-start(bf16[512,4096]{1,0:T(8,128)(2,1)} %own_w) | copy-start | bytes 12582916
  175.6 13.6 %collective-permute-start.29 = (bf16[64,4096]{1,0:T(8,128)(2,1)S(1)}, bf16[64,4096]{1,0:T(8,128)(2,1)S(1)}, u32[]{:S(2)}, u32[]{:S(2)}) collective-permute-start(bf16[64,4096]{1,0:T(8,128)(2,1)S(1)} %get-tuple-element.98), channel_id=1, source_target_pairs={{0,2},{1,3},{6,4},{7,5},{8,10},{9,11},{14,12},{15,13},{16,18},{17,... | collective-permute-start | bytes 1572872 | tf_op jit(solution)/shard_map/ppermute | solution.py:172
  178.9 16.0 %collective-permute-start.31 = (bf16[64,4096]{1,0:T(8,128)(2,1)S(1)}, bf16[64,4096]{1,0:T(8,128)(2,1)S(1)}, u32[]{:S(2)}, u32[]{:S(2)}) collective-permute-start(bf16[64,4096]{1,0:T(8,128)(2,1)S(1)} %get-tuple-element.98), channel_id=1, source_target_pairs={{2,4},{3,5},{4,2},{5,3},{10,12},{11,13},{12,10},{13,11},{18,20},{1... | collective-permute-start | bytes 1572872 | tf_op jit(solution)/shard_map/ppermute | solution.py:172
  179.6 15.4 %collective-permute-start.28 = (bf16[64,4096]{1,0:T(8,128)(2,1)S(1)}, bf16[64,4096]{1,0:T(8,128)(2,1)S(1)}, u32[]{:S(2)}, u32[]{:S(2)}) collective-permute-start(bf16[64,4096]{1,0:T(8,128)(2,1)S(1)} %get-tuple-element.97), channel_id=1, source_target_pairs={{0,4},{1,5},{6,2},{7,3},{8,12},{9,13},{14,10},{15,11},{16,20},{17,... | collective-permute-start | bytes 1572872 | tf_op jit(solution)/shard_map/ppermute | solution.py:172
  183.5 17.0 %collective-permute-start.27 = (bf16[64,4096]{1,0:T(8,128)(2,1)S(1)}, bf16[64,4096]{1,0:T(8,128)(2,1)S(1)}, u32[]{:S(2)}, u32[]{:S(2)}) collective-permute-start(bf16[64,4096]{1,0:T(8,128)(2,1)S(1)} %get-tuple-element.96), channel_id=1, source_target_pairs={{0,2},{1,3},{2,0},{3,1},{4,6},{5,7},{6,4},{7,5},{8,10},{9,11},{10,... | collective-permute-start | bytes 1572872 | tf_op jit(solution)/shard_map/ppermute | solution.py:172
  189.4 14.3 %collective-permute-start.30 = (bf16[64,4096]{1,0:T(8,128)(2,1)S(1)}, bf16[64,4096]{1,0:T(8,128)(2,1)S(1)}, u32[]{:S(2)}, u32[]{:S(2)}) collective-permute-start(bf16[64,4096]{1,0:T(8,128)(2,1)S(1)} %add_convert_fusion.1), channel_id=1, source_target_pairs={{2,6},{3,7},{4,0},{5,1},{10,14},{11,15},{12,8},{13,9},{18,22},{19,... | collective-permute-start | bytes 1572872 | tf_op jit(solution)/shard_map/ppermute | solution.py:172
  190.7 0.7 collective-permute-start.32
  204.1 2.0 collective-permute-start.33

commit v6 on v5

--- a/solution.py
+++ b/solution.py
@@ -355,7 +355,7 @@
     scores = jnp.concatenate(scores, axis=0) * SCALE
     allowed = jnp.concatenate([allowed] * len(each_head), axis=0)
     scores = jnp.where(allowed, scores, -1e30)
-    raised = jnp.where(allowed, jnp.exp(scores - jnp.max(scores, axis=-1, keepdims=True)), 0.0)
+    raised = jnp.exp(scores - jnp.max(scores, axis=-1, keepdims=True))
     share = (raised / jnp.sum(raised, axis=-1, keepdims=True)).astype(BF16)
     for k, (w, h) in enumerate(each_head):
         value = kvs[w][:, heads + h : heads + h + HEAD_DIM]

time: 209 us -> 209 us (level)
  no operation moved by 1% of the time
where the time goes in v6:
time: 209 us; the launch traced here: 207 us
  waiting for transfers between devices  112 us (54%)
  starting transfers between devices  40.2 us (19%)
  Pallas kernels  40 us (19%)
  local copies, waits for them, and re-layouts  6.89 us (3%)
  other arithmetic  6.62 us (3%)
    ppermute x22, waiting for transfers between devices, hop(): lax.ppermute(x, 'nbr', [(2 * z + c, 2 * (z ^ flip) + c) for z in chips fo...  110 us
    ppermute x22, starting transfers between devices, hop(): lax.ppermute(x, 'nbr', [(2 * z + c, 2 * (z ^ flip) + c) for z in chips fo...  34.9 us
    pallas_call x2, Pallas kernels, encode(): pl.pallas_call(functools.partial(enc_kernel, ahead), grid=(1,), in_specs=...  10.2 us
    pallas_call x1, Pallas kernels, project(): pl.pallas_call(proj_kernel, in_specs=[SMEM, VMEM, VMEM, HBM], out_specs=[...  9.73 us
    pallas_call x2, Pallas kernels, attend(): pl.pallas_call(attend_more_kernel if earlier else attend_kernel, in_specs...  8.39 us
    pallas_call x1, Pallas kernels, last_attend(): pl.pallas_call(last_kernel, in_specs=[SMEM, SMEM] + [VMEM] * 7 + [HBM, AN...  7.68 us
  transfers between devices with their start and end apart: 34, of which 19 were waited for; matrix products, arithmetic and copies ran while one was open for 5% of the time, Pallas kernels for 11%

profile of v6, /device:TPU:0, one launch (start us, length us, event | category | flops | bytes accessed | tf_op | source)
XLA Modules:
  0.0 207.2 jit_solution(2572542800149836003)
XLA Ops:
  0.6 4.1 %collective-permute-start = (bf16[64,4096]{1,0:T(8,128)(2,1)}, bf16[64,4096]{1,0:T(8,128)(2,1)}, u32[]{:S(2)}, u32[]{:S(2)}) collective-permute-start(bf16[64,4096]{1,0:T(8,128)(2,1)} %param.10), channel_id=1, source_target_pairs={{0,4},{1,5},{2,6},{3,7},{4,0},{5,1},{6,2},{7,3},{8,12},{9,13},{10,... | collective-permute-start | bytes 1572872 | tf_op jit(solution)/shard_map/ppermute | solution.py:172
  4.7 1.6 collective-permute-start.1
  6.3 0.7 broadcast_subtract_fusion
  7.4 0.6 gather_fusion.1
  8.3 0.6 gather_fusion
  8.8 0.7 collective-permute-done.2
  9.6 18.8 %collective-permute-done = bf16[64,4096]{1,0:T(8,128)(2,1)} collective-permute-done((bf16[64,4096]{1,0:T(8,128)(2,1)}, bf16[64,4096]{1,0:T(8,128)(2,1)}, u32[]{:S(2)}, u32[]{:S(2)}) %collective-permute-start) | collective-permute-done | bytes 524320 | tf_op jit(solution)/shard_map/ppermute | solution.py:172
  28.4 0.7 collective-permute-start.3
  29.1 1.3 collective-permute-start.4
  30.4 2.0 copy.21
  32.4 0.6 collective-permute-start.6
  33.1 13.1 %collective-permute-done.4 = bf16[64,4096]{1,0:T(8,128)(2,1)} collective-permute-done((bf16[64,4096]{1,0:T(8,128)(2,1)}, bf16[64,4096]{1,0:T(8,128)(2,1)}, u32[]{:S(2)}, u32[]{:S(2)}) %collective-permute-start.4) | collective-permute-done | bytes 524320 | tf_op jit(solution)/shard_map/ppermute | solution.py:172
  46.2 1.1 select_bitcast_fusion
  47.3 1.7 pad_maximum_fusion.own
  49.1 0.5 collective-permute-start.11
  49.7 3.4 %collective-permute-start.10 = (bf16[2,4,32,896]{3,2,1,0:T(8,128)(2,1)S(1)}, bf16[2,4,32,896]{3,2,1,0:T(8,128)(2,1)S(1)}, u32[]{:S(2)}, u32[]{:S(2)}) collective-permute-start(bf16[2,4,32,896]{3,2,1,0:T(8,128)(2,1)S(1)} %pad_maximum_fusion.4.refs_0_), channel_id=1, source_target_pairs={{0,2},{1,3},{2,0},{3,1},{4,6},{5,7},{6,4},{7,5},{8,10},{9,11},{10,... | collective-permute-start | bytes 1376264 | tf_op jit(solution)/shard_map/ppermute | solution.py:172
  53.1 0.2 collective-permute-done.8.other
  53.2 9.7 %project.1 = (bf16[4,64,1536]{2,1,0:T(8,128)(2,1)S(1)}, bf16[4,64,1536]{2,1,0:T(8,128)(2,1)S(1)}) custom-call(s32[2]{0:T(128)S(1)} %pad_add_fusion.pos, bf16[4,64,4096]{2,1,0:T(8,128)(2,1)S(1)} %pad_maximum_fusion.own, bf16[4,64,4096]{2,1,0:T(8,128)(2,1)S(1)} %collective-permute-done.8.other, bf16[3,4096,512]{2,1,0:T(8,128)(2,1)} %bitcast.54), custom_call_target="tpu_custom_call" | custom-call | flops 6442450944 | bytes 16777216 | tf_op jit(solution)/shard_map/project/pallas_call | solution.py:231
  63.0 10.0 %collective-permute-done.9.refs_2_ = bf16[2,4,32,896]{3,2,1,0:T(8,128)(2,1)S(1)} collective-permute-done((bf16[2,4,32,896]{3,2,1,0:T(8,128)(2,1)S(1)}, bf16[2,4,32,896]{3,2,1,0:T(8,128)(2,1)S(1)}, u32[]{:S(2)}, u32[]{:S(2)}) %collective-permute-start.9) | collective-permute-done | bytes 458784 | tf_op jit(solution)/shard_map/ppermute | solution.py:172
  73.1 0.6 collective-permute-start.14
  73.7 0.7 collective-permute-start.12
  74.4 1.3 collective-permute-start.13
  75.9 12.8 %collective-permute-done.13.refs_4_ = bf16[2,4,32,896]{3,2,1,0:T(8,128)(2,1)S(1)} collective-permute-done((bf16[2,4,32,896]{3,2,1,0:T(8,128)(2,1)S(1)}, bf16[2,4,32,896]{3,2,1,0:T(8,128)(2,1)S(1)}, u32[]{:S(2)}, u32[]{:S(2)}) %collective-permute-start.13) | collective-permute-done | bytes 458784 | tf_op jit(solution)/shard_map/ppermute | solution.py:172
  88.7 9.3 %encode.2 = (bf16[256,896]{1,0:T(8,128)(2,1)S(1)}, bf16[256,896]{1,0:T(8,128)(2,1)S(1)}, bf16[256,896]{1,0:T(8,128)(2,1)S(1)}, bf16[256,896]{1,0:T(8,128)(2,1)S(1)}, bf16[256,896]{1,0:T(8,128)(2,1)S(1)}) custom-call(s32[2]{0:T(128)S(1)} %pad_add_fusion.pos, bf16[2,4,32,896]{3,2,1,0:T(8,128)(2,1)S(1)} %pad_maximum_fusion.4.refs_0_, ...), custom_call_target="tpu_custom_call" | custom-call | flops 2013265920 | bytes 5505024 | tf_op jit(solution)/shard_map/encode/pallas_call | solution.py:304
  98.1 1.5 collective-permute-start.18
  99.6 0.7 collective-permute-start.20
  100.3 0.9 encode.3
  101.2 1.6 collective-permute-start.16
  102.8 2.8 %collective-permute-start.17 = (bf16[256,896]{1,0:T(8,128)(2,1)S(1)}, bf16[256,896]{1,0:T(8,128)(2,1)S(1)}, u32[]{:S(2)}, u32[]{:S(2)}) collective-permute-start(bf16[256,896]{1,0:T(8,128)(2,1)S(1)} %get-tuple-element.81), channel_id=1, source_target_pairs={{0,4},{1,5},{6,2},{7,3},{8,12},{9,13},{14,10},{15,11},{16,20},{17,... | collective-permute-start | bytes 1376264 | tf_op jit(solution)/shard_map/ppermute | solution.py:172
  105.6 3.6 %collective-permute-done.18 = bf16[256,896]{1,0:T(8,128)(2,1)S(1)} collective-permute-done((bf16[256,896]{1,0:T(8,128)(2,1)S(1)}, bf16[256,896]{1,0:T(8,128)(2,1)S(1)}, u32[]{:S(2)}, u32[]{:S(2)}) %collective-permute-start.18) | collective-permute-done | bytes 458784 | tf_op jit(solution)/shard_map/ppermute | solution.py:172
  109.3 1.3 collective-permute-start.19
  110.7 8.9 %collective-permute-done.16.refs_1_ = bf16[256,896]{1,0:T(8,128)(2,1)S(1)} collective-permute-done((bf16[256,896]{1,0:T(8,128)(2,1)S(1)}, bf16[256,896]{1,0:T(8,128)(2,1)S(1)}, u32[]{:S(2)}, u32[]{:S(2)}) %collective-permute-start.16) | collective-permute-done | bytes 458784 | tf_op jit(solution)/shard_map/ppermute | solution.py:172
  119.6 5.7 %collective-permute-done.17.refs_2_ = bf16[256,896]{1,0:T(8,128)(2,1)S(1)} collective-permute-done((bf16[256,896]{1,0:T(8,128)(2,1)S(1)}, bf16[256,896]{1,0:T(8,128)(2,1)S(1)}, u32[]{:S(2)}, u32[]{:S(2)}) %collective-permute-start.17) | collective-permute-done | bytes 458784 | tf_op jit(solution)/shard_map/ppermute | solution.py:172
  125.2 11.4 %collective-permute-done.19.refs_3_ = bf16[256,896]{1,0:T(8,128)(2,1)S(1)} collective-permute-done((bf16[256,896]{1,0:T(8,128)(2,1)S(1)}, bf16[256,896]{1,0:T(8,128)(2,1)S(1)}, u32[]{:S(2)}, u32[]{:S(2)}) %collective-permute-start.19) | collective-permute-done | bytes 458784 | tf_op jit(solution)/shard_map/ppermute | solution.py:172
  136.6 0.5 normed.1.rows
  137.2 2.0 collective-permute-start.25
  139.3 1.3 collective-permute-start.22
  140.8 0.2 dynamic-slice_reduce_fusion.counts
  141.0 1.3 pad_maximum_fusion.1.queries
  142.2 3.3 %attend.2.first = bf16[64,1024]{1,0:T(8,128)(2,1)S(1)} custom-call(s32[2]{0:T(128)S(1)} %pad_add_fusion.pos, s32[4]{0:T(128)S(1)} %dynamic-slice_reduce_fusion.counts, bf16[256,896]{1,0:T(8,128)(2,1)S(1)} %normed.1.rows, bf16[896,1024]{1,0:T(8,128)(2,1)S(1)} %bitcast.34, bf16[896,1024]{1,0:T(8,128)(2,1)} %collective-permute-done.6.other_kv, ...), custom_call_target="tpu_custom_call" | custom-call | flops 1006632960 | bytes 4128768 | tf_op jit(solution)/shard_map/attend/pallas_call | solution.py:382
  145.5 9.5 %collective-permute-done.21.two = bf16[256,896]{1,0:T(8,128)(2,1)} collective-permute-done((bf16[256,896]{1,0:T(8,128)(2,1)S(1)}, bf16[256,896]{1,0:T(8,128)(2,1)}, u32[]{:S(2)}, u32[]{:S(2)}) %collective-permute-start.21) | collective-permute-done | bytes 458784 | tf_op jit(solution)/shard_map/ppermute | solution.py:172
  155.0 1.4 collective-permute-start.23
  156.4 1.3 collective-permute-start.24
  157.7 5.1 %attend.3 = (bf16[3,64,1024]{2,1,0:T(8,128)(2,1)S(1)}, bf16[64,1024]{1,0:T(8,128)(2,1)S(1)}) custom-call(s32[2]{0:T(128)S(1)} %pad_add_fusion.pos, s32[4]{0:T(128)S(1)} %dynamic-slice_reduce_fusion.counts, bf16[256,896]{1,0:T(8,128)(2,1)} %collective-permute-done.25.one, bf16[256,896]{1,0:T(8,128)(2,1)} %collective-permute-done.21.two, ...), custom_call_target="tpu_custom_call" | custom-call | flops 2013265920 | bytes 4587520 | tf_op jit(solution)/shard_map/attend/pallas_call | solution.py:382
  162.9 0.7 copy-done.4
  163.6 1.3 collective-permute-start.26
  164.9 2.1 %collective-permute-done.24.far = bf16[256,896]{1,0:T(8,128)(2,1)} collective-permute-done((bf16[256,896]{1,0:T(8,128)(2,1)}, bf16[256,896]{1,0:T(8,128)(2,1)}, u32[]{:S(2)}, u32[]{:S(2)}) %collective-permute-start.24) | collective-permute-done | bytes 458784 | tf_op jit(solution)/shard_map/ppermute | solution.py:172
  167.1 1.0 copy-done.5
  168.1 7.7 %last_attend.1 = (bf16[64,4096]{1,0:T(8,128)(2,1)S(1)}, bf16[64,4096]{1,0:T(8,128)(2,1)S(1)}, bf16[64,4096]{1,0:T(8,128)(2,1)S(1)}, bf16[64,4096]{1,0:T(8,128)(2,1)S(1)}, bf16[64,1024]{1,0:T(8,128)(2,1)S(1)}) custom-call(s32[2]{0:T(128)S(1)} %pad_add_fusion.pos, s32[4]{0:T(128)S(1)} %dynamic-slice_reduce_fusion.counts, ...), custom_call_target="tpu_custom_call" | custom-call | flops 3154116608 | bytes 10485760 | tf_op jit(solution)/shard_map/last_attend/pallas_call | solution.py:442
  175.8 3.2 %collective-permute-start.29 = (bf16[64,4096]{1,0:T(8,128)(2,1)S(1)}, bf16[64,4096]{1,0:T(8,128)(2,1)S(1)}, u32[]{:S(2)}, u32[]{:S(2)}) collective-permute-start(bf16[64,4096]{1,0:T(8,128)(2,1)S(1)} %get-tuple-element.98), channel_id=1, source_target_pairs={{0,2},{1,3},{6,4},{7,5},{8,10},{9,11},{14,12},{15,13},{16,18},{17,... | collective-permute-start | bytes 1572872 | tf_op jit(solution)/shard_map/ppermute | solution.py:172
  179.0 0.7 collective-permute-start.31
  179.7 4.0 %collective-permute-start.28 = (bf16[64,4096]{1,0:T(8,128)(2,1)S(1)}, bf16[64,4096]{1,0:T(8,128)(2,1)S(1)}, u32[]{:S(2)}, u32[]{:S(2)}) collective-permute-start(bf16[64,4096]{1,0:T(8,128)(2,1)S(1)} %get-tuple-element.97), channel_id=1, source_target_pairs={{0,4},{1,5},{6,2},{7,3},{8,12},{9,13},{14,10},{15,11},{16,20},{17,... | collective-permute-start | bytes 1572872 | tf_op jit(solution)/shard_map/ppermute | solution.py:172
  183.7 5.7 %collective-permute-done.29 = bf16[64,4096]{1,0:T(8,128)(2,1)S(1)} collective-permute-done((bf16[64,4096]{1,0:T(8,128)(2,1)S(1)}, bf16[64,4096]{1,0:T(8,128)(2,1)S(1)}, u32[]{:S(2)}, u32[]{:S(2)}) %collective-permute-start.29) | collective-permute-done | bytes 524320 | tf_op jit(solution)/shard_map/ppermute | solution.py:172
  189.4 0.1 add_convert_fusion.1
  189.5 1.3 collective-permute-start.30
  190.8 0.7 collective-permute-start.32
  191.6 3.4 %late_out.1 = bf16[64,4096]{1,0:T(8,128)(2,1)S(1)} custom-call(bf16[64,1024]{1,0:T(8,128)(2,1)S(1)} %broadcast_select_fusion.before, bf16[512,4096]{1,0:T(8,128)(2,1)S(1)} %copy-done.1, bf16[512,4096]{1,0:T(8,128)(2,1)} %collective-permute-done.7.refs_3_.other_w), custom_call_target="tpu_custom_call" | custom-call | flops 536870912 | bytes 8388608 | tf_op jit(solution)/shard_map/late_out/pallas_call | solution.py:478
  195.1 5.6 %collective-permute-done.27 = bf16[64,4096]{1,0:T(8,128)(2,1)S(1)} collective-permute-done((bf16[64,4096]{1,0:T(8,128)(2,1)S(1)}, bf16[64,4096]{1,0:T(8,128)(2,1)S(1)}, u32[]{:S(2)}, u32[]{:S(2)}) %collective-permute-start.27) | collective-permute-done | bytes 524320 | tf_op jit(solution)/shard_map/ppermute | solution.py:172
  200.7 3.1 %collective-permute-done.30 = bf16[64,4096]{1,0:T(8,128)(2,1)S(1)} collective-permute-done((bf16[64,4096]{1,0:T(8,128)(2,1)S(1)}, bf16[64,4096]{1,0:T(8,128)(2,1)S(1)}, u32[]{:S(2)}, u32[]{:S(2)}) %collective-permute-start.30) | collective-permute-done | bytes 524320 | tf_op jit(solution)/shard_map/ppermute | solution.py:172
  203.8 0.4 add_convert_fusion
  204.4 0.8 copy.20
  205.2 1.0 collective-permute-done.33
  206.2 0.1 slice.48
  206.4 0.8 pad_maximum_fusion.3
  (72 shorter events, 2.1 us)
Async XLA Ops:
  0.6 6.7 %copy-start = (bf16[16,16,896]{2,1,0:T(8,128)(2,1)S(1)}, bf16[16,16,896]{2,1,0:T(8,128)(2,1)}, u32[]{:S(2)}) copy-start(bf16[16,16,896]{2,1,0:T(8,128)(2,1)} %param.11) | copy-start | bytes 1376260
  0.6 27.7 %collective-permute-start = (bf16[64,4096]{1,0:T(8,128)(2,1)}, bf16[64,4096]{1,0:T(8,128)(2,1)}, u32[]{:S(2)}, u32[]{:S(2)}) collective-permute-start(bf16[64,4096]{1,0:T(8,128)(2,1)} %param.10), channel_id=1, source_target_pairs={{0,4},{1,5},{2,6},{3,7},{4,0},{5,1},{6,2},{7,3},{8,12},{9,13},{10,... | collective-permute-start | bytes 1572872 | tf_op jit(solution)/shard_map/ppermute | solution.py:172
  4.7 23.7 %collective-permute-start.1 = (bf16[64,4096]{1,0:T(8,128)(2,1)}, bf16[64,4096]{1,0:T(8,128)(2,1)S(1)}, u32[]{:S(2)}, u32[]{:S(2)}) collective-permute-start(bf16[64,4096]{1,0:T(8,128)(2,1)} %param.10), channel_id=1, source_target_pairs={{0,2},{1,3},{2,0},{3,1},{4,6},{5,7},{6,4},{7,5},{8,10},{9,11},{10,... | collective-permute-start | bytes 1572872 | tf_op jit(solution)/shard_map/ppermute | solution.py:172
  8.0 1.6 collective-permute-start.2
  28.4 2.0 copy-start.7
  28.4 20.6 %collective-permute-start.7 = (bf16[512,4096]{1,0:T(8,128)(2,1)}, bf16[512,4096]{1,0:T(8,128)(2,1)}, u32[]{:S(2)}, u32[]{:S(2)}) collective-permute-start(bf16[512,4096]{1,0:T(8,128)(2,1)} %own_w), channel_id=1, source_target_pairs={{0,1},{1,0},{2,3},{3,2},{4,5},{5,4},{6,7},{7,6},{8,9},{9,8},{10,11... | collective-permute-start | bytes 12582920 | tf_op jit(solution)/shard_map/ppermute | solution.py:165
  28.4 4.7 %collective-permute-start.3 = (bf16[64,4096]{1,0:T(8,128)(2,1)}, bf16[64,4096]{1,0:T(8,128)(2,1)S(1)}, u32[]{:S(2)}, u32[]{:S(2)}) collective-permute-start(bf16[64,4096]{1,0:T(8,128)(2,1)} %param.10), channel_id=1, source_target_pairs={{2,4},{3,5},{4,2},{5,3},{10,12},{11,13},{12,10},{13,11},{18,20},{1... | collective-permute-start | bytes 1572872 | tf_op jit(solution)/shard_map/ppermute | solution.py:172
  29.1 17.1 %collective-permute-start.4 = (bf16[64,4096]{1,0:T(8,128)(2,1)}, bf16[64,4096]{1,0:T(8,128)(2,1)}, u32[]{:S(2)}, u32[]{:S(2)}) collective-permute-start(bf16[64,4096]{1,0:T(8,128)(2,1)} %collective-permute-done), channel_id=1, source_target_pairs={{2,0},{3,1},{4,6},{5,7},{10,8},{11,9},{12,14},{13,15},{18,16},{19,... | collective-permute-start | bytes 1572872 | tf_op jit(solution)/shard_map/ppermute | solution.py:172
  32.4 16.6 %collective-permute-start.6 = (bf16[896,1024]{1,0:T(8,128)(2,1)S(1)}, bf16[896,1024]{1,0:T(8,128)(2,1)}, u32[]{:S(2)}, u32[]{:S(2)}) collective-permute-start(bf16[896,1024]{1,0:T(8,128)(2,1)S(1)} %bitcast.33), channel_id=1, source_target_pairs={{0,1},{1,0},{2,3},{3,2},{4,5},{5,4},{6,7},{7,6},{8,9},{9,8},{10,11... | collective-permute-start | bytes 5505032 | tf_op jit(solution)/shard_map/ppermute | solution.py:165
  33.0 16.0 %collective-permute-start.5 = (bf16[512,896]{1,0:T(8,128)(2,1)}, bf16[512,896]{1,0:T(8,128)(2,1)S(1)}, u32[]{:S(2)}, u32[]{:S(2)}) collective-permute-start(bf16[512,896]{1,0:T(8,128)(2,1)} %refs_8_.1), channel_id=1, source_target_pairs={{0,1},{1,0},{2,3},{3,2},{4,5},{5,4},{6,7},{7,6},{8,9},{9,8},{10,11... | collective-permute-start | bytes 2752520 | tf_op jit(solution)/shard_map/ppermute | solution.py:165
  47.3 1.8 copy-start.2
  49.0 4.2 %collective-permute-start.8 = (bf16[4,64,4096]{2,1,0:T(8,128)(2,1)S(1)}, bf16[4,64,4096]{2,1,0:T(8,128)(2,1)S(1)}, u32[]{:S(2)}, u32[]{:S(2)}) collective-permute-start(bf16[4,64,4096]{2,1,0:T(8,128)(2,1)S(1)} %pad_maximum_fusion.own), channel_id=1, source_target_pairs={{0,1},{1,0},{2,3},{3,2},{4,5},{5,4},{6,7},{7,6},{8,9},{9,8},{10,11... | collective-permute-start | bytes 6291464 | tf_op jit(solution)/shard_map/ppermute | solution.py:165
  49.1 24.0 %collective-permute-start.11 = (bf16[896,512]{1,0:T(8,128)(2,1)S(1)}, bf16[896,512]{1,0:T(8,128)(2,1)S(1)}, u32[]{:S(2)}, u32[]{:S(2)}) collective-permute-start(bf16[896,512]{1,0:T(8,128)(2,1)S(1)} %copy-done.2), channel_id=1, source_target_pairs={{0,1},{1,0},{2,3},{3,2},{4,5},{5,4},{6,7},{7,6},{8,9},{9,8},{10,11... | collective-permute-start | bytes 2752520 | tf_op jit(solution)/shard_map/ppermute | solution.py:165
  49.7 23.3 %collective-permute-start.9 = (bf16[2,4,32,896]{3,2,1,0:T(8,128)(2,1)S(1)}, bf16[2,4,32,896]{3,2,1,0:T(8,128)(2,1)S(1)}, u32[]{:S(2)}, u32[]{:S(2)}) collective-permute-start(bf16[2,4,32,896]{3,2,1,0:T(8,128)(2,1)S(1)} %pad_maximum_fusion.4.refs_0_), channel_id=1, source_target_pairs={{0,4},{1,5},{2,6},{3,7},{4,0},{5,1},{6,2},{7,3},{8,12},{9,13},{10,... | collective-permute-start | bytes 1376264 | tf_op jit(solution)/shard_map/ppermute | solution.py:172
  49.7 23.4 %collective-permute-start.10 = (bf16[2,4,32,896]{3,2,1,0:T(8,128)(2,1)S(1)}, bf16[2,4,32,896]{3,2,1,0:T(8,128)(2,1)S(1)}, u32[]{:S(2)}, u32[]{:S(2)}) collective-permute-start(bf16[2,4,32,896]{3,2,1,0:T(8,128)(2,1)S(1)} %pad_maximum_fusion.4.refs_0_), channel_id=1, source_target_pairs={{0,2},{1,3},{2,0},{3,1},{4,6},{5,7},{6,4},{7,5},{8,10},{9,11},{10,... | collective-permute-start | bytes 1376264 | tf_op jit(solution)/shard_map/ppermute | solution.py:172
  63.0 25.7 %copy-start.3 = (bf16[512,896]{1,0:T(8,128)(2,1)S(1)}, bf16[512,896]{1,0:T(8,128)(2,1)}, u32[]{:S(2)}) copy-start(bf16[512,896]{1,0:T(8,128)(2,1)} %refs_8_.1) | copy-start | bytes 2752516
  73.1 2.7 %collective-permute-start.15 = (bf16[4,64,1536]{2,1,0:T(8,128)(2,1)S(1)}, bf16[4,64,1536]{2,1,0:T(8,128)(2,1)S(1)}, u32[]{:S(2)}, u32[]{:S(2)}) collective-permute-start(bf16[4,64,1536]{2,1,0:T(8,128)(2,1)S(1)} %get-tuple-element.65), channel_id=1, source_target_pairs={{0,1},{1,0},{2,3},{3,2},{4,5},{5,4},{6,7},{7,6},{8,9},{9,8},{10,11... | collective-permute-start | bytes 2359304 | tf_op jit(solution)/shard_map/ppermute | solution.py:165
  73.1 2.6 %collective-permute-start.14 = (bf16[4,64,512]{2,1,0:T(8,128)(2,1)S(1)}, bf16[4,64,512]{2,1,0:T(8,128)(2,1)S(1)}, u32[]{:S(2)}, u32[]{:S(2)}) collective-permute-start(bf16[4,64,512]{2,1,0:T(8,128)(2,1)S(1)} %slice.31), channel_id=1, source_target_pairs={{0,1},{1,0},{2,3},{3,2},{4,5},{5,4},{6,7},{7,6},{8,9},{9,8},{10,11... | collective-permute-start | bytes 786440 | tf_op jit(solution)/shard_map/ppermute | solution.py:165
  73.7 2.2 %collective-permute-start.12 = (bf16[2,4,32,896]{3,2,1,0:T(8,128)(2,1)S(1)}, bf16[2,4,32,896]{3,2,1,0:T(8,128)(2,1)S(1)}, u32[]{:S(2)}, u32[]{:S(2)}) collective-permute-start(bf16[2,4,32,896]{3,2,1,0:T(8,128)(2,1)S(1)} %pad_maximum_fusion.4.refs_0_), channel_id=1, source_target_pairs={{2,4},{3,5},{4,2},{5,3},{10,12},{11,13},{12,10},{13,11},{18,20},{1... | collective-permute-start | bytes 1376264 | tf_op jit(solution)/shard_map/ppermute | solution.py:172
  74.4 14.3 %collective-permute-start.13 = (bf16[2,4,32,896]{3,2,1,0:T(8,128)(2,1)S(1)}, bf16[2,4,32,896]{3,2,1,0:T(8,128)(2,1)S(1)}, u32[]{:S(2)}, u32[]{:S(2)}) collective-permute-start(bf16[2,4,32,896]{3,2,1,0:T(8,128)(2,1)S(1)} %collective-permute-done.9.refs_2_), channel_id=1, source_target_pairs={{2,0},{3,1},{4,6},{5,7},{10,8},{11,9},{12,14},{13,15},{18,16},{19,... | collective-permute-start | bytes 1376264 | tf_op jit(solution)/shard_map/ppermute | solution.py:172
  75.8 63.4 %copy-start.6 = (bf16[4,64,1024]{2,1,0:T(8,128)(2,1)}, bf16[4,64,1024]{2,1,0:T(8,128)(2,1)S(1)}, u32[]{:S(2)}) copy-start(bf16[4,64,1024]{2,1,0:T(8,128)(2,1)S(1)} %pad_maximum_fusion.2) | copy-start | bytes 1572868
  98.1 11.1 %collective-permute-start.18 = (bf16[256,896]{1,0:T(8,128)(2,1)S(1)}, bf16[256,896]{1,0:T(8,128)(2,1)S(1)}, u32[]{:S(2)}, u32[]{:S(2)}) collective-permute-start(bf16[256,896]{1,0:T(8,128)(2,1)S(1)} %get-tuple-element.82), channel_id=1, source_target_pairs={{0,2},{1,3},{6,4},{7,5},{8,10},{9,11},{14,12},{15,13},{16,18},{17,... | collective-permute-start | bytes 1376264 | tf_op jit(solution)/shard_map/ppermute | solution.py:172
  99.6 25.7 %collective-permute-start.20 = (bf16[256,896]{1,0:T(8,128)(2,1)S(1)}, bf16[256,896]{1,0:T(8,128)(2,1)S(1)}, u32[]{:S(2)}, u32[]{:S(2)}) collective-permute-start(bf16[256,896]{1,0:T(8,128)(2,1)S(1)} %get-tuple-element.82), channel_id=1, source_target_pairs={{2,4},{3,5},{4,2},{5,3},{10,12},{11,13},{12,10},{13,11},{18,20},{1... | collective-permute-start | bytes 1376264 | tf_op jit(solution)/shard_map/ppermute | solution.py:172
  100.3 10.4 %copy-start.8 = (f32[896]{0:T(1024)S(1)}, f32[896]{0:T(1024)}, u32[]{:S(2)}) copy-start(f32[896]{0:T(1024)} %param.17) | copy-start | bytes 10756
  101.2 18.4 %collective-permute-start.16 = (bf16[256,896]{1,0:T(8,128)(2,1)S(1)}, bf16[256,896]{1,0:T(8,128)(2,1)S(1)}, u32[]{:S(2)}, u32[]{:S(2)}) collective-permute-start(bf16[256,896]{1,0:T(8,128)(2,1)S(1)} %get-tuple-element.80), channel_id=1, source_target_pairs={{0,2},{1,3},{2,0},{3,1},{4,6},{5,7},{6,4},{7,5},{8,10},{9,11},{10,... | collective-permute-start | bytes 1376264 | tf_op jit(solution)/shard_map/ppermute | solution.py:172
  102.8 22.4 %collective-permute-start.17 = (bf16[256,896]{1,0:T(8,128)(2,1)S(1)}, bf16[256,896]{1,0:T(8,128)(2,1)S(1)}, u32[]{:S(2)}, u32[]{:S(2)}) collective-permute-start(bf16[256,896]{1,0:T(8,128)(2,1)S(1)} %get-tuple-element.81), channel_id=1, source_target_pairs={{0,4},{1,5},{6,2},{7,3},{8,12},{9,13},{14,10},{15,11},{16,20},{17,... | collective-permute-start | bytes 1376264 | tf_op jit(solution)/shard_map/ppermute | solution.py:172
  109.3 31.3 %copy-start.9 = (s32[32]{0:T(128)S(1)}, s32[32]{0:T(128)}, u32[]{:S(2)}) copy-start(s32[32]{0:T(128)} %param.13) | copy-start | bytes 388
  109.3 27.2 %collective-permute-start.19 = (bf16[256,896]{1,0:T(8,128)(2,1)S(1)}, bf16[256,896]{1,0:T(8,128)(2,1)S(1)}, u32[]{:S(2)}, u32[]{:S(2)}) collective-permute-start(bf16[256,896]{1,0:T(8,128)(2,1)S(1)} %add_convert_fusion.2), channel_id=1, source_target_pairs={{2,6},{3,7},{4,0},{5,1},{10,14},{11,15},{12,8},{13,9},{18,22},{19,... | collective-permute-start | bytes 1376264 | tf_op jit(solution)/shard_map/ppermute | solution.py:172
  137.1 17.9 %collective-permute-start.21 = (bf16[256,896]{1,0:T(8,128)(2,1)S(1)}, bf16[256,896]{1,0:T(8,128)(2,1)}, u32[]{:S(2)}, u32[]{:S(2)}) collective-permute-start(bf16[256,896]{1,0:T(8,128)(2,1)S(1)} %normed.1.rows), channel_id=1, source_target_pairs={{0,4},{1,5},{2,6},{3,7},{4,0},{5,1},{6,2},{7,3},{8,12},{9,13},{10,... | collective-permute-start | bytes 1376264 | tf_op jit(solution)/shard_map/ppermute | solution.py:172
  137.2 20.5 %collective-permute-start.25 = (bf16[256,896]{1,0:T(8,128)(2,1)S(1)}, bf16[256,896]{1,0:T(8,128)(2,1)}, u32[]{:S(2)}, u32[]{:S(2)}) collective-permute-start(bf16[256,896]{1,0:T(8,128)(2,1)S(1)} %normed.1.rows), channel_id=1, source_target_pairs={{0,2},{1,3},{2,0},{3,1},{4,6},{5,7},{6,4},{7,5},{8,10},{9,11},{10,... | collective-permute-start | bytes 1376264 | tf_op jit(solution)/shard_map/ppermute | solution.py:172
  139.3 1.7 collective-permute-start.22
  155.0 9.9 %collective-permute-start.23 = (bf16[256,896]{1,0:T(8,128)(2,1)S(1)}, bf16[256,896]{1,0:T(8,128)(2,1)}, u32[]{:S(2)}, u32[]{:S(2)}) collective-permute-start(bf16[256,896]{1,0:T(8,128)(2,1)S(1)} %normed.1.rows), channel_id=1, source_target_pairs={{2,4},{3,5},{4,2},{5,3},{10,12},{11,13},{12,10},{13,11},{18,20},{1... | collective-permute-start | bytes 1376264 | tf_op jit(solution)/shard_map/ppermute | solution.py:172
  156.4 10.7 %collective-permute-start.24 = (bf16[256,896]{1,0:T(8,128)(2,1)}, bf16[256,896]{1,0:T(8,128)(2,1)}, u32[]{:S(2)}, u32[]{:S(2)}) collective-permute-start(bf16[256,896]{1,0:T(8,128)(2,1)} %collective-permute-done.21.two), channel_id=1, source_target_pairs={{2,0},{3,1},{4,6},{5,7},{10,8},{11,9},{12,14},{13,15},{18,16},{19,... | collective-permute-start | bytes 1376264 | tf_op jit(solution)/shard_map/ppermute | solution.py:172
  162.9 0.7 copy-start.4
  163.6 1.3 collective-permute-start.26
  167.1 1.0 copy-start.5
  168.1 23.5 %copy-start.1 = (bf16[512,4096]{1,0:T(8,128)(2,1)S(1)}, bf16[512,4096]{1,0:T(8,128)(2,1)}, u32[]{:S(2)}) copy-start(bf16[512,4096]{1,0:T(8,128)(2,1)} %own_w) | copy-start | bytes 12582916
  175.8 13.6 %collective-permute-start.29 = (bf16[64,4096]{1,0:T(8,128)(2,1)S(1)}, bf16[64,4096]{1,0:T(8,128)(2,1)S(1)}, u32[]{:S(2)}, u32[]{:S(2)}) collective-permute-start(bf16[64,4096]{1,0:T(8,128)(2,1)S(1)} %get-tuple-element.98), channel_id=1, source_target_pairs={{0,2},{1,3},{6,4},{7,5},{8,10},{9,11},{14,12},{15,13},{16,18},{17,... | collective-permute-start | bytes 1572872 | tf_op jit(solution)/shard_map/ppermute | solution.py:172
  179.0 16.0 %collective-permute-start.31 = (bf16[64,4096]{1,0:T(8,128)(2,1)S(1)}, bf16[64,4096]{1,0:T(8,128)(2,1)S(1)}, u32[]{:S(2)}, u32[]{:S(2)}) collective-permute-start(bf16[64,4096]{1,0:T(8,128)(2,1)S(1)} %get-tuple-element.98), channel_id=1, source_target_pairs={{2,4},{3,5},{4,2},{5,3},{10,12},{11,13},{12,10},{13,11},{18,20},{1... | collective-permute-start | bytes 1572872 | tf_op jit(solution)/shard_map/ppermute | solution.py:172
  179.7 15.4 %collective-permute-start.28 = (bf16[64,4096]{1,0:T(8,128)(2,1)S(1)}, bf16[64,4096]{1,0:T(8,128)(2,1)S(1)}, u32[]{:S(2)}, u32[]{:S(2)}) collective-permute-start(bf16[64,4096]{1,0:T(8,128)(2,1)S(1)} %get-tuple-element.97), channel_id=1, source_target_pairs={{0,4},{1,5},{6,2},{7,3},{8,12},{9,13},{14,10},{15,11},{16,20},{17,... | collective-permute-start | bytes 1572872 | tf_op jit(solution)/shard_map/ppermute | solution.py:172
  183.7 17.0 %collective-permute-start.27 = (bf16[64,4096]{1,0:T(8,128)(2,1)S(1)}, bf16[64,4096]{1,0:T(8,128)(2,1)S(1)}, u32[]{:S(2)}, u32[]{:S(2)}) collective-permute-start(bf16[64,4096]{1,0:T(8,128)(2,1)S(1)} %get-tuple-element.96), channel_id=1, source_target_pairs={{0,2},{1,3},{2,0},{3,1},{4,6},{5,7},{6,4},{7,5},{8,10},{9,11},{10,... | collective-permute-start | bytes 1572872 | tf_op jit(solution)/shard_map/ppermute | solution.py:172
  189.5 14.3 %collective-permute-start.30 = (bf16[64,4096]{1,0:T(8,128)(2,1)S(1)}, bf16[64,4096]{1,0:T(8,128)(2,1)S(1)}, u32[]{:S(2)}, u32[]{:S(2)}) collective-permute-start(bf16[64,4096]{1,0:T(8,128)(2,1)S(1)} %add_convert_fusion.1), channel_id=1, source_target_pairs={{2,6},{3,7},{4,0},{5,1},{10,14},{11,15},{12,8},{13,9},{18,22},{19,... | collective-permute-start | bytes 1572872 | tf_op jit(solution)/shard_map/ppermute | solution.py:172
  190.8 0.7 collective-permute-start.32
  204.3 2.0 collective-permute-start.33
